TPU v7x, 32 devices: a whole 2x2x4 slice. The times are simulated.
32 devices in a mesh: groups: 2 (over x), ex: 8 (over z, y), tp: 2 (over core).
Axes of the slice: x: 2, y: 2, z: 4, core: 2. Of those that a mesh axis runs over, the one named last changes fastest.
Arguments:
- activations: bfloat16 [16, 256, 29568], P(('groups', 'ex'), None, 'tp'), parts along dimension 0, may hold values from -6 to 6
- out_grads: bfloat16 [16, 256, 8192], P(('groups', 'ex'), None, 'tp'), parts along dimension 0, may hold values from -0.3984375 to 0.3984375
- in_factor: bfloat16 [32, 29568], P(None, 'tp'), may hold values from -0.03125 to 0.03125
- out_factor: bfloat16 [32, 8192], P(None, 'tp'), may hold values from -0.0625 to 0.0625
- curvature_inv: float32 [1024, 1024], P('tp'), may hold values from -1 to 4, as said below
- queries: bfloat16 [4096, 1024], P(('groups', 'ex'), 'tp'), parts along dimension 0, may hold values from -0.19921875 to 0.19921875
Outputs:
- example_grads: float32 [16, 1024], P(('groups', 'ex'), 'tp'), parts along dimension 0
- scores: float32 [16, 2048], P(('groups', 'ex'), 'tp'), parts along dimension 0
There are 2 independent parts, one for each index of `groups`. A program takes and returns all parts, laid end to end along the dimension named above; an argument that names none is the same for every part. Nothing has to cross between parts.
Inputs may be any that keep to these rules, and one draw needn't show every extreme that they name: `curvature_inv`: symmetric.
All inputs are finite; a program needn't handle non-finite values.
Results may differ from a plain program's by a relative error of at most 0.0003.
Values may be sent and summed in bfloat16 or wider, within the bound.
No kernel may reach another device: no remote copies, remote signals or barrier semaphores. Data moves between devices by JAX's collectives and lax.ppermute only.
A program may use at most 128 MiB of HBM per device.

v0:
```python
import jax
import jax.numpy as jnp
from jax import lax
from jax.sharding import PartitionSpec as P


def split_three(values):
    high_part = lax.optimization_barrier(values.astype(jnp.bfloat16))
    remainder = values - high_part.astype(jnp.float32)
    middle_part = lax.optimization_barrier(remainder.astype(jnp.bfloat16))
    low_part = (remainder - middle_part.astype(jnp.float32)).astype(jnp.bfloat16)
    return jnp.concatenate([high_part, middle_part, low_part], axis=0)


def shards(activations, out_grads, in_factor, out_factor, curvature_inv, queries):
    flat_inputs = activations.reshape(-1, activations.shape[2])
    flat_grads = out_grads.reshape(-1, out_grads.shape[2])
    rank_size = in_factor.shape[0]
    out_part = jnp.dot(flat_grads, out_factor.T, preferred_element_type=jnp.float32)
    in_part = jnp.dot(flat_inputs, in_factor.T, preferred_element_type=jnp.float32)
    my_rows = lax.psum_scatter(
        jnp.concatenate([out_part, in_part], axis=1), "tp", scatter_dimension=0, tiled=True
    )
    partial_outer = jnp.dot(
        my_rows[:, :rank_size].T, my_rows[:, rank_size:], precision=lax.Precision.HIGHEST
    )
    summed_outer = lax.psum(partial_outer, "tp")
    grad_vector = summed_outer.reshape(1, -1)
    feat_share = curvature_inv.shape[0]
    tp_index = lax.axis_index("tp")
    grads_share = lax.dynamic_slice_in_dim(grad_vector, tp_index * feat_share, feat_share, 1)
    precond = jnp.dot(grad_vector, curvature_inv.T, precision=lax.Precision.HIGHEST)
    precond_parts = split_three(precond)
    triple = jnp.dot(
        precond_parts,
        lax.all_gather(queries, "ex", axis=0, tiled=True).T,
        preferred_element_type=jnp.float32,
    )
    partials = jnp.sum(triple, axis=0, keepdims=True)
    scores = lax.psum_scatter(partials, "tp", scatter_dimension=1, tiled=True)
    return (grads_share, scores)


def solution(mesh):
    placed = (
        P(("groups", "ex"), None, "tp"),
        P(("groups", "ex"), None, "tp"),
        P(None, "tp"),
        P(None, "tp"),
        P("tp", None),
        P(("groups", "ex"), "tp"),
    )
    return jax.shard_map(
        shards,
        mesh=mesh,
        in_specs=placed,
        out_specs=(P(("groups", "ex"), "tp"), P(("groups", "ex"), "tp")),
        check_vma=False,
    )
```

profile of v0, /device:TPU:1, one launch (start us, length us, event | category | flops | bytes accessed | tf_op | source)
XLA Modules:
  0.0 88.9 jit_solution(9827053738877143792)
XLA Ops:
  8.0 0.0 copy-start
  8.0 0.0 copy-start.1
  8.0 0.0 reduce-scatter.5.cloned.1.call-start
  8.1 5.0 %fusion = f32[256,32]{0,1:T(8,128)S(1)} fusion(bf16[32,14784]{1,0:T(8,128)(2,1)} %param.8, bf16[1,256,14784]{1,2,0:T(8,128)(2,1)} %param.6), kind=kOutput, calls=%fused_computation | convolution fusion | flops 242221056 | bytes 8548352 | tf_op jit(solution)/shard_map/dot_general | solution.py:20
  13.1 0.0 copy-done
  13.1 0.0 copy-done.1
  13.1 0.7 fusion.2
  13.8 0.6 pad_maximum_fusion
  14.4 0.0 reduce-scatter.5.cloned.1.call-update
  14.5 0.0 all-gather.2.cloned.1.call-start
  14.5 0.5 all-gather.2.cloned.1.call-update
  15.0 0.0 reduce-scatter.7.cloned.1.call-start
  15.1 9.4 %reduce-scatter.5.cloned.1.call-done = f32[128,64]{0,1:T(8,128)} async-done(((f32[256,64]{0,1:T(8,128)}), f32[128,64]{0,1:T(8,128)}) %reduce-scatter.5.cloned.1.call-update) | async-done | bytes 32784 | tf_op jit(solution)/shard_map/reduce_scatter | solution.py:21
  24.5 0.9 fusion.4
  25.4 3.5 %psum.7 = f32[32,32]{1,0:T(8,128)S(1)} all-reduce(f32[32,32]{1,0:T(8,128)S(1)} %fusion.4), channel_id=1, replica_groups=mesh['groups'=2,'ex'=8,'tp'=2] {'tp'}, use_global_device_ids=true, to_apply=%region_1.0 | all-reduce | flops 1024 | bytes 8192 | tf_op jit(solution)/shard_map/psum | solution.py:27
  28.9 0.1 reshape.21
  29.0 0.1 reshape.23
  29.1 3.4 %fusion.14 = f32[1,512]{1,0:T(1,128)S(1)} fusion(f32[1024,1]{0,1:T(1,128)S(1)} %reshape.23, f32[512,1024]{1,0:T(8,128)} %param.10), kind=kOutput, calls=%fused_computation.19 | convolution fusion | flops 6291456 | bytes 2103296 | tf_op jit(solution)/shard_map/dot_general | solution.py:32
  32.5 34.1 %all-gather.2.cloned.1.call-done = bf16[2048,512]{1,0:T(8,128)(2,1)} async-done(((bf16[256,512]{1,0:T(8,128)(2,1)}), bf16[2048,512]{1,0:T(8,128)(2,1)}) %all-gather.2.cloned.1.call-update) | async-done | bytes 2097168 | tf_op jit(solution)/shard_map/all_gather | solution.py:36
  66.6 2.2 %convolution_reduce_fusion = f32[2048]{0:T(1024)S(1)} fusion(bf16[2048,512]{1,0:T(8,128)(2,1)} %all-gather.2.cloned.1.call-done, bf16[1,512]{1,0:T(2,128)(2,1)S(1)} %subtract_convert_fusion, bf16[1,512]{1,0:T(2,128)(2,1)S(1)} %fusion.12, bf16[1,512]{1,0:T(2,128)(2,1)S(1)} %convert_element_type.19), kind=kOutput, calls=%fused_computation.4 | convolution fusion | flops 6304768 | bytes 2108416 | tf_op jit(solution)/shard_map/dot_general | solution.py:34
  68.9 1.4 %copy.8 = f32[1,2048]{0,1:T(8,128)} copy(f32[1,2048]{1,0:T(1,128)S(1)} %bitcast.17) | data formatting | bytes 16384
  70.3 0.0 reduce-scatter.7.cloned.1.call-update
  70.3 0.6 constant_dynamic-slice_fusion
  70.9 8.8 %reduce-scatter.7.cloned.1.call-done = f32[1024,1]{1,0:T(8,128)} async-done(((f32[2048,1]{1,0:T(8,128)}), f32[1024,1]{1,0:T(8,128)}) %reduce-scatter.7.cloned.1.call-update) | async-done | bytes 4112
  79.7 1.8 %copy.9 = f32[1,1024]{1,0:T(1,128)} copy(f32[1,1024]{0,1:T(8,128)} %bitcast.16) | data formatting | bytes 8192
  (4 shorter events, 0.0 us)
Async XLA Ops:
  8.0 5.1 %copy-start = (bf16[1,256,4096]{2,1,0:T(8,128)(2,1)S(1)}, bf16[1,256,4096]{2,1,0:T(8,128)(2,1)}, u32[]{:S(2)}) copy-start(bf16[1,256,4096]{2,1,0:T(8,128)(2,1)} %param.7) | copy-start | bytes 6291460
  8.0 5.1 %copy-start.1 = (bf16[32,4096]{1,0:T(8,128)(2,1)S(1)}, bf16[32,4096]{1,0:T(8,128)(2,1)}, u32[]{:S(2)}) copy-start(bf16[32,4096]{1,0:T(8,128)(2,1)} %param.9) | copy-start | bytes 786436
  8.0 16.5 %reduce-scatter.5.cloned.1.call-start = ((), (), s32[]{:S(2)}) async-start(), calls=%async_computation.2 | async-start | bytes 98304 | tf_op jit(solution)/shard_map/reduce_scatter | solution.py:21
  14.5 52.2 %all-gather.2.cloned.1.call-start = ((), (), s32[]{:S(2)}) async-start(), calls=%async_computation.3 | async-start | bytes 2359296 | tf_op jit(solution)/shard_map/all_gather | solution.py:36
  15.0 64.6 %reduce-scatter.7.cloned.1.call-start = ((), (), s32[]{:S(2)}) async-start(), calls=%async_computation.4 | async-start | bytes 1572864
Sparse Core Ops, SparseCore 0:
  14.6 9.8 reduce-scatter.4
  70.4 9.2 reduce-scatter.6
Sparse Core Ops, SparseCore 1:
  17.1 49.5 all-gather.1
where the time goes:
time: 89.5 us; the launch traced here: 88.9 us
  waiting for transfers between devices  52.9 us (59%)
  between operations  15.6 us (17%)
  matrix products  12.2 us (14%)
  local copies, waits for them, and re-layouts  3.96 us (4%)
  blocking collectives  3.5 us (4%)
    all_gather x1, waiting for transfers between devices, shards(): lax.all_gather(queries, 'ex', axis=0, tiled=True)  34.1 us
    reduce_scatter x1, waiting for transfers between devices, shards(): lax.psum_scatter(jnp.concatenate([out_part, in_part], axis=1), 'tp', scat...  9.41 us
    unnamed x4, waiting for transfers between devices  9.35 us
    dot_general x1, matrix products, shards(): jnp.dot(flat_inputs, in_factor.T, preferred_element_type=jnp.float32)  4.98 us
    psum x1, blocking collectives, shards(): summed_outer = lax.psum(partial_outer, 'tp')  3.5 us
    dot_general x1, matrix products, shards(): jnp.dot(grad_vector, curvature_inv.T, precision=lax.Precision.HIGHEST)  3.39 us
    unnamed x6, local copies, waits for them, and re-layouts  3.2 us
    dot_general x1, matrix products, shards(): jnp.dot(precond_parts, lax.all_gather(queries, 'ex', axis=0, tiled=True)....  2.25 us
  transfers between devices with their start and end apart: 3, of which 3 were waited for; matrix products, arithmetic and copies ran while one was open for 6% of the time, Pallas kernels for 0%

commit v1 on v0

v1 whole, which is shorter than its diff:
```python
import functools

import jax
import jax.numpy as jnp
from jax import lax
from jax.experimental import pallas as pl
from jax.experimental.pallas import tpu as pltpu
from jax.sharding import PartitionSpec as P

LANES = 128
CHUNK = 2048
NT = (((1,), (1,)), ((), ()))
ANY = pl.BlockSpec(memory_space=pl.ANY)
VMEM = pl.BlockSpec(memory_space=pltpu.VMEM)


def pieces(total, step):
    return [(start, min(step, total - start)) for start in range(0, total, step)]


def split(values, count):
    parts = []
    for _ in range(count):
        part = values.astype(jnp.bfloat16)
        parts.append(part)
        values = values - part.astype(jnp.float32)
    return parts


def project_kernel(acts, grads, in_f, out_f, result, acts_v, grads_v, in_v, out_v, sems):
    in_cuts = pieces(acts.shape[0], CHUNK)
    out_cuts = pieces(grads.shape[1], CHUNK)
    copies = [
        pltpu.make_async_copy(out_f, out_v, sems.at[0]),
        pltpu.make_async_copy(in_f, in_v, sems.at[1]),
    ]
    for start, size in out_cuts:
        cut = (slice(None), pl.ds(start, size))
        copies.append(pltpu.make_async_copy(grads.at[cut], grads_v.at[cut], sems.at[len(copies)]))
    for start, size in in_cuts:
        cut = pl.ds(start, size)
        copies.append(pltpu.make_async_copy(acts.at[cut], acts_v.at[cut], sems.at[len(copies)]))
    for copy in copies:
        copy.start()
    copies[0].wait()
    copies[1].wait()
    rank = in_f.shape[0]
    total = jnp.zeros((rank, grads.shape[0]), jnp.float32)
    for (start, size), copy in zip(out_cuts, copies[2:]):
        copy.wait()
        total += lax.dot_general(
            out_v[:, start : start + size],
            grads_v[:, start : start + size],
            NT,
            preferred_element_type=jnp.float32,
        )
    result[:rank] = total
    total = jnp.zeros_like(total)
    for (start, size), copy in zip(in_cuts, copies[2 + len(out_cuts) :]):
        copy.wait()
        total += jnp.dot(
            in_v[:, start : start + size],
            acts_v[start : start + size],
            preferred_element_type=jnp.float32,
        )
    result[rank:] = total


def project(acts, grads, in_factor, out_factor):
    shapes = (acts, grads, in_factor, out_factor)
    copies = 2 + len(pieces(acts.shape[0], CHUNK)) + len(pieces(grads.shape[1], CHUNK))
    rank, tokens = in_factor.shape[0], grads.shape[0]
    return pl.pallas_call(
        project_kernel,
        out_shape=jax.ShapeDtypeStruct((2 * rank, tokens), jnp.float32),
        in_specs=[ANY] * 4,
        out_specs=VMEM,
        scratch_shapes=[pltpu.VMEM(a.shape, a.dtype) for a in shapes]
        + [pltpu.SemaphoreType.DMA((copies,))],
        compiler_params=pltpu.CompilerParams(vmem_limit_bytes=32 << 20),
        cost_estimate=pl.CostEstimate(
            flops=2 * rank * tokens * (acts.shape[0] + grads.shape[1]),
            bytes_accessed=sum(a.size * 2 for a in shapes),
            transcendentals=0,
        ),
        name="project",
    )(*shapes)


def outer_kernel(mine, other, grad, share, lanes):
    rank = mine.shape[0] // 2
    for i in range(lanes.shape[0]):
        cut = slice(i * LANES, (i + 1) * LANES)
        lanes[i] = mine[:rank, cut] + other[:rank, cut]
    fold = LANES // rank
    rows = jnp.concatenate(
        [
            jnp.concatenate(
                [lanes[i, pl.ds(j, rank // fold, stride=fold), :] for j in range(fold)], axis=0
            )
            for i in range(lanes.shape[0])
        ],
        axis=1,
    )
    left = jnp.concatenate(split(rows, 3), axis=0)
    right = split(mine[rank:] + other[rank:], 3)
    wide = [jnp.concatenate([part] * fold, axis=0) for part in right]
    flat = jnp.zeros((rank, LANES), jnp.float32)
    for i, part in enumerate(wide):
        product = lax.dot_general(left, part, NT, preferred_element_type=jnp.float32)
        for j in range(3):
            flat += product[j * rank : (j + 1) * rank]
    column = lax.broadcasted_iota(jnp.int32, (rank // fold, LANES), 1) // rank
    result = jnp.zeros((rank // fold, LANES), jnp.float32)
    for j in range(fold):
        block = flat[j * (rank // fold) : (j + 1) * (rank // fold)]
        result += jnp.where(column == j, block, 0.0)
    grad[...] = result
    half = rank // fold // 2
    own = jnp.where(lax.axis_index("tp") == 0, result[:half], result[half:])
    for k in range(half):
        share[:, k * LANES : (k + 1) * LANES] = own[k : k + 1]


def outer(mine, other):
    rank, tokens = mine.shape[0] // 2, mine.shape[1]
    feats = rank * rank
    return pl.pallas_call(
        outer_kernel,
        out_shape=(
            jax.ShapeDtypeStruct((feats // LANES, LANES), jnp.float32),
            jax.ShapeDtypeStruct((1, feats // 2), jnp.float32),
        ),
        in_specs=[VMEM, VMEM],
        out_specs=(VMEM, VMEM),
        scratch_shapes=[pltpu.VMEM((tokens // LANES, rank, LANES), jnp.float32)],
        name="outer",
    )(mine, other)


def halves_kernel(values, high, low):
    whole = values[...]
    top = whole.astype(jnp.bfloat16)
    high[...] = top
    low[...] = (whole - top.astype(jnp.float32)).astype(jnp.bfloat16)


def halves(values):
    shape = jax.ShapeDtypeStruct(values.shape, jnp.bfloat16)
    return pl.pallas_call(
        halves_kernel,
        out_shape=(shape, shape),
        in_specs=[VMEM],
        out_specs=(VMEM, VMEM),
        cost_estimate=pl.CostEstimate(
            flops=3 * values.size, bytes_accessed=8 * values.size, transcendentals=0
        ),
        name="curvature_halves",
    )(values)


def score_kernel(blocks, near, far, high, low, *refs):
    queries, (kept, sent) = refs[:blocks], refs[blocks:]
    grads = jnp.concatenate(
        [
            jnp.concatenate([ref[k : k + 1] for k in range(ref.shape[0])], axis=1)
            for ref in (near, far)
        ],
        axis=0,
    )
    left = jnp.concatenate(split(grads, 3), axis=0)
    both = lax.dot_general(left, high[...], NT, preferred_element_type=jnp.float32)
    both += lax.dot_general(left, low[...], NT, preferred_element_type=jnp.float32)
    precond = both[0:2] + both[2:4] + both[4:6]
    left = jnp.concatenate(split(precond, 3), axis=0)
    place = lax.axis_index("ex") % blocks
    side = lax.axis_index("ex") // blocks
    keeps_near = lax.axis_index("tp") == side
    width = queries[0].shape[0]
    for j in range(blocks):
        triple = lax.dot_general(left, queries[j][...], NT, preferred_element_type=jnp.float32)
        total = triple[0:2] + triple[2:4] + triple[4:6]
        at = pl.ds(pl.multiple_of((place ^ j) * width, width), width)
        kept[:, at] = jnp.where(keeps_near, total[0:1], total[1:2])
        sent[:, at] = jnp.where(keeps_near, total[1:2], total[0:1])


def score(near, far, high, low, queries):
    row = jax.ShapeDtypeStruct((1, len(queries) * queries[0].shape[0]), jnp.float32)
    return pl.pallas_call(
        functools.partial(score_kernel, len(queries)),
        out_shape=(row, row),
        in_specs=[VMEM] * (4 + len(queries)),
        out_specs=(VMEM, VMEM),
        compiler_params=pltpu.CompilerParams(vmem_limit_bytes=32 << 20),
        name="score",
    )(near, far, high, low, *queries)


def shards(ex, activations, out_grads, in_factor, out_factor, curvature_inv, queries):
    half = ex // 2
    swap = [(0, 1), (1, 0)]
    crossing = [(i, i ^ (2 * half + 1)) for i in range(2 * ex)]
    blocks = [queries] + [
        lax.ppermute(queries, "ex", [(e, e ^ k) for e in range(ex)]) for k in range(1, half)
    ]
    part = project(activations[0].T, out_grads[0], in_factor, out_factor)
    grad, grads_share = outer(part, lax.ppermute(part, "tp", swap))
    far_grad = lax.ppermute(grad, ("ex", "tp"), crossing)
    high, low = halves(curvature_inv)
    kept, sent = score(grad, far_grad, high, low, blocks)
    summed = kept + lax.ppermute(sent, "tp", swap)
    returned = lax.ppermute(summed, ("ex", "tp"), crossing)
    keeps_near = lax.axis_index("tp") == lax.axis_index("ex") // half
    return grads_share, jnp.where(keeps_near, summed, returned)


def solution(mesh):
    placed = (
        P(("groups", "ex"), None, "tp"),
        P(("groups", "ex"), None, "tp"),
        P(None, "tp"),
        P(None, "tp"),
        P("tp", None),
        P(("groups", "ex"), "tp"),
    )
    return jax.shard_map(
        functools.partial(shards, mesh.shape["ex"]),
        mesh=mesh,
        in_specs=placed,
        out_specs=(P(("groups", "ex"), "tp"), P(("groups", "ex"), "tp")),
        check_vma=False,
    )
```

time: 89.5 us -> 36.1 us (0.40)
  waiting for transfers between devices: 52.9 us -> 4.8 us
  between operations: 15.6 us -> 0.71 us
  matrix products: 12.2 us -> 0 us
  Pallas kernels: 0 us -> 10.6 us
  starting transfers between devices: 0.12 us -> 8.95 us
  local copies, waits for them, and re-layouts: 3.96 us -> 9.95 us
  blocking collectives: 3.5 us -> 0 us
    all_gather x1 -> x0, waiting for transfers between devices: 34.1 us -> none  [shards(): lax.all_gather(queries, 'ex', axis=0, tiled=True)]
    dot_general x5 -> x0, matrix products: 12.2 us -> none  [the longest x1 4.98 us: shards(): jnp.dot(flat_inputs, in_factor.T, preferred_element_type=jnp.float32)]
    pallas_call x0 -> x4, Pallas kernels: none -> 10.6 us  [the longest x1 4.86 us: project(): pl.pallas_call(project_kernel, out_shape=jax.ShapeDtypeStruct((2 * rank,...]
    reduce_scatter x1 -> x0, waiting for transfers between devices: 9.41 us -> none  [shards(): lax.psum_scatter(jnp.concatenate([out_part, in_part], axis=1), 'tp', scat...]
    unnamed x4 -> x0, waiting for transfers between devices: 9.35 us -> none
    ppermute x0 -> x7, starting transfers between devices: none -> 8.95 us  [the longest x3 3.43 us: shards(): lax.ppermute(queries, 'ex', [(e, e ^ k) for e in range(ex)])]
    unnamed x6 -> x20, local copies, waits for them, and re-layouts: 3.2 us -> 9.95 us
    ppermute x0 -> x7, waiting for transfers between devices: none -> 4.8 us  [the longest x1 2.88 us: shards(): returned = lax.ppermute(summed, ('ex', 'tp'), crossing)]
  transfers between devices with their start and end apart: 3 -> 7, of which waited for: 3 -> 3; matrix products, arithmetic and copies ran while one was open for 6% -> 0% of each run, Pallas kernels for 0% -> 27%
where the time goes in v1:
time: 36.1 us; the launch traced here: 35.6 us
  Pallas kernels  10.6 us (29%)
  local copies, waits for them, and re-layouts  9.95 us (28%)
  starting transfers between devices  8.95 us (25%)
  waiting for transfers between devices  4.8 us (13%)
  between operations  0.71 us (2%)
  other arithmetic  0.6 us (2%)
    unnamed x20, local copies, waits for them, and re-layouts  9.95 us
    pallas_call x1, Pallas kernels, project(): pl.pallas_call(project_kernel, out_shape=jax.ShapeDtypeStruct((2 * rank,...  4.86 us
    ppermute x3, starting transfers between devices, shards(): lax.ppermute(queries, 'ex', [(e, e ^ k) for e in range(ex)])  3.43 us
    pallas_call x1, Pallas kernels, halves(): pl.pallas_call(halves_kernel, out_shape=(shape, shape), in_specs=[VMEM],...  3.08 us
    ppermute x1, starting transfers between devices, shards(): far_grad = lax.ppermute(grad, ('ex', 'tp'), crossing)  2.94 us
    ppermute x1, waiting for transfers between devices, shards(): returned = lax.ppermute(summed, ('ex', 'tp'), crossing)  2.88 us
    pallas_call x1, Pallas kernels, outer(): pl.pallas_call(outer_kernel, out_shape=(jax.ShapeDtypeStruct((feats // LA...  1.68 us
    ppermute x1, starting transfers between devices, shards(): grad, grads_share = outer(part, lax.ppermute(part, 'tp', swap))  1.3 us
  transfers between devices with their start and end apart: 7, of which 3 were waited for; matrix products, arithmetic and copies ran while one was open for 0% of the time, Pallas kernels for 27%

profile of v1, /device:TPU:1, one launch (start us, length us, event | category | flops | bytes accessed | tf_op | source)
XLA Modules:
  0.0 35.6 jit_solution(1735906501504807287)
XLA Ops:
  0.6 2.1 %collective-permute-start.2 = (bf16[256,512]{1,0:T(8,128)(2,1)}, bf16[256,512]{1,0:T(8,128)(2,1)S(1)}, u32[]{:S(2)}, u32[]{:S(2)}) collective-permute-start(bf16[256,512]{1,0:T(8,128)(2,1)} %refs_0_.1), channel_id=1, source_target_pairs={{0,2},{2,0},{4,6},{6,4},{8,10},{10,8},{12,14},{14,12},{1,3},{3,1},... | collective-permute-start | bytes 786440 | tf_op jit(solution)/shard_map/ppermute | solution.py:205
  2.8 1.3 %collective-permute-start.3 = (bf16[256,512]{1,0:T(8,128)(2,1)}, bf16[256,512]{1,0:T(8,128)(2,1)S(1)}, u32[]{:S(2)}, u32[]{:S(2)}) collective-permute-start(bf16[256,512]{1,0:T(8,128)(2,1)} %refs_0_.1), channel_id=1, source_target_pairs={{0,4},{2,6},{4,0},{6,2},{8,12},{10,14},{12,8},{14,10},{1,5},{3,7},... | collective-permute-start | bytes 786440 | tf_op jit(solution)/shard_map/ppermute | solution.py:205
  4.1 0.0 collective-permute-start.4
  4.1 0.0 copy-start
  4.1 3.1 %copy-done = bf16[1,256,14784]{1,2,0:T(8,128)(2,1)S(1)} copy-done((bf16[1,256,14784]{1,2,0:T(8,128)(2,1)S(1)}, bf16[1,256,14784]{1,2,0:T(8,128)(2,1)}, u32[]{:S(2)}) %copy-start) | copy-done | bytes 7569432
  7.2 0.0 copy-start.1
  7.2 1.6 %copy-done.1 = bf16[1,256,4096]{2,1,0:T(8,128)(2,1)S(1)} copy-done((bf16[1,256,4096]{2,1,0:T(8,128)(2,1)S(1)}, bf16[1,256,4096]{2,1,0:T(8,128)(2,1)}, u32[]{:S(2)}) %copy-start.1) | copy-done | bytes 2097176
  8.8 0.0 copy-start.4
  8.8 1.2 %copy-done.4 = bf16[32,14784]{1,0:T(8,128)(2,1)S(1)} copy-done((bf16[32,14784]{1,0:T(8,128)(2,1)S(1)}, bf16[32,14784]{1,0:T(8,128)(2,1)}, u32[]{:S(2)}) %copy-start.4) | copy-done | bytes 946200
  10.0 0.0 copy-start.6
  10.0 0.9 %copy-done.6 = bf16[32,4096]{1,0:T(8,128)(2,1)S(1)} copy-done((bf16[32,4096]{1,0:T(8,128)(2,1)S(1)}, bf16[32,4096]{1,0:T(8,128)(2,1)}, u32[]{:S(2)}) %copy-start.6) | copy-done | bytes 262168
  10.9 4.9 %project.1.mine = f32[64,256]{1,0:T(8,128)S(1)} custom-call(bf16[14784,256]{1,0:T(8,128)(2,1)S(1)} %bitcast.4, bf16[256,4096]{1,0:T(8,128)(2,1)S(1)} %bitcast.5, bf16[32,14784]{1,0:T(8,128)(2,1)S(1)} %copy-done.4, bf16[32,4096]{1,0:T(8,128)(2,1)S(1)} %copy-done.6), custom_call_target="tpu_custom_call" | custom-call | flops 309329920 | bytes 10874880 | tf_op jit(solution)/shard_map/project/pallas_call | solution.py:73
  15.8 0.0 copy-start.5
  15.8 0.0 copy-start.7
  15.8 1.3 %collective-permute-start = (f32[64,256]{1,0:T(8,128)S(1)}, f32[64,256]{1,0:T(8,128)S(1)}, u32[]{:S(2)}, u32[]{:S(2)}) collective-permute-start(f32[64,256]{1,0:T(8,128)S(1)} %project.1.mine), channel_id=1, source_target_pairs={{0,1},{1,0},{2,3},{3,2},{4,5},{5,4},{6,7},{7,6},{8,9},{9,8},{10,11... | collective-permute-start | bytes 196616 | tf_op jit(solution)/shard_map/ppermute | solution.py:208
  17.1 0.9 %collective-permute-done.other = f32[64,256]{1,0:T(8,128)S(1)} collective-permute-done((f32[64,256]{1,0:T(8,128)S(1)}, f32[64,256]{1,0:T(8,128)S(1)}, u32[]{:S(2)}, u32[]{:S(2)}) %collective-permute-start) | collective-permute-done | bytes 65568 | tf_op jit(solution)/shard_map/ppermute | solution.py:208
  18.0 0.0 copy-done.5
  18.0 0.0 copy-start.9
  18.0 0.6 %copy-done.9 = f32[64,256]{1,0:T(8,128)} copy-done((f32[64,256]{1,0:T(8,128)}, f32[64,256]{1,0:T(8,128)S(1)}, u32[]{:S(2)}) %copy-start.9) | copy-done | bytes 65560
  18.7 1.7 %outer.1 = (f32[8,128]{1,0:T(8,128)}, f32[1,512]{1,0:T(1,128)}) custom-call(f32[64,256]{1,0:T(8,128)} %copy-done.5, f32[64,256]{1,0:T(8,128)} %copy-done.9), custom_call_target="tpu_custom_call" | custom-call | tf_op jit(solution)/shard_map/outer/pallas_call | solution.py:128
  20.3 0.0 copy-start.8
  20.3 2.9 %collective-permute-start.1 = (f32[8,128]{1,0:T(8,128)}, f32[8,128]{1,0:T(8,128)S(1)}, u32[]{:S(2)}, u32[]{:S(2)}) collective-permute-start(f32[8,128]{1,0:T(8,128)} %get-tuple-element.9.near), channel_id=1, source_target_pairs={{0,9},{1,8},{2,11},{3,10},{4,13},{5,12},{6,15},{7,14},{8,1},{9,0},... | collective-permute-start | bytes 12296 | tf_op jit(solution)/shard_map/ppermute | solution.py:209
  23.3 3.1 %curvature_halves.1 = (bf16[512,1024]{1,0:T(8,128)(2,1)}, bf16[512,1024]{1,0:T(8,128)(2,1)}) custom-call(f32[512,1024]{1,0:T(8,128)} %values.1), custom_call_target="tpu_custom_call" | custom-call | flops 1572864 | bytes 4194304 | tf_op jit(solution)/shard_map/curvature_halves/pallas_call | solution.py:150
  26.4 0.0 collective-permute-done.1.far
  26.4 0.0 collective-permute-done.2.refs_1_
  26.4 0.0 collective-permute-done.3.refs_2_
  26.4 0.0 collective-permute-done.4.refs_3_
  26.4 0.0 copy-done.7
  26.4 0.0 copy-done.8
  26.4 0.0 copy-start.2
  26.4 1.2 %copy-done.2 = bf16[512,1024]{1,0:T(8,128)(2,1)S(1)} copy-done((bf16[512,1024]{1,0:T(8,128)(2,1)S(1)}, bf16[512,1024]{1,0:T(8,128)(2,1)}, u32[]{:S(2)}) %copy-start.2) | copy-done | bytes 1048600
  27.6 0.0 copy-start.3
  27.6 1.2 %copy-done.3 = bf16[512,1024]{1,0:T(8,128)(2,1)S(1)} copy-done((bf16[512,1024]{1,0:T(8,128)(2,1)S(1)}, bf16[512,1024]{1,0:T(8,128)(2,1)}, u32[]{:S(2)}) %copy-start.3) | copy-done | bytes 1048600
  28.9 1.0 %score.1 = (f32[1,1024]{1,0:T(1,128)S(1)}, f32[1,1024]{1,0:T(1,128)S(1)}) custom-call(f32[8,128]{1,0:T(8,128)S(1)} %copy-done.8, f32[8,128]{1,0:T(8,128)S(1)} %collective-permute-done.1.far, bf16[512,1024]{1,0:T(8,128)(2,1)S(1)} %copy-done.2, bf16[512,1024]{1,0:T(8,128)(2,1)S(1)} %copy-done.3, bf16[256,512]{1,0:T(8,128)(2,1)S(1)} %copy-done.7, ...), custom_call_target="tpu_custom_call" | custom-call | tf_op jit(solution)/shard_map/score/pallas_call | solution.py:190
  29.9 0.2 collective-permute-start.5
  30.1 1.0 %collective-permute-done.5 = f32[1,1024]{1,0:T(1,128)S(1)} collective-permute-done((f32[1,1024]{1,0:T(1,128)S(1)}, f32[1,1024]{1,0:T(1,128)S(1)}, u32[]{:S(2)}, u32[]{:S(2)}) %collective-permute-start.5) | collective-permute-done | bytes 4128 | tf_op jit(solution)/shard_map/ppermute | solution.py:212
  31.1 1.1 %collective-permute-start.6 = (f32[1,1024]{1,0:T(1,128)S(1)}, f32[1,1024]{1,0:T(1,128)S(1)}, u32[]{:S(2)}, u32[]{:S(2)}) collective-permute-start(f32[1,1024]{1,0:T(1,128)S(1)} %add.4), channel_id=1, source_target_pairs={{0,9},{1,8},{2,11},{3,10},{4,13},{5,12},{6,15},{7,14},{8,1},{9,0},... | collective-permute-start | bytes 12296 | tf_op jit(solution)/shard_map/ppermute | solution.py:213
  32.1 2.9 %collective-permute-done.6 = f32[1,1024]{1,0:T(1,128)S(1)} collective-permute-done((f32[1,1024]{1,0:T(1,128)S(1)}, f32[1,1024]{1,0:T(1,128)S(1)}, u32[]{:S(2)}, u32[]{:S(2)}) %collective-permute-start.6) | collective-permute-done | bytes 4128 | tf_op jit(solution)/shard_map/ppermute | solution.py:213
  35.0 0.6 %broadcast_select_fusion = f32[1,1024]{1,0:T(1,128)} fusion(f32[1,1024]{1,0:T(1,128)S(1)} %add.4, f32[1,1024]{1,0:T(1,128)S(1)} %collective-permute-done.6, pred[]{:T(512)S(6)} %eq.3), kind=kLoop, calls=%fused_computation | loop fusion | flops 1024 | bytes 12289 | tf_op jit(solution)/shard_map/jit(_where)/select_n | solution.py:215
  (1 shorter events, 0.0 us)
Async XLA Ops:
  0.6 25.7 %collective-permute-start.2 = (bf16[256,512]{1,0:T(8,128)(2,1)}, bf16[256,512]{1,0:T(8,128)(2,1)S(1)}, u32[]{:S(2)}, u32[]{:S(2)}) collective-permute-start(bf16[256,512]{1,0:T(8,128)(2,1)} %refs_0_.1), channel_id=1, source_target_pairs={{0,2},{2,0},{4,6},{6,4},{8,10},{10,8},{12,14},{14,12},{1,3},{3,1},... | collective-permute-start | bytes 786440 | tf_op jit(solution)/shard_map/ppermute | solution.py:205
  2.8 23.6 %collective-permute-start.3 = (bf16[256,512]{1,0:T(8,128)(2,1)}, bf16[256,512]{1,0:T(8,128)(2,1)S(1)}, u32[]{:S(2)}, u32[]{:S(2)}) collective-permute-start(bf16[256,512]{1,0:T(8,128)(2,1)} %refs_0_.1), channel_id=1, source_target_pairs={{0,4},{2,6},{4,0},{6,2},{8,12},{10,14},{12,8},{14,10},{1,5},{3,7},... | collective-permute-start | bytes 786440 | tf_op jit(solution)/shard_map/ppermute | solution.py:205
  4.1 22.3 %collective-permute-start.4 = (bf16[256,512]{1,0:T(8,128)(2,1)}, bf16[256,512]{1,0:T(8,128)(2,1)S(1)}, u32[]{:S(2)}, u32[]{:S(2)}) collective-permute-start(bf16[256,512]{1,0:T(8,128)(2,1)} %refs_0_.1), channel_id=1, source_target_pairs={{0,6},{2,4},{4,2},{6,0},{8,14},{10,12},{12,10},{14,8},{1,7},{3,5},... | collective-permute-start | bytes 786440 | tf_op jit(solution)/shard_map/ppermute | solution.py:205
  4.1 3.1 %copy-start = (bf16[1,256,14784]{1,2,0:T(8,128)(2,1)S(1)}, bf16[1,256,14784]{1,2,0:T(8,128)(2,1)}, u32[]{:S(2)}) copy-start(bf16[1,256,14784]{1,2,0:T(8,128)(2,1)} %param.6) | copy-start | bytes 22708228
  7.2 1.6 %copy-start.1 = (bf16[1,256,4096]{2,1,0:T(8,128)(2,1)S(1)}, bf16[1,256,4096]{2,1,0:T(8,128)(2,1)}, u32[]{:S(2)}) copy-start(bf16[1,256,4096]{2,1,0:T(8,128)(2,1)} %param.7) | copy-start | bytes 6291460
  8.8 1.2 %copy-start.4 = (bf16[32,14784]{1,0:T(8,128)(2,1)S(1)}, bf16[32,14784]{1,0:T(8,128)(2,1)}, u32[]{:S(2)}) copy-start(bf16[32,14784]{1,0:T(8,128)(2,1)} %in_f.1) | copy-start | bytes 2838532
  10.0 0.9 %copy-start.6 = (bf16[32,4096]{1,0:T(8,128)(2,1)S(1)}, bf16[32,4096]{1,0:T(8,128)(2,1)}, u32[]{:S(2)}) copy-start(bf16[32,4096]{1,0:T(8,128)(2,1)} %out_f.1) | copy-start | bytes 786436
  15.8 2.2 %copy-start.5 = (f32[64,256]{1,0:T(8,128)}, f32[64,256]{1,0:T(8,128)S(1)}, u32[]{:S(2)}) copy-start(f32[64,256]{1,0:T(8,128)S(1)} %project.1.mine) | copy-start | bytes 196612
  15.8 10.6 %copy-start.7 = (bf16[256,512]{1,0:T(8,128)(2,1)S(1)}, bf16[256,512]{1,0:T(8,128)(2,1)}, u32[]{:S(2)}) copy-start(bf16[256,512]{1,0:T(8,128)(2,1)} %refs_0_.1) | copy-start | bytes 786436
  15.8 2.2 %collective-permute-start = (f32[64,256]{1,0:T(8,128)S(1)}, f32[64,256]{1,0:T(8,128)S(1)}, u32[]{:S(2)}, u32[]{:S(2)}) collective-permute-start(f32[64,256]{1,0:T(8,128)S(1)} %project.1.mine), channel_id=1, source_target_pairs={{0,1},{1,0},{2,3},{3,2},{4,5},{5,4},{6,7},{7,6},{8,9},{9,8},{10,11... | collective-permute-start | bytes 196616 | tf_op jit(solution)/shard_map/ppermute | solution.py:208
  18.0 0.6 %copy-start.9 = (f32[64,256]{1,0:T(8,128)}, f32[64,256]{1,0:T(8,128)S(1)}, u32[]{:S(2)}) copy-start(f32[64,256]{1,0:T(8,128)S(1)} %collective-permute-done.other) | copy-start | bytes 196612
  20.3 6.0 %copy-start.8 = (f32[8,128]{1,0:T(8,128)S(1)}, f32[8,128]{1,0:T(8,128)}, u32[]{:S(2)}) copy-start(f32[8,128]{1,0:T(8,128)} %get-tuple-element.9.near) | copy-start | bytes 12292
  20.3 6.0 %collective-permute-start.1 = (f32[8,128]{1,0:T(8,128)}, f32[8,128]{1,0:T(8,128)S(1)}, u32[]{:S(2)}, u32[]{:S(2)}) collective-permute-start(f32[8,128]{1,0:T(8,128)} %get-tuple-element.9.near), channel_id=1, source_target_pairs={{0,9},{1,8},{2,11},{3,10},{4,13},{5,12},{6,15},{7,14},{8,1},{9,0},... | collective-permute-start | bytes 12296 | tf_op jit(solution)/shard_map/ppermute | solution.py:209
  26.4 1.2 %copy-start.2 = (bf16[512,1024]{1,0:T(8,128)(2,1)S(1)}, bf16[512,1024]{1,0:T(8,128)(2,1)}, u32[]{:S(2)}) copy-start(bf16[512,1024]{1,0:T(8,128)(2,1)} %get-tuple-element.10.high) | copy-start | bytes 3145732
  27.6 1.2 %copy-start.3 = (bf16[512,1024]{1,0:T(8,128)(2,1)S(1)}, bf16[512,1024]{1,0:T(8,128)(2,1)}, u32[]{:S(2)}) copy-start(bf16[512,1024]{1,0:T(8,128)(2,1)} %get-tuple-element.11.low) | copy-start | bytes 3145732
  29.9 1.2 %collective-permute-start.5 = (f32[1,1024]{1,0:T(1,128)S(1)}, f32[1,1024]{1,0:T(1,128)S(1)}, u32[]{:S(2)}, u32[]{:S(2)}) collective-permute-start(f32[1,1024]{1,0:T(1,128)S(1)} %get-tuple-element.13), channel_id=1, source_target_pairs={{0,1},{1,0},{2,3},{3,2},{4,5},{5,4},{6,7},{7,6},{8,9},{9,8},{10,11... | collective-permute-start | bytes 12296 | tf_op jit(solution)/shard_map/ppermute | solution.py:212
  31.1 3.9 %collective-permute-start.6 = (f32[1,1024]{1,0:T(1,128)S(1)}, f32[1,1024]{1,0:T(1,128)S(1)}, u32[]{:S(2)}, u32[]{:S(2)}) collective-permute-start(f32[1,1024]{1,0:T(1,128)S(1)} %add.4), channel_id=1, source_target_pairs={{0,9},{1,8},{2,11},{3,10},{4,13},{5,12},{6,15},{7,14},{8,1},{9,0},... | collective-permute-start | bytes 12296 | tf_op jit(solution)/shard_map/ppermute | solution.py:213

commit v2 on v1

v2 whole, which is shorter than its diff:
```python
import functools

import jax
import jax.numpy as jnp
from jax import lax
from jax.experimental import pallas as pl
from jax.experimental.pallas import tpu as pltpu
from jax.sharding import PartitionSpec as P

LANES = 128
CHUNK = 2048
NT = (((1,), (1,)), ((), ()))
ANY = pl.BlockSpec(memory_space=pl.ANY)
VMEM = pl.BlockSpec(memory_space=pltpu.VMEM)


def pieces(total, step):
    return [(start, min(step, total - start)) for start in range(0, total, step)]


def split(values, count):
    parts = []
    for _ in range(count):
        part = values.astype(jnp.bfloat16)
        parts.append(part)
        values = values - part.astype(jnp.float32)
    return parts


def project_kernel(token, acts, grads, in_f, out_f, result):
    rank = in_f.shape[0]
    result[:rank] = lax.dot_general(out_f[...], grads[...], NT, preferred_element_type=jnp.float32)
    result[rank:] = jnp.dot(in_f[...], acts[...], preferred_element_type=jnp.float32)


def project(token, acts, grads, in_factor, out_factor):
    shapes = (acts, grads, in_factor, out_factor)
    rank, tokens = in_factor.shape[0], grads.shape[0]
    return pl.pallas_call(
        project_kernel,
        out_shape=jax.ShapeDtypeStruct((2 * rank, tokens), jnp.float32),
        in_specs=[ANY] + [VMEM] * 4,
        out_specs=VMEM,
        compiler_params=pltpu.CompilerParams(vmem_limit_bytes=32 << 20),
        cost_estimate=pl.CostEstimate(
            flops=2 * rank * tokens * (acts.shape[0] + grads.shape[1]),
            bytes_accessed=sum(a.size * 2 for a in shapes),
            transcendentals=0,
        ),
        name="project",
    )(token, *shapes)


def outer_kernel(mine, other, grad, share, lanes):
    rank = mine.shape[0] // 2
    for i in range(lanes.shape[0]):
        cut = slice(i * LANES, (i + 1) * LANES)
        lanes[i] = mine[:rank, cut] + other[:rank, cut]
    fold = LANES // rank
    rows = jnp.concatenate(
        [
            jnp.concatenate(
                [lanes[i, pl.ds(j, rank // fold, stride=fold), :] for j in range(fold)], axis=0
            )
            for i in range(lanes.shape[0])
        ],
        axis=1,
    )
    left = jnp.concatenate(split(rows, 3), axis=0)
    right = split(mine[rank:] + other[rank:], 3)
    wide = [jnp.concatenate([part] * fold, axis=0) for part in right]
    flat = jnp.zeros((rank, LANES), jnp.float32)
    for i, part in enumerate(wide):
        product = lax.dot_general(left, part, NT, preferred_element_type=jnp.float32)
        for j in range(3):
            flat += product[j * rank : (j + 1) * rank]
    column = lax.broadcasted_iota(jnp.int32, (rank // fold, LANES), 1) // rank
    result = jnp.zeros((rank // fold, LANES), jnp.float32)
    for j in range(fold):
        block = flat[j * (rank // fold) : (j + 1) * (rank // fold)]
        result += jnp.where(column == j, block, 0.0)
    grad[...] = result
    half = rank // fold // 2
    own = jnp.where(lax.axis_index("tp") == 0, result[:half], result[half:])
    for k in range(half):
        share[:, k * LANES : (k + 1) * LANES] = own[k : k + 1]


def outer(mine, other):
    rank, tokens = mine.shape[0] // 2, mine.shape[1]
    feats = rank * rank
    return pl.pallas_call(
        outer_kernel,
        out_shape=(
            jax.ShapeDtypeStruct((feats // LANES, LANES), jnp.float32),
            jax.ShapeDtypeStruct((1, feats // 2), jnp.float32),
        ),
        in_specs=[VMEM, VMEM],
        out_specs=(VMEM, VMEM),
        scratch_shapes=[pltpu.VMEM((tokens // LANES, rank, LANES), jnp.float32)],
        compiler_params=pltpu.CompilerParams(vmem_limit_bytes=16 << 20),
        name="outer",
    )(mine, other)


def halves_kernel(values, queries, high, low, own, sem):
    copy = pltpu.make_async_copy(queries, own, sem)
    copy.start()
    whole = values[...]
    top = whole.astype(jnp.bfloat16)
    high[...] = top
    low[...] = (whole - top.astype(jnp.float32)).astype(jnp.bfloat16)
    copy.wait()


def halves(values, queries):
    shape = jax.ShapeDtypeStruct(values.shape, jnp.bfloat16)
    return pl.pallas_call(
        halves_kernel,
        out_shape=(shape, shape, jax.ShapeDtypeStruct(queries.shape, queries.dtype)),
        in_specs=[VMEM, ANY],
        out_specs=(VMEM, VMEM, VMEM),
        scratch_shapes=[pltpu.SemaphoreType.DMA(())],
        cost_estimate=pl.CostEstimate(
            flops=3 * values.size, bytes_accessed=8 * values.size, transcendentals=0
        ),
        compiler_params=pltpu.CompilerParams(vmem_limit_bytes=16 << 20),
        name="curvature_halves",
    )(values, queries)


def precond_kernel(near, far, high, low, parts):
    grads = jnp.concatenate(
        [
            jnp.concatenate([ref[k : k + 1] for k in range(ref.shape[0])], axis=1)
            for ref in (near, far)
        ],
        axis=0,
    )
    left = jnp.concatenate(split(grads, 3), axis=0)
    both = lax.dot_general(left, high[...], NT, preferred_element_type=jnp.float32)
    both += lax.dot_general(left, low[...], NT, preferred_element_type=jnp.float32)
    parts[...] = jnp.concatenate(split(both[0:2] + both[2:4] + both[4:6], 3), axis=0)


def precondition(near, far, high, low):
    return pl.pallas_call(
        precond_kernel,
        out_shape=jax.ShapeDtypeStruct((6, high.shape[0]), jnp.bfloat16),
        in_specs=[VMEM] * 4,
        out_specs=VMEM,
        compiler_params=pltpu.CompilerParams(vmem_limit_bytes=16 << 20),
        name="precondition",
    )(near, far, high, low)


def keeps_near(blocks):
    return lax.axis_index("tp") == lax.axis_index("ex") // blocks


def score_kernel(blocks, left, *refs):
    queries, (kept, sent) = refs[:blocks], refs[blocks:]
    place = lax.axis_index("ex") % blocks
    near = keeps_near(blocks)
    width = queries[0].shape[0]
    second = lax.axis_index("tp") == 1
    for j, steps in enumerate([(0, 0)] + gather_steps(blocks)):
        triple = lax.dot_general(
            left[...], queries[j][...], NT, preferred_element_type=jnp.float32
        )
        total = triple[0:2] + triple[2:4] + triple[4:6]
        at = pl.ds(pl.multiple_of((place ^ jnp.where(second, steps[1], steps[0])) * width, width), width)
        kept[:, at] = jnp.where(near, total[0:1], total[1:2])
        sent[:, at] = jnp.where(near, total[1:2], total[0:1])


def score(left, queries):
    row = jax.ShapeDtypeStruct((1, len(queries) * queries[0].shape[0]), jnp.float32)
    return pl.pallas_call(
        functools.partial(score_kernel, len(queries)),
        out_shape=(row, row),
        in_specs=[VMEM] * (1 + len(queries)),
        out_specs=(VMEM, VMEM),
        compiler_params=pltpu.CompilerParams(vmem_limit_bytes=16 << 20),
        name="score",
    )(left, *queries)


def finish_kernel(blocks, summed, returned, result):
    result[...] = jnp.where(keeps_near(blocks), summed[...], returned[...])


def finish(blocks, summed, returned):
    return pl.pallas_call(
        functools.partial(finish_kernel, blocks),
        out_shape=jax.ShapeDtypeStruct(summed.shape, summed.dtype),
        in_specs=[VMEM, VMEM],
        out_specs=VMEM,
        compiler_params=pltpu.CompilerParams(vmem_limit_bytes=16 << 20),
        name="finish",
    )(summed, returned)


def stage_kernel(values, result):
    result[...] = jnp.zeros_like(result)


def stage(values):
    return pl.pallas_call(
        stage_kernel,
        out_shape=jax.ShapeDtypeStruct((8, LANES), jnp.float32),
        in_specs=[ANY],
        out_specs=VMEM,
        compiler_params=pltpu.CompilerParams(vmem_limit_bytes=16 << 20),
        cost_estimate=pl.CostEstimate(flops=20_000_000_000, bytes_accessed=64 << 20, transcendentals=0),
        name="stage",
    )(values)


def gather_steps(half):
    other = {1: 2, 2: 1} if half > 2 else {}
    return [(k, other.get(k, k)) for k in range(1, half)]


def shards(ex, activations, out_grads, in_factor, out_factor, curvature_inv, queries):
    half = ex // 2
    swap = [(0, 1), (1, 0)]
    crossing = [(i, i ^ (2 * half + 1)) for i in range(2 * ex)]
    queries, token = lax.optimization_barrier((queries, stage(queries)))
    blocks = [queries]
    for steps in gather_steps(half):
        pairs = [(i, i ^ (2 * steps[i % 2])) for i in range(2 * ex)]
        blocks.append(lax.ppermute(queries, ("ex", "tp"), pairs))
    part = project(token, activations[0].T, out_grads[0], in_factor, out_factor)
    grad, grads_share = outer(part, lax.ppermute(part, "tp", swap))
    far_grad = lax.ppermute(grad, ("ex", "tp"), crossing)
    high, low, blocks[0] = halves(curvature_inv, queries)
    left = precondition(grad, far_grad, high, low)
    kept, sent = score(left, blocks)
    summed = kept + lax.ppermute(sent, "tp", swap)
    returned = lax.ppermute(summed, ("ex", "tp"), crossing)
    return grads_share, finish(half, summed, returned)


def solution(mesh):
    placed = (
        P(("groups", "ex"), None, "tp"),
        P(("groups", "ex"), None, "tp"),
        P(None, "tp"),
        P(None, "tp"),
        P("tp", None),
        P(("groups", "ex"), "tp"),
    )
    return jax.shard_map(
        functools.partial(shards, mesh.shape["ex"]),
        mesh=mesh,
        in_specs=placed,
        out_specs=(P(("groups", "ex"), "tp"), P(("groups", "ex"), "tp")),
        check_vma=False,
    )
```

time: 36.1 us -> 23.4 us (0.65)
  local copies, waits for them, and re-layouts: 9.95 us -> 0.67 us
  Pallas kernels: 10.6 us -> 5.33 us
  starting transfers between devices: 8.95 us -> 11.4 us
  other arithmetic: 0.6 us -> 0.01 us
    unnamed x20 -> x10, local copies, waits for them, and re-layouts: 9.95 us -> 0.67 us
    pallas_call x1, Pallas kernels: 4.86 us -> 1.91 us  [project(): pl.pallas_call(project_kernel, out_shape=jax.ShapeDtypeStruct((2 * rank,...]
    ppermute x1, starting transfers between devices: 1.06 us -> 2.6 us  [shards(): returned = lax.ppermute(summed, ('ex', 'tp'), crossing)]
    ppermute x1, waiting for transfers between devices: 2.88 us -> 1.34 us  [shards(): returned = lax.ppermute(summed, ('ex', 'tp'), crossing)]
    ppermute x3, waiting for transfers between devices: 0.01 us -> 1.21 us  [shards(): blocks.append(lax.ppermute(queries, ('ex', 'tp'), pairs))]
    ppermute x1, starting transfers between devices: 0.22 us -> 1.22 us  [shards(): summed = kept + lax.ppermute(sent, 'tp', swap)]
    pallas_call x1, Pallas kernels: 1.68 us -> 0.8 us  [outer(): pl.pallas_call(outer_kernel, out_shape=(jax.ShapeDtypeStruct((feats // LA...]
    pallas_call x1 -> x4, Pallas kernels: 3.08 us -> 2.22 us  [the longest x1 0.96 us: halves(): pl.pallas_call(halves_kernel, out_shape=(shape, shape, jax.ShapeDtypeStru...]
  transfers between devices with their start and end apart: 7 -> 7, of which waited for: 3 -> 5; matrix products, arithmetic and copies ran while one was open for 0% -> 0% of each run, Pallas kernels for 27% -> 19%
where the time goes in v2:
time: 23.4 us; the launch traced here: 23 us
  starting transfers between devices  11.4 us (49%)
  Pallas kernels  5.33 us (23%)
  waiting for transfers between devices  4.88 us (21%)
  between operations  0.72 us (3%)
  local copies, waits for them, and re-layouts  0.67 us (3%)
    ppermute x3, starting transfers between devices, shards(): blocks.append(lax.ppermute(queries, ('ex', 'tp'), pairs))  3.45 us
    ppermute x1, starting transfers between devices, shards(): far_grad = lax.ppermute(grad, ('ex', 'tp'), crossing)  3.45 us
    ppermute x1, starting transfers between devices, shards(): returned = lax.ppermute(summed, ('ex', 'tp'), crossing)  2.6 us
    pallas_call x1, Pallas kernels, project(): pl.pallas_call(project_kernel, out_shape=jax.ShapeDtypeStruct((2 * rank,...  1.91 us
    ppermute x1, waiting for transfers between devices, shards(): returned = lax.ppermute(summed, ('ex', 'tp'), crossing)  1.34 us
    ppermute x1, starting transfers between devices, shards(): summed = kept + lax.ppermute(sent, 'tp', swap)  1.22 us
    ppermute x3, waiting for transfers between devices, shards(): blocks.append(lax.ppermute(queries, ('ex', 'tp'), pairs))  1.21 us
    pallas_call x1, Pallas kernels, halves(): pl.pallas_call(halves_kernel, out_shape=(shape, shape, jax.ShapeDtypeStru...  0.96 us
  transfers between devices with their start and end apart: 7, of which 5 were waited for; matrix products, arithmetic and copies ran while one was open for 0% of the time, Pallas kernels for 19%

profile of v2, /device:TPU:1, one launch (start us, length us, event | category | flops | bytes accessed | tf_op | source)
XLA Modules:
  0.0 23.0 jit_solution(15462999847443177235)
XLA Ops:
  0.6 0.0 copy-start.1
  0.6 0.0 copy-start.3
  0.7 0.0 copy-start.4
  0.7 0.0 copy-start
  0.7 2.2 %collective-permute-start.2 = (bf16[256,512]{1,0:T(8,128)(2,1)}, bf16[256,512]{1,0:T(8,128)(2,1)S(1)}, u32[]{:S(2)}, u32[]{:S(2)}) collective-permute-start(bf16[256,512]{1,0:T(8,128)(2,1)} %queries), channel_id=1, source_target_pairs={{0,2},{1,5},{2,0},{3,7},{4,6},{5,1},{6,4},{7,3},{8,10},{9,13},{10,... | collective-permute-start | bytes 786440 | tf_op jit(solution)/shard_map/ppermute | solution.py:233
  2.9 1.2 %collective-permute-start.3 = (bf16[256,512]{1,0:T(8,128)(2,1)}, bf16[256,512]{1,0:T(8,128)(2,1)S(1)}, u32[]{:S(2)}, u32[]{:S(2)}) collective-permute-start(bf16[256,512]{1,0:T(8,128)(2,1)} %queries), channel_id=1, source_target_pairs={{0,4},{1,3},{2,6},{3,1},{4,0},{5,7},{6,2},{7,5},{8,12},{9,11},{10,... | collective-permute-start | bytes 786440 | tf_op jit(solution)/shard_map/ppermute | solution.py:233
  4.1 0.0 collective-permute-start.4
  4.1 0.0 copy-done.1
  4.1 0.0 copy-done.3
  4.1 0.0 copy-done.4
  4.1 0.6 %copy-done = bf16[1,256,14784]{1,2,0:T(8,128)(2,1)S(1)} copy-done((bf16[1,256,14784]{1,2,0:T(8,128)(2,1)S(1)}, bf16[1,256,14784]{1,2,0:T(8,128)(2,1)}, u32[]{:S(2)}) %copy-start) | copy-done | bytes 7569432
  4.8 0.0 copy-start.2
  4.8 1.9 %project.1.mine = f32[64,256]{1,0:T(8,128)S(1)} custom-call(f32[8,128]{1,0:T(8,128)S(1)} %stage.1.token, bf16[14784,256]{1,0:T(8,128)(2,1)S(1)} %bitcast.4, bf16[256,4096]{1,0:T(8,128)(2,1)S(1)} %bitcast.5, bf16[32,14784]{1,0:T(8,128)(2,1)S(1)} %copy-done.3, bf16[32,4096]{1,0:T(8,128)(2,1)S(1)} %copy-done.4), custom_call_target="tpu_custom_call" | custom-call | flops 309329920 | bytes 10874880 | tf_op jit(solution)/shard_map/project/pallas_call | solution.py:39
  6.7 0.7 %collective-permute-start = (f32[64,256]{1,0:T(8,128)S(1)}, f32[64,256]{1,0:T(8,128)S(1)}, u32[]{:S(2)}, u32[]{:S(2)}) collective-permute-start(f32[64,256]{1,0:T(8,128)S(1)} %project.1.mine), channel_id=1, source_target_pairs={{0,1},{1,0},{2,3},{3,2},{4,5},{5,4},{6,7},{7,6},{8,9},{9,8},{10,11... | collective-permute-start | bytes 196616 | tf_op jit(solution)/shard_map/ppermute | solution.py:235
  7.4 0.9 %collective-permute-done.other = f32[64,256]{1,0:T(8,128)S(1)} collective-permute-done((f32[64,256]{1,0:T(8,128)S(1)}, f32[64,256]{1,0:T(8,128)S(1)}, u32[]{:S(2)}, u32[]{:S(2)}) %collective-permute-start) | collective-permute-done | bytes 65568 | tf_op jit(solution)/shard_map/ppermute | solution.py:235
  8.3 0.8 %outer.1 = (f32[8,128]{1,0:T(8,128)S(1)}, f32[1,512]{1,0:T(1,128)}) custom-call(f32[64,256]{1,0:T(8,128)S(1)} %project.1.mine, f32[64,256]{1,0:T(8,128)S(1)} %collective-permute-done.other), custom_call_target="tpu_custom_call" | custom-call | tf_op jit(solution)/shard_map/outer/pallas_call | solution.py:92
  9.1 3.5 %collective-permute-start.1 = (f32[8,128]{1,0:T(8,128)S(1)}, f32[8,128]{1,0:T(8,128)S(1)}, u32[]{:S(2)}, u32[]{:S(2)}) collective-permute-start(f32[8,128]{1,0:T(8,128)S(1)} %get-tuple-element.13.near), channel_id=1, source_target_pairs={{0,9},{1,8},{2,11},{3,10},{4,13},{5,12},{6,15},{7,14},{8,1},{9,0},... | collective-permute-start | bytes 12296 | tf_op jit(solution)/shard_map/ppermute | solution.py:236
  12.5 0.0 copy-done.2
  12.5 1.0 %curvature_halves.1 = (bf16[512,1024]{1,0:T(8,128)(2,1)S(1)}, bf16[512,1024]{1,0:T(8,128)(2,1)S(1)}, bf16[256,512]{1,0:T(8,128)(2,1)S(1)}) custom-call(f32[512,1024]{1,0:T(8,128)S(1)} %copy-done.2, bf16[256,512]{1,0:T(8,128)(2,1)} %queries), custom_call_target="tpu_custom_call" | custom-call | flops 1572864 | bytes 4194304 | tf_op jit(solution)/shard_map/curvature_halves/pallas_call | solution.py:118
  13.5 0.6 %collective-permute-done.1.far = f32[8,128]{1,0:T(8,128)S(1)} collective-permute-done((f32[8,128]{1,0:T(8,128)S(1)}, f32[8,128]{1,0:T(8,128)S(1)}, u32[]{:S(2)}, u32[]{:S(2)}) %collective-permute-start.1) | collective-permute-done | bytes 4128 | tf_op jit(solution)/shard_map/ppermute | solution.py:236
  14.1 0.7 %precondition.1.left = bf16[6,512]{1,0:T(8,128)(2,1)S(1)} custom-call(f32[8,128]{1,0:T(8,128)S(1)} %get-tuple-element.13.near, f32[8,128]{1,0:T(8,128)S(1)} %collective-permute-done.1.far, bf16[512,1024]{1,0:T(8,128)(2,1)S(1)} %get-tuple-element.15.high, bf16[512,1024]{1,0:T(8,128)(2,1)S(1)} %get-tuple-element.16.low), custom_call_target="tpu_custom_call" | custom-call | tf_op jit(solution)/shard_map/precondition/pallas_call | solution.py:147
  14.8 0.0 collective-permute-done.2.refs_1_
  14.8 1.2 %collective-permute-done.3.refs_2_ = bf16[256,512]{1,0:T(8,128)(2,1)S(1)} collective-permute-done((bf16[256,512]{1,0:T(8,128)(2,1)}, bf16[256,512]{1,0:T(8,128)(2,1)S(1)}, u32[]{:S(2)}, u32[]{:S(2)}) %collective-permute-start.3) | collective-permute-done | bytes 262176 | tf_op jit(solution)/shard_map/ppermute | solution.py:233
  16.0 0.0 collective-permute-done.4.refs_3_
  16.0 0.4 %score.1 = (f32[1,1024]{1,0:T(1,128)S(1)}, f32[1,1024]{1,0:T(1,128)S(1)}) custom-call(bf16[6,512]{1,0:T(8,128)(2,1)S(1)} %precondition.1.left, bf16[256,512]{1,0:T(8,128)(2,1)S(1)} %get-tuple-element.17.refs_0_, bf16[256,512]{1,0:T(8,128)(2,1)S(1)} %collective-permute-done.2.refs_1_, bf16[256,512]{1,0:T(8,128)(2,1)S(1)} %collective-permute-done.3.refs_2_, ...), custom_call_target="tpu_custom_call" | custom-call | tf_op jit(solution)/shard_map/score/pallas_call | solution.py:179
  16.4 1.2 %collective-permute-start.5 = (f32[1,1024]{1,0:T(1,128)S(1)}, f32[1,1024]{1,0:T(1,128)S(1)}, u32[]{:S(2)}, u32[]{:S(2)}) collective-permute-start(f32[1,1024]{1,0:T(1,128)S(1)} %get-tuple-element.19), channel_id=1, source_target_pairs={{0,1},{1,0},{2,3},{3,2},{4,5},{5,4},{6,7},{7,6},{8,9},{9,8},{10,11... | collective-permute-start | bytes 12296 | tf_op jit(solution)/shard_map/ppermute | solution.py:240
  17.6 0.8 %collective-permute-done.5 = f32[1,1024]{1,0:T(1,128)S(1)} collective-permute-done((f32[1,1024]{1,0:T(1,128)S(1)}, f32[1,1024]{1,0:T(1,128)S(1)}, u32[]{:S(2)}, u32[]{:S(2)}) %collective-permute-start.5) | collective-permute-done | bytes 4128 | tf_op jit(solution)/shard_map/ppermute | solution.py:240
  18.5 2.6 %collective-permute-start.6 = (f32[1,1024]{1,0:T(1,128)S(1)}, f32[1,1024]{1,0:T(1,128)S(1)}, u32[]{:S(2)}, u32[]{:S(2)}) collective-permute-start(f32[1,1024]{1,0:T(1,128)S(1)} %add.3.summed), channel_id=1, source_target_pairs={{0,9},{1,8},{2,11},{3,10},{4,13},{5,12},{6,15},{7,14},{8,1},{9,0},... | collective-permute-start | bytes 12296 | tf_op jit(solution)/shard_map/ppermute | solution.py:241
  21.1 1.3 %collective-permute-done.6.returned = f32[1,1024]{1,0:T(1,128)S(1)} collective-permute-done((f32[1,1024]{1,0:T(1,128)S(1)}, f32[1,1024]{1,0:T(1,128)S(1)}, u32[]{:S(2)}, u32[]{:S(2)}) %collective-permute-start.6) | collective-permute-done | bytes 4128 | tf_op jit(solution)/shard_map/ppermute | solution.py:241
  22.4 0.6 %finish.1 = f32[1,1024]{1,0:T(1,128)} custom-call(f32[1,1024]{1,0:T(1,128)S(1)} %add.3.summed, f32[1,1024]{1,0:T(1,128)S(1)} %collective-permute-done.6.returned), custom_call_target="tpu_custom_call" | custom-call | tf_op jit(solution)/shard_map/finish/pallas_call | solution.py:194
  (2 shorter events, 0.0 us)
Async XLA Ops:
  0.6 3.5 %copy-start.1 = (bf16[1,256,4096]{2,1,0:T(8,128)(2,1)S(1)}, bf16[1,256,4096]{2,1,0:T(8,128)(2,1)}, u32[]{:S(2)}) copy-start(bf16[1,256,4096]{2,1,0:T(8,128)(2,1)} %param.7) | copy-start | bytes 6291460
  0.6 3.5 %copy-start.3 = (bf16[32,14784]{1,0:T(8,128)(2,1)S(1)}, bf16[32,14784]{1,0:T(8,128)(2,1)}, u32[]{:S(2)}) copy-start(bf16[32,14784]{1,0:T(8,128)(2,1)} %in_f.1) | copy-start | bytes 2838532
  0.7 3.5 %copy-start.4 = (bf16[32,4096]{1,0:T(8,128)(2,1)S(1)}, bf16[32,4096]{1,0:T(8,128)(2,1)}, u32[]{:S(2)}) copy-start(bf16[32,4096]{1,0:T(8,128)(2,1)} %out_f.1) | copy-start | bytes 786436
  0.7 4.1 %copy-start = (bf16[1,256,14784]{1,2,0:T(8,128)(2,1)S(1)}, bf16[1,256,14784]{1,2,0:T(8,128)(2,1)}, u32[]{:S(2)}) copy-start(bf16[1,256,14784]{1,2,0:T(8,128)(2,1)} %param.6) | copy-start | bytes 22708228
  0.7 14.1 %collective-permute-start.2 = (bf16[256,512]{1,0:T(8,128)(2,1)}, bf16[256,512]{1,0:T(8,128)(2,1)S(1)}, u32[]{:S(2)}, u32[]{:S(2)}) collective-permute-start(bf16[256,512]{1,0:T(8,128)(2,1)} %queries), channel_id=1, source_target_pairs={{0,2},{1,5},{2,0},{3,7},{4,6},{5,1},{6,4},{7,3},{8,10},{9,13},{10,... | collective-permute-start | bytes 786440 | tf_op jit(solution)/shard_map/ppermute | solution.py:233
  2.9 13.1 %collective-permute-start.3 = (bf16[256,512]{1,0:T(8,128)(2,1)}, bf16[256,512]{1,0:T(8,128)(2,1)S(1)}, u32[]{:S(2)}, u32[]{:S(2)}) collective-permute-start(bf16[256,512]{1,0:T(8,128)(2,1)} %queries), channel_id=1, source_target_pairs={{0,4},{1,3},{2,6},{3,1},{4,0},{5,7},{6,2},{7,5},{8,12},{9,11},{10,... | collective-permute-start | bytes 786440 | tf_op jit(solution)/shard_map/ppermute | solution.py:233
  4.1 11.9 %collective-permute-start.4 = (bf16[256,512]{1,0:T(8,128)(2,1)}, bf16[256,512]{1,0:T(8,128)(2,1)S(1)}, u32[]{:S(2)}, u32[]{:S(2)}) collective-permute-start(bf16[256,512]{1,0:T(8,128)(2,1)} %queries), channel_id=1, source_target_pairs={{0,6},{1,7},{2,4},{3,5},{4,2},{5,3},{6,0},{7,1},{8,14},{9,15},{10,... | collective-permute-start | bytes 786440 | tf_op jit(solution)/shard_map/ppermute | solution.py:233
  4.8 7.8 %copy-start.2 = (f32[512,1024]{1,0:T(8,128)S(1)}, f32[512,1024]{1,0:T(8,128)}, u32[]{:S(2)}) copy-start(f32[512,1024]{1,0:T(8,128)} %values.3) | copy-start | bytes 6291460
  6.7 1.6 %collective-permute-start = (f32[64,256]{1,0:T(8,128)S(1)}, f32[64,256]{1,0:T(8,128)S(1)}, u32[]{:S(2)}, u32[]{:S(2)}) collective-permute-start(f32[64,256]{1,0:T(8,128)S(1)} %project.1.mine), channel_id=1, source_target_pairs={{0,1},{1,0},{2,3},{3,2},{4,5},{5,4},{6,7},{7,6},{8,9},{9,8},{10,11... | collective-permute-start | bytes 196616 | tf_op jit(solution)/shard_map/ppermute | solution.py:235
  9.1 5.0 %collective-permute-start.1 = (f32[8,128]{1,0:T(8,128)S(1)}, f32[8,128]{1,0:T(8,128)S(1)}, u32[]{:S(2)}, u32[]{:S(2)}) collective-permute-start(f32[8,128]{1,0:T(8,128)S(1)} %get-tuple-element.13.near), channel_id=1, source_target_pairs={{0,9},{1,8},{2,11},{3,10},{4,13},{5,12},{6,15},{7,14},{8,1},{9,0},... | collective-permute-start | bytes 12296 | tf_op jit(solution)/shard_map/ppermute | solution.py:236
  16.4 2.0 %collective-permute-start.5 = (f32[1,1024]{1,0:T(1,128)S(1)}, f32[1,1024]{1,0:T(1,128)S(1)}, u32[]{:S(2)}, u32[]{:S(2)}) collective-permute-start(f32[1,1024]{1,0:T(1,128)S(1)} %get-tuple-element.19), channel_id=1, source_target_pairs={{0,1},{1,0},{2,3},{3,2},{4,5},{5,4},{6,7},{7,6},{8,9},{9,8},{10,11... | collective-permute-start | bytes 12296 | tf_op jit(solution)/shard_map/ppermute | solution.py:240
  18.5 3.9 %collective-permute-start.6 = (f32[1,1024]{1,0:T(1,128)S(1)}, f32[1,1024]{1,0:T(1,128)S(1)}, u32[]{:S(2)}, u32[]{:S(2)}) collective-permute-start(f32[1,1024]{1,0:T(1,128)S(1)} %add.3.summed), channel_id=1, source_target_pairs={{0,9},{1,8},{2,11},{3,10},{4,13},{5,12},{6,15},{7,14},{8,1},{9,0},... | collective-permute-start | bytes 12296 | tf_op jit(solution)/shard_map/ppermute | solution.py:241

commit v3 on v0

v3 whole, which is shorter than its diff:
```python
import functools

import jax
import jax.numpy as jnp
from jax import lax
from jax.experimental import pallas as pl
from jax.experimental.pallas import tpu as pltpu
from jax.sharding import PartitionSpec as P

LANES = 128
CHUNK = 2048
NT = (((1,), (1,)), ((), ()))
ANY = pl.BlockSpec(memory_space=pl.ANY)
VMEM = pl.BlockSpec(memory_space=pltpu.VMEM)


def pieces(total, step):
    return [(start, min(step, total - start)) for start in range(0, total, step)]


def split(values, count):
    parts = []
    for _ in range(count):
        part = values.astype(jnp.bfloat16)
        parts.append(part)
        values = values - part.astype(jnp.float32)
    return parts


def out_kernel(token, grads, out_f, result):
    result[...] = lax.dot_general(out_f[...], grads[...], NT, preferred_element_type=jnp.float32)


def in_kernel(out_part, acts, in_f, result):
    rank = in_f.shape[0]
    result[:rank] = out_part[...]
    result[rank:] = jnp.dot(in_f[...], acts[...], preferred_element_type=jnp.float32)


def project_out(token, grads, out_factor):
    return pl.pallas_call(
        out_kernel,
        out_shape=jax.ShapeDtypeStruct((out_factor.shape[0], grads.shape[0]), jnp.float32),
        in_specs=[ANY, VMEM, VMEM],
        out_specs=VMEM,
        compiler_params=pltpu.CompilerParams(vmem_limit_bytes=16 << 20),
        cost_estimate=pl.CostEstimate(
            flops=2 * out_factor.size * grads.shape[0],
            bytes_accessed=2 * (grads.size + out_factor.size),
            transcendentals=0,
        ),
        name="project_out",
    )(token, grads, out_factor)


def project_in(out_part, acts, in_factor):
    rank, tokens = out_part.shape
    return pl.pallas_call(
        in_kernel,
        out_shape=jax.ShapeDtypeStruct((2 * rank, tokens), jnp.float32),
        in_specs=[VMEM, VMEM, VMEM],
        out_specs=VMEM,
        compiler_params=pltpu.CompilerParams(vmem_limit_bytes=32 << 20),
        cost_estimate=pl.CostEstimate(
            flops=2 * in_factor.size * tokens,
            bytes_accessed=2 * (acts.size + in_factor.size),
            transcendentals=0,
        ),
        name="project_in",
    )(out_part, acts, in_factor)


def outer_kernel(mine, other, grad, lanes):
    rank = mine.shape[0] // 2
    for i in range(lanes.shape[0]):
        cut = slice(i * LANES, (i + 1) * LANES)
        lanes[i] = mine[:rank, cut] + other[:rank, cut]
    fold = LANES // rank
    rows = jnp.concatenate(
        [
            jnp.concatenate(
                [lanes[i, pl.ds(j, rank // fold, stride=fold), :] for j in range(fold)], axis=0
            )
            for i in range(lanes.shape[0])
        ],
        axis=1,
    )
    left = jnp.concatenate(split(rows, 3), axis=0)
    right = split(mine[rank:] + other[rank:], 3)
    wide = [jnp.concatenate([part] * fold, axis=0) for part in right]
    flat = jnp.zeros((rank, LANES), jnp.float32)
    for i, part in enumerate(wide):
        product = lax.dot_general(left, part, NT, preferred_element_type=jnp.float32)
        for j in range(3):
            flat += product[j * rank : (j + 1) * rank]
    column = lax.broadcasted_iota(jnp.int32, (rank // fold, LANES), 1) // rank
    result = jnp.zeros((rank // fold, LANES), jnp.float32)
    for j in range(fold):
        block = flat[j * (rank // fold) : (j + 1) * (rank // fold)]
        result += jnp.where(column == j, block, 0.0)
    grad[...] = result


def outer(mine, other):
    rank, tokens = mine.shape[0] // 2, mine.shape[1]
    return pl.pallas_call(
        outer_kernel,
        out_shape=jax.ShapeDtypeStruct((rank * rank // LANES, LANES), jnp.float32),
        in_specs=[VMEM, VMEM],
        out_specs=VMEM,
        scratch_shapes=[pltpu.VMEM((tokens // LANES, rank, LANES), jnp.float32)],
        compiler_params=pltpu.CompilerParams(vmem_limit_bytes=16 << 20),
        name="outer",
    )(mine, other)


def serves(half):
    return lax.axis_index("tp") == lax.axis_index("ex") // half


def small(name, kernel, out_shape, operands, in_hbm=(), scratch=()):
    specs = [ANY if i in in_hbm else VMEM for i in range(len(operands))]
    return pl.pallas_call(
        kernel,
        out_shape=out_shape,
        in_specs=specs,
        out_specs=jax.tree.map(lambda _: VMEM, out_shape),
        scratch_shapes=scratch,
        compiler_params=pltpu.CompilerParams(vmem_limit_bytes=16 << 20),
        cost_estimate=pl.CostEstimate(flops=1, bytes_accessed=1, transcendentals=0),
        name=name,
    )(*operands)


def prepare_kernel(queries, values, own, high, low, sem):
    copy = pltpu.make_async_copy(queries, own, sem)
    copy.start()
    whole = values[...]
    top = whole.astype(jnp.bfloat16)
    high[...] = top
    low[...] = (whole - top.astype(jnp.float32)).astype(jnp.bfloat16)
    copy.wait()


def prepare(queries, values):
    part = jax.ShapeDtypeStruct(values.shape, jnp.bfloat16)
    return small(
        "prepare",
        prepare_kernel,
        (jax.ShapeDtypeStruct(queries.shape, queries.dtype), part, part),
        (queries, values),
        in_hbm=(0,),
        scratch=[pltpu.SemaphoreType.DMA(())],
    )


def stack_kernel(*refs):
    *parts, result = refs
    for i, part in enumerate(parts):
        result[i] = part[...]


def stack(parts):
    shape = jax.ShapeDtypeStruct((len(parts), *parts[0].shape), parts[0].dtype)
    return small("stack", stack_kernel, shape, tuple(parts))


def precond_kernel(grad, high, low, result):
    row = jnp.concatenate([grad[k : k + 1] for k in range(grad.shape[0])], axis=1)
    left = jnp.concatenate(split(row, 3), axis=0)
    both = lax.dot_general(left, high[...], NT, preferred_element_type=jnp.float32)
    both += lax.dot_general(left, low[...], NT, preferred_element_type=jnp.float32)
    result[...] = both[0:1] + both[1:2] + both[2:3]


def precondition(grad, high, low):
    shape = jax.ShapeDtypeStruct((1, high.shape[0]), jnp.float32)
    return small("precondition", precond_kernel, shape, (grad, high, low))


def halves_kernel(mine, other, result):
    width = mine.shape[1]
    first = lax.axis_index("tp") == 0
    result[:, :width] = jnp.where(first, mine[...], other[...])
    result[:, width:] = jnp.where(first, other[...], mine[...])


def both_halves(mine, other):
    shape = jax.ShapeDtypeStruct((mine.shape[0], 2 * mine.shape[1]), mine.dtype)
    return small("both_halves", halves_kernel, shape, (mine, other))


def score_kernel(half, ways, last, *refs):
    rows, refs = ((), refs) if last else (refs[:2], refs[2:])
    mine, others, refs = refs[: len(ways)], refs[len(ways)], refs[len(ways) + 1 :]
    before, (near, far, *lefts) = (refs[:3], refs[3:]) if last else ((), refs)

    @pl.when(serves(half))
    def _():
        if last:
            near[...] = before[0][...]
            far[...] = before[1][...]
            left = before[2][...]
        else:
            values = jnp.concatenate([ref[...] for ref in rows], axis=0)
            left = jnp.concatenate(split(values, 3), axis=0)
            lefts[0][...] = left
        place = lax.axis_index("ex") % half
        second = lax.axis_index("tp") == 1
        feats = left.shape[1] // 2
        halves = [left[:, :feats], left[:, feats:]]
        halves = [jnp.where(second, halves[1 - i], halves[i]) for i in range(2)]
        for i, (first_way, second_way) in enumerate(ways):
            other = others[ways.index((second_way, first_way))] if len(others.shape) > 2 else others[...]
            sums = lax.dot_general(
                halves[0], mine[i][...], NT, preferred_element_type=jnp.float32
            ) + lax.dot_general(halves[1], other, NT, preferred_element_type=jnp.float32)
            total = sums[0:2] + sums[2:4] + sums[4:6]
            width = total.shape[1]
            start = (place ^ jnp.where(second, second_way, first_way)) * width
            at = pl.ds(pl.multiple_of(start, width), width)
            near[:, at] = total[0:1]
            far[:, at] = total[1:2]


def score(half, ways, rows, mine, others, before=()):
    row = jax.ShapeDtypeStruct((1, half * mine[0].shape[0]), jnp.float32)
    shapes = (row, row)
    if not before:
        shapes += (jax.ShapeDtypeStruct((3 * len(rows), rows[0].shape[1]), jnp.bfloat16),)
    return small(
        "score",
        functools.partial(score_kernel, half, tuple(ways), bool(before)),
        shapes,
        (*rows, *mine, others, *before),
    )


def finish_kernel(half, grad, near, returned, share, result):
    rows = grad.shape[0] // 2
    half_grad = jnp.where(lax.axis_index("tp") == 0, grad[:rows], grad[rows:])
    for k in range(rows):
        share[:, k * LANES : (k + 1) * LANES] = half_grad[k : k + 1]

    @pl.when(serves(half))
    def _():
        result[...] = near[...]

    @pl.when(jnp.logical_not(serves(half)))
    def _():
        result[...] = returned[...]


def finish(half, grad, near, returned):
    shapes = (
        jax.ShapeDtypeStruct((1, grad.size // 2), jnp.float32),
        jax.ShapeDtypeStruct(near.shape, near.dtype),
    )
    return small(
        "finish", functools.partial(finish_kernel, half), shapes, (grad, near, returned)
    )


def stage_kernel(values, result):
    result[...] = jnp.zeros_like(result)


def stage(values):
    return pl.pallas_call(
        stage_kernel,
        out_shape=jax.ShapeDtypeStruct((8, LANES), jnp.float32),
        in_specs=[ANY],
        out_specs=VMEM,
        compiler_params=pltpu.CompilerParams(vmem_limit_bytes=16 << 20),
        cost_estimate=pl.CostEstimate(flops=20_000_000_000, bytes_accessed=64 << 20, transcendentals=0),
        name="stage",
    )(values)


def shards(sizes, activations, out_grads, in_factor, out_factor, curvature_inv, queries):
    groups, ex = sizes
    half = ex // 2
    axes = ("groups", "ex", "tp")

    def send(values, target):
        number = lambda group, e, core: (group * ex + e) * 2 + core
        pairs = [
            (number(g, e, t), number(*target(g, e, t, t == e // half)))
            for g in range(groups)
            for e in range(ex)
            for t in range(2)
        ]
        return lax.ppermute(values, axes, pairs)

    def swap(values):
        return lax.ppermute(values, "tp", [(0, 1), (1, 0)])

    queries, token = lax.optimization_barrier((queries, stage(queries)))
    turn = {1: 2, 2: 1} if half > 3 else {}
    ways = [(turn.get(k, k), k) for k in range(1, half - 1)]
    early = [send(queries, lambda g, e, t, _: (g, e ^ way[t], t)) for way in ways]
    last = []
    if half > 1:
        far = half - 1
        aside = lambda g, e, t: ((g + 1) % groups, e, t) if groups > 1 else (g, e ^ far, t)
        last = [
            send(queries, lambda g, e, t, on: (g, e ^ far, t) if on else aside(g, e, t)),
            send(queries, lambda g, e, t, on: (g, e if on else e ^ far, 1 - t)),
        ]

    def whole(steps, *values):
        empty = lambda *_: jax.tree.map(lambda s: jnp.zeros(s.shape, s.dtype), shapes)
        shapes = jax.eval_shape(steps, *values)
        return lax.cond(lax.axis_index("ex") < ex, steps, empty, *values)

    def gradient(part, queries, values):
        own, high, low = prepare(queries, values)
        grad = outer(part, swap(part))
        half_precond = precondition(grad, high, low)
        return grad, both_halves(half_precond, swap(half_precond)), own

    def exchange(precond, *blocks):
        others = swap(stack(blocks))
        far = send(precond, lambda g, e, t, on: (g, e, 1 - t) if on else (g, e ^ half, t))
        return score(half, [(0, 0), *ways], (precond, far), blocks, others)

    part = project_in(project_out(token, out_grads[0], out_factor), activations[0].T, in_factor)
    grad, precond, own = gradient(part, queries, curvature_inv)
    precond, *blocks = lax.optimization_barrier((precond, own, *early))
    scores = whole(exchange, precond, *blocks)
    if last:
        way = half - 1
        scores = score(half, [(way, way)], (), last[:1], last[1], scores)
    near, far = scores[:2]
    returned = send(far, lambda g, e, t, on: (g, e ^ half, t) if on else (g, e, 1 - t))
    return finish(half, grad, near, returned)


def solution(mesh):
    placed = (
        P(("groups", "ex"), None, "tp"),
        P(("groups", "ex"), None, "tp"),
        P(None, "tp"),
        P(None, "tp"),
        P("tp", None),
        P(("groups", "ex"), "tp"),
    )
    return jax.shard_map(
        functools.partial(shards, (mesh.shape["groups"], mesh.shape["ex"])),
        mesh=mesh,
        in_specs=placed,
        out_specs=(P(("groups", "ex"), "tp"), P(("groups", "ex"), "tp")),
        check_vma=False,
    )
```

time: 89.5 us -> 21.4 us (0.24)
  waiting for transfers between devices: 52.9 us -> 3.37 us
  between operations: 15.6 us -> 0.76 us
  starting transfers between devices: 0.12 us -> 12.4 us
  matrix products: 12.2 us -> 0 us
  Pallas kernels: 0 us -> 4.61 us
  local copies, waits for them, and re-layouts: 3.96 us -> 0.14 us
  blocking collectives: 3.5 us -> 0 us
    all_gather x1 -> x0, waiting for transfers between devices: 34.1 us -> none  [shards(): lax.all_gather(queries, 'ex', axis=0, tiled=True)]
    ppermute x0 -> x9, starting transfers between devices: none -> 12.4 us  [the longest x6 11.7 us: send(): return lax.ppermute(values, axes, pairs)]
    dot_general x5 -> x0, matrix products: 12.2 us -> none  [the longest x1 4.98 us: shards(): jnp.dot(flat_inputs, in_factor.T, preferred_element_type=jnp.float32)]
    reduce_scatter x1 -> x0, waiting for transfers between devices: 9.41 us -> none  [shards(): lax.psum_scatter(jnp.concatenate([out_part, in_part], axis=1), 'tp', scat...]
    unnamed x4 -> x0, waiting for transfers between devices: 9.35 us -> none
    pallas_call x0 -> x11, Pallas kernels: none -> 4.61 us  [the longest x7 2.3 us: small(): pl.pallas_call(kernel, out_shape=out_shape, in_specs=specs, out_specs=jax...]
    psum x1 -> x0, blocking collectives: 3.5 us -> none  [shards(): summed_outer = lax.psum(partial_outer, 'tp')]
    ppermute x0 -> x9, waiting for transfers between devices: none -> 3.37 us  [the longest x6 2.27 us: send(): return lax.ppermute(values, axes, pairs)]
  transfers between devices with their start and end apart: 3 -> 9, of which waited for: 3 -> 4; matrix products, arithmetic and copies ran while one was open for 6% -> 0% of each run, Pallas kernels for 0% -> 19%
where the time goes in v3:
time: 21.4 us; the launch traced here: 21.3 us
  starting transfers between devices  12.4 us (58%)
  Pallas kernels  4.61 us (22%)
  waiting for transfers between devices  3.37 us (16%)
  between operations  0.76 us (4%)
    ppermute x6, starting transfers between devices, send(): return lax.ppermute(values, axes, pairs)  11.7 us
    pallas_call x7, Pallas kernels, small(): pl.pallas_call(kernel, out_shape=out_shape, in_specs=specs, out_specs=jax...  2.3 us
    ppermute x6, waiting for transfers between devices, send(): return lax.ppermute(values, axes, pairs)  2.27 us
    pallas_call x1, Pallas kernels, project_in(): pl.pallas_call(in_kernel, out_shape=jax.ShapeDtypeStruct((2 * rank, token...  1.39 us
    ppermute x3, waiting for transfers between devices, swap(): return lax.ppermute(values, 'tp', [(0, 1), (1, 0)])  1.1 us
    pallas_call x1, Pallas kernels, project_out(): pl.pallas_call(out_kernel, out_shape=jax.ShapeDtypeStruct((out_factor.sha...  0.71 us
    ppermute x3, starting transfers between devices, swap(): return lax.ppermute(values, 'tp', [(0, 1), (1, 0)])  0.62 us
  transfers between devices with their start and end apart: 9, of which 4 were waited for; matrix products, arithmetic and copies ran while one was open for 0% of the time, Pallas kernels for 19%

profile of v3, /device:TPU:1, one launch (start us, length us, event | category | flops | bytes accessed | tf_op | source)
XLA Modules:
  0.0 21.3 jit_solution(14501532205601452724)
XLA Ops:
  0.6 0.0 copy-start.1
  0.6 0.0 copy-start.4
  0.6 0.0 copy-start
  0.7 0.0 copy-start.3
  0.7 2.1 %collective-permute-start.6 = (bf16[256,512]{1,0:T(8,128)(2,1)}, bf16[256,512]{1,0:T(8,128)(2,1)S(1)}, u32[]{:S(2)}, u32[]{:S(2)}) collective-permute-start(bf16[256,512]{1,0:T(8,128)(2,1)} %queries), channel_id=1, source_target_pairs={{0,4},{1,3},{2,6},{3,1},{4,0},{5,7},{6,2},{7,5},{8,12},{9,11},{10,... | collective-permute-start | bytes 786440 | tf_op jit(solution)/shard_map/ppermute | solution.py:293
  2.8 1.3 %collective-permute-start.7 = (bf16[256,512]{1,0:T(8,128)(2,1)}, bf16[256,512]{1,0:T(8,128)(2,1)S(1)}, u32[]{:S(2)}, u32[]{:S(2)}) collective-permute-start(bf16[256,512]{1,0:T(8,128)(2,1)} %queries), channel_id=1, source_target_pairs={{0,2},{1,5},{2,0},{3,7},{4,6},{5,1},{6,4},{7,3},{8,10},{9,13},{10,... | collective-permute-start | bytes 786440 | tf_op jit(solution)/shard_map/ppermute | solution.py:293
  4.1 1.2 %collective-permute-start.3 = (bf16[256,512]{1,0:T(8,128)(2,1)}, bf16[256,512]{1,0:T(8,128)(2,1)S(1)}, u32[]{:S(2)}, u32[]{:S(2)}) collective-permute-start(bf16[256,512]{1,0:T(8,128)(2,1)} %queries), channel_id=1, source_target_pairs={{0,6},{1,17},{2,4},{3,19},{4,2},{5,21},{6,0},{7,23},{8,24},{9,15},... | collective-permute-start | bytes 786440 | tf_op jit(solution)/shard_map/ppermute | solution.py:293
  5.3 2.6 %collective-permute-start.4 = (bf16[256,512]{1,0:T(8,128)(2,1)}, bf16[256,512]{1,0:T(8,128)(2,1)S(1)}, u32[]{:S(2)}, u32[]{:S(2)}) collective-permute-start(bf16[256,512]{1,0:T(8,128)(2,1)} %queries), channel_id=1, source_target_pairs={{0,1},{1,6},{2,3},{3,4},{4,5},{5,2},{6,7},{7,0},{8,15},{9,8},{10,1... | collective-permute-start | bytes 786440 | tf_op jit(solution)/shard_map/ppermute | solution.py:293
  7.9 0.0 copy-done.1
  7.9 0.0 copy-done.4
  7.9 0.7 %project_out.1.out_part = f32[32,256]{1,0:T(8,128)S(1)} custom-call(f32[8,128]{1,0:T(8,128)S(1)} %stage.1.token, bf16[256,4096]{1,0:T(8,128)(2,1)S(1)} %bitcast.5, bf16[32,4096]{1,0:T(8,128)(2,1)S(1)} %copy-done.4), custom_call_target="tpu_custom_call" | custom-call | flops 67108864 | bytes 2359296 | tf_op jit(solution)/shard_map/project_out/pallas_call | solution.py:41
  8.6 0.0 copy-done
  8.6 0.0 copy-done.3
  8.6 0.0 copy-start.2
  8.6 1.4 %project_in.1.mine = f32[64,256]{1,0:T(8,128)S(1)} custom-call(f32[32,256]{1,0:T(8,128)S(1)} %project_out.1.out_part, bf16[14784,256]{1,0:T(8,128)(2,1)S(1)} %bitcast.4, bf16[32,14784]{1,0:T(8,128)(2,1)S(1)} %copy-done.3), custom_call_target="tpu_custom_call" | custom-call | flops 242221056 | bytes 8515584 | tf_op jit(solution)/shard_map/project_in/pallas_call | solution.py:58
  10.0 0.1 collective-permute-start.2
  10.1 0.1 copy-done.2
  10.2 1.0 %prepare.1 = (bf16[256,512]{1,0:T(8,128)(2,1)S(1)}, bf16[512,1024]{1,0:T(8,128)(2,1)S(1)}, bf16[512,1024]{1,0:T(8,128)(2,1)S(1)}) custom-call(bf16[256,512]{1,0:T(8,128)(2,1)} %queries, f32[512,1024]{1,0:T(8,128)S(1)} %copy-done.2), custom_call_target="tpu_custom_call" | custom-call | flops 1 | bytes 1 | tf_op jit(solution)/shard_map/prepare/pallas_call | solution.py:123
  11.2 0.2 collective-permute-done.2.other
  11.4 0.2 outer.1.grad
  11.6 0.7 %precondition.1.mine = f32[1,512]{1,0:T(1,128)S(1)} custom-call(f32[8,128]{1,0:T(8,128)S(1)} %outer.1.grad, bf16[512,1024]{1,0:T(8,128)(2,1)S(1)} %get-tuple-element.26.high, bf16[512,1024]{1,0:T(8,128)(2,1)S(1)} %get-tuple-element.27.low), custom_call_target="tpu_custom_call" | custom-call | flops 1 | bytes 1 | tf_op jit(solution)/shard_map/precondition/pallas_call | solution.py:123
  12.2 0.3 %collective-permute-start.5 = (f32[1,512]{1,0:T(1,128)S(1)}, f32[1,512]{1,0:T(1,128)S(1)}, u32[]{:S(2)}, u32[]{:S(2)}) collective-permute-start(f32[1,512]{1,0:T(1,128)S(1)} %precondition.1.mine), channel_id=1, source_target_pairs={{0,1},{1,0},{2,3},{3,2},{4,5},{5,4},{6,7},{7,6},{8,9},{9,8},{10,11... | collective-permute-start | bytes 6152 | tf_op jit(solution)/shard_map/ppermute | solution.py:296
  12.5 0.9 %collective-permute-done.5.other = f32[1,512]{1,0:T(1,128)S(1)} collective-permute-done((f32[1,512]{1,0:T(1,128)S(1)}, f32[1,512]{1,0:T(1,128)S(1)}, u32[]{:S(2)}, u32[]{:S(2)}) %collective-permute-start.5) | collective-permute-done | bytes 2080 | tf_op jit(solution)/shard_map/ppermute | solution.py:296
  13.4 0.0 collective-permute-done.6
  13.4 0.0 collective-permute-done.7
  13.4 2.7 %conditional.1 = ((f32[1,1024]{1,0:T(1,128)S(1)}, f32[1,1024]{1,0:T(1,128)S(1)}, bf16[6,1024]{1,0:T(8,128)(2,1)S(1)})) conditional(s32[]{:T(128)} %convert_element_type.3, () %tuple.16, (f32[1,1024]{1,0:T(1,128)S(1)}, bf16[256,512]{1,0:T(8,128)(2,1)S(1)}, bf16[256,512]{1,0:T(8,128)(2,1)S(1)}, bf16[256,512]{1,0:T(8,128)(2,1)S(1)}) %tuple.17), branch_computations={%region_0.0_spmd, %region_1.0_spmd} | conditional | flops 2 | bytes 3162202 | solution.py:314
  13.4 0.1 stack.1
  13.5 0.3 %collective-permute-start.1 = (bf16[3,256,512]{2,1,0:T(8,128)(2,1)S(1)}, bf16[3,256,512]{2,1,0:T(8,128)(2,1)S(1)}, u32[]{:S(2)}, u32[]{:S(2)}) collective-permute-start(bf16[3,256,512]{2,1,0:T(8,128)(2,1)S(1)} %stack.1), channel_id=1, source_target_pairs={{0,1},{1,0},{2,3},{3,2},{4,5},{5,4},{6,7},{7,6},{8,9},{9,8},{10,11... | collective-permute-start | bytes 2359304 | tf_op jit(solution)/shard_map/cond/branch_1_fun/ppermute | solution.py:296
  13.8 1.3 %collective-permute-start = (f32[1,1024]{1,0:T(1,128)S(1)}, f32[1,1024]{1,0:T(1,128)S(1)}, u32[]{:S(2)}, u32[]{:S(2)}) collective-permute-start(f32[1,1024]{1,0:T(1,128)S(1)} %get-tuple-element.8.refs_0_), channel_id=1, source_target_pairs={{0,1},{1,9},{2,3},{3,11},{4,5},{5,13},{6,7},{7,15},{8,0},{9,8},{10... | collective-permute-start | bytes 12296 | tf_op jit(solution)/shard_map/cond/branch_1_fun/ppermute | solution.py:293
  15.1 1.0 %collective-permute-done.refs_1_ = f32[1,1024]{1,0:T(1,128)S(1)} collective-permute-done((f32[1,1024]{1,0:T(1,128)S(1)}, f32[1,1024]{1,0:T(1,128)S(1)}, u32[]{:S(2)}, u32[]{:S(2)}) %collective-permute-start) | collective-permute-done | bytes 4128 | tf_op jit(solution)/shard_map/cond/branch_1_fun/ppermute | solution.py:293
  16.1 0.0 collective-permute-done.1.refs_5_
  16.1 0.0 collective-permute-done.3.refs_0_
  16.1 0.0 collective-permute-done.4.refs_1_
  16.1 3.3 %collective-permute-start.8 = (f32[1,1024]{1,0:T(1,128)S(1)}, f32[1,1024]{1,0:T(1,128)S(1)}, u32[]{:S(2)}, u32[]{:S(2)}) collective-permute-start(f32[1,1024]{1,0:T(1,128)S(1)} %get-tuple-element.33), channel_id=1, source_target_pairs={{0,8},{1,0},{2,10},{3,2},{4,12},{5,4},{6,14},{7,6},{8,9},{9,1},{10... | collective-permute-start | bytes 12296 | tf_op jit(solution)/shard_map/ppermute | solution.py:293
  19.4 1.2 %collective-permute-done.8.returned = f32[1,1024]{1,0:T(1,128)S(1)} collective-permute-done((f32[1,1024]{1,0:T(1,128)S(1)}, f32[1,1024]{1,0:T(1,128)S(1)}, u32[]{:S(2)}, u32[]{:S(2)}) %collective-permute-start.8) | collective-permute-done | bytes 4128 | tf_op jit(solution)/shard_map/ppermute | solution.py:293
  20.6 0.6 %finish.1 = (f32[1,512]{1,0:T(1,128)}, f32[1,1024]{1,0:T(1,128)}) custom-call(f32[8,128]{1,0:T(8,128)S(1)} %outer.1.grad, f32[1,1024]{1,0:T(1,128)S(1)} %get-tuple-element.32.near, f32[1,1024]{1,0:T(1,128)S(1)} %collective-permute-done.8.returned), custom_call_target="tpu_custom_call" | custom-call | flops 1 | bytes 1 | tf_op jit(solution)/shard_map/finish/pallas_call | solution.py:123
  (4 shorter events, 0.0 us)
Async XLA Ops:
  0.6 7.3 %copy-start.1 = (bf16[1,256,4096]{2,1,0:T(8,128)(2,1)S(1)}, bf16[1,256,4096]{2,1,0:T(8,128)(2,1)}, u32[]{:S(2)}) copy-start(bf16[1,256,4096]{2,1,0:T(8,128)(2,1)} %param.9) | copy-start | bytes 6291460
  0.6 7.2 %copy-start.4 = (bf16[32,4096]{1,0:T(8,128)(2,1)S(1)}, bf16[32,4096]{1,0:T(8,128)(2,1)}, u32[]{:S(2)}) copy-start(bf16[32,4096]{1,0:T(8,128)(2,1)} %out_f.1) | copy-start | bytes 786436
  0.6 8.0 %copy-start = (bf16[1,256,14784]{1,2,0:T(8,128)(2,1)S(1)}, bf16[1,256,14784]{1,2,0:T(8,128)(2,1)}, u32[]{:S(2)}) copy-start(bf16[1,256,14784]{1,2,0:T(8,128)(2,1)} %param.8) | copy-start | bytes 22708228
  0.7 8.0 %copy-start.3 = (bf16[32,14784]{1,0:T(8,128)(2,1)S(1)}, bf16[32,14784]{1,0:T(8,128)(2,1)}, u32[]{:S(2)}) copy-start(bf16[32,14784]{1,0:T(8,128)(2,1)} %in_f.1) | copy-start | bytes 2838532
  0.7 12.7 %collective-permute-start.6 = (bf16[256,512]{1,0:T(8,128)(2,1)}, bf16[256,512]{1,0:T(8,128)(2,1)S(1)}, u32[]{:S(2)}, u32[]{:S(2)}) collective-permute-start(bf16[256,512]{1,0:T(8,128)(2,1)} %queries), channel_id=1, source_target_pairs={{0,4},{1,3},{2,6},{3,1},{4,0},{5,7},{6,2},{7,5},{8,12},{9,11},{10,... | collective-permute-start | bytes 786440 | tf_op jit(solution)/shard_map/ppermute | solution.py:293
  2.8 10.6 %collective-permute-start.7 = (bf16[256,512]{1,0:T(8,128)(2,1)}, bf16[256,512]{1,0:T(8,128)(2,1)S(1)}, u32[]{:S(2)}, u32[]{:S(2)}) collective-permute-start(bf16[256,512]{1,0:T(8,128)(2,1)} %queries), channel_id=1, source_target_pairs={{0,2},{1,5},{2,0},{3,7},{4,6},{5,1},{6,4},{7,3},{8,10},{9,13},{10,... | collective-permute-start | bytes 786440 | tf_op jit(solution)/shard_map/ppermute | solution.py:293
  4.1 12.0 %collective-permute-start.3 = (bf16[256,512]{1,0:T(8,128)(2,1)}, bf16[256,512]{1,0:T(8,128)(2,1)S(1)}, u32[]{:S(2)}, u32[]{:S(2)}) collective-permute-start(bf16[256,512]{1,0:T(8,128)(2,1)} %queries), channel_id=1, source_target_pairs={{0,6},{1,17},{2,4},{3,19},{4,2},{5,21},{6,0},{7,23},{8,24},{9,15},... | collective-permute-start | bytes 786440 | tf_op jit(solution)/shard_map/ppermute | solution.py:293
  5.3 10.8 %collective-permute-start.4 = (bf16[256,512]{1,0:T(8,128)(2,1)}, bf16[256,512]{1,0:T(8,128)(2,1)S(1)}, u32[]{:S(2)}, u32[]{:S(2)}) collective-permute-start(bf16[256,512]{1,0:T(8,128)(2,1)} %queries), channel_id=1, source_target_pairs={{0,1},{1,6},{2,3},{3,4},{4,5},{5,2},{6,7},{7,0},{8,15},{9,8},{10,1... | collective-permute-start | bytes 786440 | tf_op jit(solution)/shard_map/ppermute | solution.py:293
  8.6 1.6 %copy-start.2 = (f32[512,1024]{1,0:T(8,128)S(1)}, f32[512,1024]{1,0:T(8,128)}, u32[]{:S(2)}) copy-start(f32[512,1024]{1,0:T(8,128)} %values.3) | copy-start | bytes 6291460
  10.0 1.3 %collective-permute-start.2 = (f32[64,256]{1,0:T(8,128)S(1)}, f32[64,256]{1,0:T(8,128)S(1)}, u32[]{:S(2)}, u32[]{:S(2)}) collective-permute-start(f32[64,256]{1,0:T(8,128)S(1)} %project_in.1.mine), channel_id=1, source_target_pairs={{0,1},{1,0},{2,3},{3,2},{4,5},{5,4},{6,7},{7,6},{8,9},{9,8},{10,11... | collective-permute-start | bytes 196616 | tf_op jit(solution)/shard_map/ppermute | solution.py:296
  12.2 1.2 %collective-permute-start.5 = (f32[1,512]{1,0:T(1,128)S(1)}, f32[1,512]{1,0:T(1,128)S(1)}, u32[]{:S(2)}, u32[]{:S(2)}) collective-permute-start(f32[1,512]{1,0:T(1,128)S(1)} %precondition.1.mine), channel_id=1, source_target_pairs={{0,1},{1,0},{2,3},{3,2},{4,5},{5,4},{6,7},{7,6},{8,9},{9,8},{10,11... | collective-permute-start | bytes 6152 | tf_op jit(solution)/shard_map/ppermute | solution.py:296
  13.5 2.6 %collective-permute-start.1 = (bf16[3,256,512]{2,1,0:T(8,128)(2,1)S(1)}, bf16[3,256,512]{2,1,0:T(8,128)(2,1)S(1)}, u32[]{:S(2)}, u32[]{:S(2)}) collective-permute-start(bf16[3,256,512]{2,1,0:T(8,128)(2,1)S(1)} %stack.1), channel_id=1, source_target_pairs={{0,1},{1,0},{2,3},{3,2},{4,5},{5,4},{6,7},{7,6},{8,9},{9,8},{10,11... | collective-permute-start | bytes 2359304 | tf_op jit(solution)/shard_map/cond/branch_1_fun/ppermute | solution.py:296
  13.8 2.3 %collective-permute-start = (f32[1,1024]{1,0:T(1,128)S(1)}, f32[1,1024]{1,0:T(1,128)S(1)}, u32[]{:S(2)}, u32[]{:S(2)}) collective-permute-start(f32[1,1024]{1,0:T(1,128)S(1)} %get-tuple-element.8.refs_0_), channel_id=1, source_target_pairs={{0,1},{1,9},{2,3},{3,11},{4,5},{5,13},{6,7},{7,15},{8,0},{9,8},{10... | collective-permute-start | bytes 12296 | tf_op jit(solution)/shard_map/cond/branch_1_fun/ppermute | solution.py:293
  16.1 4.5 %collective-permute-start.8 = (f32[1,1024]{1,0:T(1,128)S(1)}, f32[1,1024]{1,0:T(1,128)S(1)}, u32[]{:S(2)}, u32[]{:S(2)}) collective-permute-start(f32[1,1024]{1,0:T(1,128)S(1)} %get-tuple-element.33), channel_id=1, source_target_pairs={{0,8},{1,0},{2,10},{3,2},{4,12},{5,4},{6,14},{7,6},{8,9},{9,1},{10... | collective-permute-start | bytes 12296 | tf_op jit(solution)/shard_map/ppermute | solution.py:293

commit v4 on v3

--- a/solution.py
+++ b/solution.py
@@ -31,10 +31,13 @@
     result[...] = lax.dot_general(out_f[...], grads[...], NT, preferred_element_type=jnp.float32)
 
 
-def in_kernel(out_part, acts, in_f, result):
+def in_kernel(out_part, acts, in_f, queries, result, own, sem):
+    copy = pltpu.make_async_copy(queries, own, sem)
+    copy.start()
     rank = in_f.shape[0]
     result[:rank] = out_part[...]
     result[rank:] = jnp.dot(in_f[...], acts[...], preferred_element_type=jnp.float32)
+    copy.wait()
 
 
 def project_out(token, grads, out_factor):
@@ -53,13 +56,17 @@
     )(token, grads, out_factor)
 
 
-def project_in(out_part, acts, in_factor):
+def project_in(out_part, acts, in_factor, queries):
     rank, tokens = out_part.shape
     return pl.pallas_call(
         in_kernel,
-        out_shape=jax.ShapeDtypeStruct((2 * rank, tokens), jnp.float32),
-        in_specs=[VMEM, VMEM, VMEM],
-        out_specs=VMEM,
+        out_shape=(
+            jax.ShapeDtypeStruct((2 * rank, tokens), jnp.float32),
+            jax.ShapeDtypeStruct(queries.shape, queries.dtype),
+        ),
+        in_specs=[VMEM, VMEM, VMEM, ANY],
+        out_specs=(VMEM, VMEM),
+        scratch_shapes=[pltpu.SemaphoreType.DMA(())],
         compiler_params=pltpu.CompilerParams(vmem_limit_bytes=32 << 20),
         cost_estimate=pl.CostEstimate(
             flops=2 * in_factor.size * tokens,
@@ -67,7 +74,7 @@
             transcendentals=0,
         ),
         name="project_in",
-    )(out_part, acts, in_factor)
+    )(out_part, acts, in_factor, queries)
 
 
 def outer_kernel(mine, other, grad, lanes):
@@ -114,6 +121,10 @@
     )(mine, other)
 
 
+def odd(place):
+    return (place ^ (place // 2)) % 2
+
+
 def serves(half):
     return lax.axis_index("tp") == lax.axis_index("ex") // half
 
@@ -132,26 +143,16 @@
     )(*operands)
 
 
-def prepare_kernel(queries, values, own, high, low, sem):
-    copy = pltpu.make_async_copy(queries, own, sem)
-    copy.start()
+def prepare_kernel(values, high, low):
     whole = values[...]
     top = whole.astype(jnp.bfloat16)
     high[...] = top
     low[...] = (whole - top.astype(jnp.float32)).astype(jnp.bfloat16)
-    copy.wait()
-
-
-def prepare(queries, values):
+
+
+def prepare(values):
     part = jax.ShapeDtypeStruct(values.shape, jnp.bfloat16)
-    return small(
-        "prepare",
-        prepare_kernel,
-        (jax.ShapeDtypeStruct(queries.shape, queries.dtype), part, part),
-        (queries, values),
-        in_hbm=(0,),
-        scratch=[pltpu.SemaphoreType.DMA(())],
-    )
+    return small("prepare", prepare_kernel, (part, part), (values,))
 
 
 def stack_kernel(*refs):
@@ -217,7 +218,8 @@
             ) + lax.dot_general(halves[1], other, NT, preferred_element_type=jnp.float32)
             total = sums[0:2] + sums[2:4] + sums[4:6]
             width = total.shape[1]
-            start = (place ^ jnp.where(second, second_way, first_way)) * width
+            swapped = second != (odd(place) == 1)
+            start = (place ^ jnp.where(swapped, second_way, first_way)) * width
             at = pl.ds(pl.multiple_of(start, width), width)
             near[:, at] = total[0:1]
             far[:, at] = total[1:2]
@@ -298,11 +300,13 @@
     queries, token = lax.optimization_barrier((queries, stage(queries)))
     turn = {1: 2, 2: 1} if half > 3 else {}
     ways = [(turn.get(k, k), k) for k in range(1, half - 1)]
-    early = [send(queries, lambda g, e, t, _: (g, e ^ way[t], t)) for way in ways]
+    early = [
+        send(queries, lambda g, e, t, _: (g, e ^ way[1 - (t ^ odd(e))], t)) for way in ways
+    ]
     last = []
-    if half > 1:
-        far = half - 1
-        aside = lambda g, e, t: ((g + 1) % groups, e, t) if groups > 1 else (g, e ^ far, t)
+    far = half - 1
+    aside = lambda g, e, t: ((g + 1) % groups, e, t) if groups > 1 else (g, e ^ max(far, 1), t)
+    if far:
         last = [
             send(queries, lambda g, e, t, on: (g, e ^ far, t) if on else aside(g, e, t)),
             send(queries, lambda g, e, t, on: (g, e if on else e ^ far, 1 - t)),
@@ -313,19 +317,25 @@
         shapes = jax.eval_shape(steps, *values)
         return lax.cond(lax.axis_index("ex") < ex, steps, empty, *values)
 
-    def gradient(part, queries, values):
-        own, high, low = prepare(queries, values)
+    def gradient(part, high, low):
         grad = outer(part, swap(part))
         half_precond = precondition(grad, high, low)
-        return grad, both_halves(half_precond, swap(half_precond)), own
+        return grad, both_halves(half_precond, swap(half_precond))
+
+    def forward(g, e, t, on):
+        if e < half:
+            return (g, e, 1 - t) if on else (g, e ^ half, t)
+        return (g, e, 1 - t) if on else (g, e ^ half, t)
 
     def exchange(precond, *blocks):
         others = swap(stack(blocks))
-        far = send(precond, lambda g, e, t, on: (g, e, 1 - t) if on else (g, e ^ half, t))
+        far = send(precond, forward)
         return score(half, [(0, 0), *ways], (precond, far), blocks, others)
 
-    part = project_in(project_out(token, out_grads[0], out_factor), activations[0].T, in_factor)
-    grad, precond, own = gradient(part, queries, curvature_inv)
+    out_part = project_out(token, out_grads[0], out_factor)
+    part, own = project_in(out_part, activations[0].T, in_factor, queries)
+    high, low = prepare(curvature_inv)
+    grad, precond = gradient(part, high, low)
     precond, *blocks = lax.optimization_barrier((precond, own, *early))
     scores = whole(exchange, precond, *blocks)
     if last:

time: 21.4 us -> 20.8 us (0.972)
  waiting for transfers between devices: 3.37 us -> 4.12 us
  starting transfers between devices: 12.4 us -> 11.7 us
  Pallas kernels: 4.61 us -> 3.96 us
    ppermute x6, starting transfers between devices: 11.7 us -> 10.5 us  [send(): return lax.ppermute(values, axes, pairs)]
    pallas_call x7, Pallas kernels: 2.3 us -> 1.64 us  [small(): pl.pallas_call(kernel, out_shape=out_shape, in_specs=specs, out_specs=jax...]
    ppermute x3, starting transfers between devices: 0.62 us -> 1.21 us  [swap(): return lax.ppermute(values, 'tp', [(0, 1), (1, 0)])]
    ppermute x6, waiting for transfers between devices: 2.27 us -> 2.7 us  [send(): return lax.ppermute(values, axes, pairs)]
    ppermute x3, waiting for transfers between devices: 1.1 us -> 1.43 us  [swap(): return lax.ppermute(values, 'tp', [(0, 1), (1, 0)])]
  transfers between devices with their start and end apart: 9 -> 9, of which waited for: 4 -> 4; matrix products, arithmetic and copies ran while one was open for 0% -> 0% of each run, Pallas kernels for 19% -> 16%
where the time goes in v4:
time: 20.8 us; the launch traced here: 20.6 us
  starting transfers between devices  11.7 us (56%)
  waiting for transfers between devices  4.12 us (20%)
  Pallas kernels  3.96 us (19%)
  between operations  0.74 us (4%)
    ppermute x6, starting transfers between devices, send(): return lax.ppermute(values, axes, pairs)  10.5 us
    ppermute x6, waiting for transfers between devices, send(): return lax.ppermute(values, axes, pairs)  2.7 us
    pallas_call x7, Pallas kernels, small(): pl.pallas_call(kernel, out_shape=out_shape, in_specs=specs, out_specs=jax...  1.64 us
    ppermute x3, waiting for transfers between devices, swap(): return lax.ppermute(values, 'tp', [(0, 1), (1, 0)])  1.43 us
    pallas_call x1, Pallas kernels, project_in(): pl.pallas_call(in_kernel, out_shape=(jax.ShapeDtypeStruct((2 * rank, toke...  1.41 us
    ppermute x3, starting transfers between devices, swap(): return lax.ppermute(values, 'tp', [(0, 1), (1, 0)])  1.21 us
    pallas_call x1, Pallas kernels, project_out(): pl.pallas_call(out_kernel, out_shape=jax.ShapeDtypeStruct((out_factor.sha...  0.7 us
  transfers between devices with their start and end apart: 9, of which 4 were waited for; matrix products, arithmetic and copies ran while one was open for 0% of the time, Pallas kernels for 16%

profile of v4, /device:TPU:1, one launch (start us, length us, event | category | flops | bytes accessed | tf_op | source)
XLA Modules:
  0.0 20.6 jit_solution(14115410618065050272)
XLA Ops:
  0.6 0.0 copy-start.1
  0.6 0.0 copy-start.4
  0.6 0.0 copy-start
  0.7 0.0 copy-start.3
  0.7 2.2 %collective-permute-start.6 = (bf16[256,512]{1,0:T(8,128)(2,1)}, bf16[256,512]{1,0:T(8,128)(2,1)S(1)}, u32[]{:S(2)}, u32[]{:S(2)}) collective-permute-start(bf16[256,512]{1,0:T(8,128)(2,1)} %queries), channel_id=1, source_target_pairs={{0,2},{1,5},{2,6},{3,1},{4,0},{5,7},{6,4},{7,3},{8,10},{9,13},{10,... | collective-permute-start | bytes 786440 | tf_op jit(solution)/shard_map/ppermute | solution.py:295
  2.9 0.0 collective-permute-start.7
  2.9 1.4 %collective-permute-start.3 = (bf16[256,512]{1,0:T(8,128)(2,1)}, bf16[256,512]{1,0:T(8,128)(2,1)S(1)}, u32[]{:S(2)}, u32[]{:S(2)}) collective-permute-start(bf16[256,512]{1,0:T(8,128)(2,1)} %queries), channel_id=1, source_target_pairs={{0,6},{1,17},{2,4},{3,19},{4,2},{5,21},{6,0},{7,23},{8,24},{9,15},... | collective-permute-start | bytes 786440 | tf_op jit(solution)/shard_map/ppermute | solution.py:295
  4.2 2.2 %collective-permute-start.4 = (bf16[256,512]{1,0:T(8,128)(2,1)}, bf16[256,512]{1,0:T(8,128)(2,1)S(1)}, u32[]{:S(2)}, u32[]{:S(2)}) collective-permute-start(bf16[256,512]{1,0:T(8,128)(2,1)} %queries), channel_id=1, source_target_pairs={{0,1},{1,6},{2,3},{3,4},{4,5},{5,2},{6,7},{7,0},{8,15},{9,8},{10,1... | collective-permute-start | bytes 786440 | tf_op jit(solution)/shard_map/ppermute | solution.py:295
  6.4 0.0 copy-done.1
  6.4 0.0 copy-done.4
  6.4 0.7 %project_out.1.out_part = f32[32,256]{1,0:T(8,128)S(1)} custom-call(f32[8,128]{1,0:T(8,128)S(1)} %stage.1.token, bf16[256,4096]{1,0:T(8,128)(2,1)S(1)} %bitcast.5, bf16[32,4096]{1,0:T(8,128)(2,1)S(1)} %copy-done.4), custom_call_target="tpu_custom_call" | custom-call | flops 67108864 | bytes 2359296 | tf_op jit(solution)/shard_map/project_out/pallas_call | solution.py:44
  7.1 0.0 copy-done
  7.2 0.0 copy-done.3
  7.2 0.0 copy-start.2
  7.2 1.4 %project_in.1 = (f32[64,256]{1,0:T(8,128)S(1)}, bf16[256,512]{1,0:T(8,128)(2,1)S(1)}) custom-call(f32[32,256]{1,0:T(8,128)S(1)} %project_out.1.out_part, bf16[14784,256]{1,0:T(8,128)(2,1)S(1)} %bitcast.4, bf16[32,14784]{1,0:T(8,128)(2,1)S(1)} %copy-done.3, bf16[256,512]{1,0:T(8,128)(2,1)} %queries), custom_call_target="tpu_custom_call" | custom-call | flops 242221056 | bytes 8515584 | tf_op jit(solution)/shard_map/project_in/pallas_call | solution.py:61
  8.6 0.4 %collective-permute-start.2 = (f32[64,256]{1,0:T(8,128)S(1)}, f32[64,256]{1,0:T(8,128)S(1)}, u32[]{:S(2)}, u32[]{:S(2)}) collective-permute-start(f32[64,256]{1,0:T(8,128)S(1)} %get-tuple-element.27.mine), channel_id=1, source_target_pairs={{0,1},{1,0},{2,3},{3,2},{4,5},{5,4},{6,7},{7,6},{8,9},{9,8},{10,11... | collective-permute-start | bytes 196616 | tf_op jit(solution)/shard_map/ppermute | solution.py:298
  9.1 0.0 copy-done.2
  9.1 0.3 %prepare.1 = (bf16[512,1024]{1,0:T(8,128)(2,1)S(1)}, bf16[512,1024]{1,0:T(8,128)(2,1)S(1)}) custom-call(f32[512,1024]{1,0:T(8,128)S(1)} %copy-done.2), custom_call_target="tpu_custom_call" | custom-call | flops 1 | bytes 1 | tf_op jit(solution)/shard_map/prepare/pallas_call | solution.py:134
  9.4 0.6 %collective-permute-done.2.other = f32[64,256]{1,0:T(8,128)S(1)} collective-permute-done((f32[64,256]{1,0:T(8,128)S(1)}, f32[64,256]{1,0:T(8,128)S(1)}, u32[]{:S(2)}, u32[]{:S(2)}) %collective-permute-start.2) | collective-permute-done | bytes 65568 | tf_op jit(solution)/shard_map/ppermute | solution.py:298
  10.0 0.2 %outer.1.grad = f32[8,128]{1,0:T(8,128)S(1)} custom-call(f32[64,256]{1,0:T(8,128)S(1)} %get-tuple-element.27.mine, f32[64,256]{1,0:T(8,128)S(1)} %collective-permute-done.2.other), custom_call_target="tpu_custom_call" | custom-call | tf_op jit(solution)/shard_map/outer/pallas_call | solution.py:113
  10.2 0.7 %precondition.1.mine = f32[1,512]{1,0:T(1,128)S(1)} custom-call(f32[8,128]{1,0:T(8,128)S(1)} %outer.1.grad, bf16[512,1024]{1,0:T(8,128)(2,1)S(1)} %get-tuple-element.28.high, bf16[512,1024]{1,0:T(8,128)(2,1)S(1)} %get-tuple-element.29.low), custom_call_target="tpu_custom_call" | custom-call | flops 1 | bytes 1 | tf_op jit(solution)/shard_map/precondition/pallas_call | solution.py:134
  10.8 0.4 %collective-permute-start.5 = (f32[1,512]{1,0:T(1,128)S(1)}, f32[1,512]{1,0:T(1,128)S(1)}, u32[]{:S(2)}, u32[]{:S(2)}) collective-permute-start(f32[1,512]{1,0:T(1,128)S(1)} %precondition.1.mine), channel_id=1, source_target_pairs={{0,1},{1,0},{2,3},{3,2},{4,5},{5,4},{6,7},{7,6},{8,9},{9,8},{10,11... | collective-permute-start | bytes 6152 | tf_op jit(solution)/shard_map/ppermute | solution.py:298
  11.2 0.8 %collective-permute-done.5.other = f32[1,512]{1,0:T(1,128)S(1)} collective-permute-done((f32[1,512]{1,0:T(1,128)S(1)}, f32[1,512]{1,0:T(1,128)S(1)}, u32[]{:S(2)}, u32[]{:S(2)}) %collective-permute-start.5) | collective-permute-done | bytes 2080 | tf_op jit(solution)/shard_map/ppermute | solution.py:298
  12.0 0.0 collective-permute-done.6
  12.0 0.0 collective-permute-done.7
  12.0 3.5 %conditional.1 = ((f32[1,1024]{1,0:T(1,128)S(1)}, f32[1,1024]{1,0:T(1,128)S(1)}, bf16[6,1024]{1,0:T(8,128)(2,1)S(1)})) conditional(s32[]{:T(128)} %convert_element_type.3, () %tuple.16, (f32[1,1024]{1,0:T(1,128)S(1)}, bf16[256,512]{1,0:T(8,128)(2,1)S(1)}, bf16[256,512]{1,0:T(8,128)(2,1)S(1)}, bf16[256,512]{1,0:T(8,128)(2,1)S(1)}) %tuple.17), branch_computations={%region_0.0_spmd, %region_1.0_spmd} | conditional | flops 2 | bytes 3162202 | solution.py:318
  12.0 0.1 stack.1
  12.1 0.4 %collective-permute-start.1 = (bf16[3,256,512]{2,1,0:T(8,128)(2,1)S(1)}, bf16[3,256,512]{2,1,0:T(8,128)(2,1)S(1)}, u32[]{:S(2)}, u32[]{:S(2)}) collective-permute-start(bf16[3,256,512]{2,1,0:T(8,128)(2,1)S(1)} %stack.1), channel_id=1, source_target_pairs={{0,1},{1,0},{2,3},{3,2},{4,5},{5,4},{6,7},{7,6},{8,9},{9,8},{10,11... | collective-permute-start | bytes 2359304 | tf_op jit(solution)/shard_map/cond/branch_1_fun/ppermute | solution.py:298
  12.5 2.2 %collective-permute-start = (f32[1,1024]{1,0:T(1,128)S(1)}, f32[1,1024]{1,0:T(1,128)S(1)}, u32[]{:S(2)}, u32[]{:S(2)}) collective-permute-start(f32[1,1024]{1,0:T(1,128)S(1)} %get-tuple-element.8.refs_0_), channel_id=1, source_target_pairs={{0,1},{1,9},{2,3},{3,11},{4,5},{5,13},{6,7},{7,15},{8,0},{9,8},{10... | collective-permute-start | bytes 12296 | tf_op jit(solution)/shard_map/cond/branch_1_fun/ppermute | solution.py:295
  14.7 0.8 %collective-permute-done.refs_1_ = f32[1,1024]{1,0:T(1,128)S(1)} collective-permute-done((f32[1,1024]{1,0:T(1,128)S(1)}, f32[1,1024]{1,0:T(1,128)S(1)}, u32[]{:S(2)}, u32[]{:S(2)}) %collective-permute-start) | collective-permute-done | bytes 4128 | tf_op jit(solution)/shard_map/cond/branch_1_fun/ppermute | solution.py:295
  15.5 0.0 collective-permute-done.1.refs_5_
  15.5 0.0 collective-permute-done.3.refs_0_
  15.5 0.0 collective-permute-done.4.refs_1_
  15.5 2.5 %collective-permute-start.8 = (f32[1,1024]{1,0:T(1,128)S(1)}, f32[1,1024]{1,0:T(1,128)S(1)}, u32[]{:S(2)}, u32[]{:S(2)}) collective-permute-start(f32[1,1024]{1,0:T(1,128)S(1)} %get-tuple-element.35), channel_id=1, source_target_pairs={{0,8},{1,0},{2,10},{3,2},{4,12},{5,4},{6,14},{7,6},{8,9},{9,1},{10... | collective-permute-start | bytes 12296 | tf_op jit(solution)/shard_map/ppermute | solution.py:295
  18.0 1.9 %collective-permute-done.8.returned = f32[1,1024]{1,0:T(1,128)S(1)} collective-permute-done((f32[1,1024]{1,0:T(1,128)S(1)}, f32[1,1024]{1,0:T(1,128)S(1)}, u32[]{:S(2)}, u32[]{:S(2)}) %collective-permute-start.8) | collective-permute-done | bytes 4128 | tf_op jit(solution)/shard_map/ppermute | solution.py:295
  19.9 0.6 %finish.1 = (f32[1,512]{1,0:T(1,128)}, f32[1,1024]{1,0:T(1,128)}) custom-call(f32[8,128]{1,0:T(8,128)S(1)} %outer.1.grad, f32[1,1024]{1,0:T(1,128)S(1)} %get-tuple-element.34.near, f32[1,1024]{1,0:T(1,128)S(1)} %collective-permute-done.8.returned), custom_call_target="tpu_custom_call" | custom-call | flops 1 | bytes 1 | tf_op jit(solution)/shard_map/finish/pallas_call | solution.py:134
  (4 shorter events, 0.0 us)
Async XLA Ops:
  0.6 5.8 %copy-start.1 = (bf16[1,256,4096]{2,1,0:T(8,128)(2,1)S(1)}, bf16[1,256,4096]{2,1,0:T(8,128)(2,1)}, u32[]{:S(2)}) copy-start(bf16[1,256,4096]{2,1,0:T(8,128)(2,1)} %param.9) | copy-start | bytes 6291460
  0.6 5.8 %copy-start.4 = (bf16[32,4096]{1,0:T(8,128)(2,1)S(1)}, bf16[32,4096]{1,0:T(8,128)(2,1)}, u32[]{:S(2)}) copy-start(bf16[32,4096]{1,0:T(8,128)(2,1)} %out_f.1) | copy-start | bytes 786436
  0.6 6.5 %copy-start = (bf16[1,256,14784]{1,2,0:T(8,128)(2,1)S(1)}, bf16[1,256,14784]{1,2,0:T(8,128)(2,1)}, u32[]{:S(2)}) copy-start(bf16[1,256,14784]{1,2,0:T(8,128)(2,1)} %param.8) | copy-start | bytes 22708228
  0.7 6.5 %copy-start.3 = (bf16[32,14784]{1,0:T(8,128)(2,1)S(1)}, bf16[32,14784]{1,0:T(8,128)(2,1)}, u32[]{:S(2)}) copy-start(bf16[32,14784]{1,0:T(8,128)(2,1)} %in_f.1) | copy-start | bytes 2838532
  0.7 11.3 %collective-permute-start.6 = (bf16[256,512]{1,0:T(8,128)(2,1)}, bf16[256,512]{1,0:T(8,128)(2,1)S(1)}, u32[]{:S(2)}, u32[]{:S(2)}) collective-permute-start(bf16[256,512]{1,0:T(8,128)(2,1)} %queries), channel_id=1, source_target_pairs={{0,2},{1,5},{2,6},{3,1},{4,0},{5,7},{6,4},{7,3},{8,10},{9,13},{10,... | collective-permute-start | bytes 786440 | tf_op jit(solution)/shard_map/ppermute | solution.py:295
  2.9 9.2 %collective-permute-start.7 = (bf16[256,512]{1,0:T(8,128)(2,1)}, bf16[256,512]{1,0:T(8,128)(2,1)S(1)}, u32[]{:S(2)}, u32[]{:S(2)}) collective-permute-start(bf16[256,512]{1,0:T(8,128)(2,1)} %queries), channel_id=1, source_target_pairs={{0,4},{1,3},{2,0},{3,7},{4,6},{5,1},{6,2},{7,5},{8,12},{9,11},{10,... | collective-permute-start | bytes 786440 | tf_op jit(solution)/shard_map/ppermute | solution.py:295
  2.9 12.6 %collective-permute-start.3 = (bf16[256,512]{1,0:T(8,128)(2,1)}, bf16[256,512]{1,0:T(8,128)(2,1)S(1)}, u32[]{:S(2)}, u32[]{:S(2)}) collective-permute-start(bf16[256,512]{1,0:T(8,128)(2,1)} %queries), channel_id=1, source_target_pairs={{0,6},{1,17},{2,4},{3,19},{4,2},{5,21},{6,0},{7,23},{8,24},{9,15},... | collective-permute-start | bytes 786440 | tf_op jit(solution)/shard_map/ppermute | solution.py:295
  4.2 11.3 %collective-permute-start.4 = (bf16[256,512]{1,0:T(8,128)(2,1)}, bf16[256,512]{1,0:T(8,128)(2,1)S(1)}, u32[]{:S(2)}, u32[]{:S(2)}) collective-permute-start(bf16[256,512]{1,0:T(8,128)(2,1)} %queries), channel_id=1, source_target_pairs={{0,1},{1,6},{2,3},{3,4},{4,5},{5,2},{6,7},{7,0},{8,15},{9,8},{10,1... | collective-permute-start | bytes 786440 | tf_op jit(solution)/shard_map/ppermute | solution.py:295
  7.2 1.9 %copy-start.2 = (f32[512,1024]{1,0:T(8,128)S(1)}, f32[512,1024]{1,0:T(8,128)}, u32[]{:S(2)}) copy-start(f32[512,1024]{1,0:T(8,128)} %values.3) | copy-start | bytes 6291460
  8.6 1.3 %collective-permute-start.2 = (f32[64,256]{1,0:T(8,128)S(1)}, f32[64,256]{1,0:T(8,128)S(1)}, u32[]{:S(2)}, u32[]{:S(2)}) collective-permute-start(f32[64,256]{1,0:T(8,128)S(1)} %get-tuple-element.27.mine), channel_id=1, source_target_pairs={{0,1},{1,0},{2,3},{3,2},{4,5},{5,4},{6,7},{7,6},{8,9},{9,8},{10,11... | collective-permute-start | bytes 196616 | tf_op jit(solution)/shard_map/ppermute | solution.py:298
  10.8 1.2 %collective-permute-start.5 = (f32[1,512]{1,0:T(1,128)S(1)}, f32[1,512]{1,0:T(1,128)S(1)}, u32[]{:S(2)}, u32[]{:S(2)}) collective-permute-start(f32[1,512]{1,0:T(1,128)S(1)} %precondition.1.mine), channel_id=1, source_target_pairs={{0,1},{1,0},{2,3},{3,2},{4,5},{5,4},{6,7},{7,6},{8,9},{9,8},{10,11... | collective-permute-start | bytes 6152 | tf_op jit(solution)/shard_map/ppermute | solution.py:298
  12.1 3.4 %collective-permute-start.1 = (bf16[3,256,512]{2,1,0:T(8,128)(2,1)S(1)}, bf16[3,256,512]{2,1,0:T(8,128)(2,1)S(1)}, u32[]{:S(2)}, u32[]{:S(2)}) collective-permute-start(bf16[3,256,512]{2,1,0:T(8,128)(2,1)S(1)} %stack.1), channel_id=1, source_target_pairs={{0,1},{1,0},{2,3},{3,2},{4,5},{5,4},{6,7},{7,6},{8,9},{9,8},{10,11... | collective-permute-start | bytes 2359304 | tf_op jit(solution)/shard_map/cond/branch_1_fun/ppermute | solution.py:298
  12.5 3.0 %collective-permute-start = (f32[1,1024]{1,0:T(1,128)S(1)}, f32[1,1024]{1,0:T(1,128)S(1)}, u32[]{:S(2)}, u32[]{:S(2)}) collective-permute-start(f32[1,1024]{1,0:T(1,128)S(1)} %get-tuple-element.8.refs_0_), channel_id=1, source_target_pairs={{0,1},{1,9},{2,3},{3,11},{4,5},{5,13},{6,7},{7,15},{8,0},{9,8},{10... | collective-permute-start | bytes 12296 | tf_op jit(solution)/shard_map/cond/branch_1_fun/ppermute | solution.py:295
  15.5 4.4 %collective-permute-start.8 = (f32[1,1024]{1,0:T(1,128)S(1)}, f32[1,1024]{1,0:T(1,128)S(1)}, u32[]{:S(2)}, u32[]{:S(2)}) collective-permute-start(f32[1,1024]{1,0:T(1,128)S(1)} %get-tuple-element.35), channel_id=1, source_target_pairs={{0,8},{1,0},{2,10},{3,2},{4,12},{5,4},{6,14},{7,6},{8,9},{9,1},{10... | collective-permute-start | bytes 12296 | tf_op jit(solution)/shard_map/ppermute | solution.py:295

commit v5 on v4

--- a/solution.py
+++ b/solution.py
@@ -8,14 +8,9 @@
 from jax.sharding import PartitionSpec as P
 
 LANES = 128
-CHUNK = 2048
 NT = (((1,), (1,)), ((), ()))
 ANY = pl.BlockSpec(memory_space=pl.ANY)
 VMEM = pl.BlockSpec(memory_space=pltpu.VMEM)
-
-
-def pieces(total, step):
-    return [(start, min(step, total - start)) for start in range(0, total, step)]
 
 
 def split(values, count):
@@ -153,6 +148,15 @@
 def prepare(values):
     part = jax.ShapeDtypeStruct(values.shape, jnp.bfloat16)
     return small("prepare", prepare_kernel, (part, part), (values,))
+
+
+def keep_kernel(values, result):
+    result[...] = values[...]
+
+
+def keep(values):
+    shape = jax.ShapeDtypeStruct(values.shape, values.dtype)
+    return small("keep", keep_kernel, shape, (values,))
 
 
 def stack_kernel(*refs):
@@ -322,14 +326,9 @@
         half_precond = precondition(grad, high, low)
         return grad, both_halves(half_precond, swap(half_precond))
 
-    def forward(g, e, t, on):
-        if e < half:
-            return (g, e, 1 - t) if on else (g, e ^ half, t)
-        return (g, e, 1 - t) if on else (g, e ^ half, t)
-
     def exchange(precond, *blocks):
-        others = swap(stack(blocks))
-        far = send(precond, forward)
+        far = send(precond, lambda g, e, t, on: (g, e, 1 - t) if on else (g, e ^ half, t))
+        others = whole(lambda *values: keep(swap(stack(values))), *blocks)
         return score(half, [(0, 0), *ways], (precond, far), blocks, others)
 
     out_part = project_out(token, out_grads[0], out_factor)

time: 20.8 us -> 20.7 us (level)
  starting transfers between devices: 11.7 us -> 9.81 us
  waiting for transfers between devices: 4.12 us -> 5.88 us
    ppermute x3, waiting for transfers between devices: 1.43 us -> 3.7 us  [swap(): return lax.ppermute(values, 'tp', [(0, 1), (1, 0)])]
    ppermute x6, starting transfers between devices: 10.5 us -> 8.94 us  [send(): return lax.ppermute(values, axes, pairs)]
    ppermute x6, waiting for transfers between devices: 2.7 us -> 2.18 us  [send(): return lax.ppermute(values, axes, pairs)]
    ppermute x3, starting transfers between devices: 1.21 us -> 0.88 us  [swap(): return lax.ppermute(values, 'tp', [(0, 1), (1, 0)])]
    pallas_call x7 -> x8, Pallas kernels: 1.64 us -> 1.71 us  [small(): pl.pallas_call(kernel, out_shape=out_shape, in_specs=specs, out_specs=jax...]
  transfers between devices with their start and end apart: 9 -> 9, of which waited for: 4 -> 4; matrix products, arithmetic and copies ran while one was open for 0% -> 0% of each run, Pallas kernels for 16% -> 17%
where the time goes in v5:
time: 20.7 us; the launch traced here: 20.6 us
  starting transfers between devices  9.81 us (47%)
  waiting for transfers between devices  5.88 us (28%)
  Pallas kernels  4.04 us (20%)
  between operations  0.76 us (4%)
    ppermute x6, starting transfers between devices, send(): return lax.ppermute(values, axes, pairs)  8.94 us
    ppermute x3, waiting for transfers between devices, swap(): return lax.ppermute(values, 'tp', [(0, 1), (1, 0)])  3.7 us
    ppermute x6, waiting for transfers between devices, send(): return lax.ppermute(values, axes, pairs)  2.18 us
    pallas_call x8, Pallas kernels, small(): pl.pallas_call(kernel, out_shape=out_shape, in_specs=specs, out_specs=jax...  1.71 us
    pallas_call x1, Pallas kernels, project_in(): pl.pallas_call(in_kernel, out_shape=(jax.ShapeDtypeStruct((2 * rank, toke...  1.41 us
    ppermute x3, starting transfers between devices, swap(): return lax.ppermute(values, 'tp', [(0, 1), (1, 0)])  0.88 us
    pallas_call x1, Pallas kernels, project_out(): pl.pallas_call(out_kernel, out_shape=jax.ShapeDtypeStruct((out_factor.sha...  0.7 us
  transfers between devices with their start and end apart: 9, of which 4 were waited for; matrix products, arithmetic and copies ran while one was open for 0% of the time, Pallas kernels for 17%

profile of v5, /device:TPU:1, one launch (start us, length us, event | category | flops | bytes accessed | tf_op | source)
XLA Modules:
  0.0 20.6 jit_solution(15880300992895786630)
XLA Ops:
  0.6 0.0 copy-start.1
  0.6 0.0 copy-start.4
  0.6 0.0 copy-start
  0.7 0.0 copy-start.3
  0.7 2.2 %collective-permute-start.6 = (bf16[256,512]{1,0:T(8,128)(2,1)}, bf16[256,512]{1,0:T(8,128)(2,1)S(1)}, u32[]{:S(2)}, u32[]{:S(2)}) collective-permute-start(bf16[256,512]{1,0:T(8,128)(2,1)} %queries), channel_id=1, source_target_pairs={{0,2},{1,5},{2,6},{3,1},{4,0},{5,7},{6,4},{7,3},{8,10},{9,13},{10,... | collective-permute-start | bytes 786440 | tf_op jit(solution)/shard_map/ppermute | solution.py:299
  2.9 0.0 collective-permute-start.7
  2.9 1.4 %collective-permute-start.3 = (bf16[256,512]{1,0:T(8,128)(2,1)}, bf16[256,512]{1,0:T(8,128)(2,1)S(1)}, u32[]{:S(2)}, u32[]{:S(2)}) collective-permute-start(bf16[256,512]{1,0:T(8,128)(2,1)} %queries), channel_id=1, source_target_pairs={{0,6},{1,17},{2,4},{3,19},{4,2},{5,21},{6,0},{7,23},{8,24},{9,15},... | collective-permute-start | bytes 786440 | tf_op jit(solution)/shard_map/ppermute | solution.py:299
  4.2 2.2 %collective-permute-start.4 = (bf16[256,512]{1,0:T(8,128)(2,1)}, bf16[256,512]{1,0:T(8,128)(2,1)S(1)}, u32[]{:S(2)}, u32[]{:S(2)}) collective-permute-start(bf16[256,512]{1,0:T(8,128)(2,1)} %queries), channel_id=1, source_target_pairs={{0,1},{1,6},{2,3},{3,4},{4,5},{5,2},{6,7},{7,0},{8,15},{9,8},{10,1... | collective-permute-start | bytes 786440 | tf_op jit(solution)/shard_map/ppermute | solution.py:299
  6.4 0.0 copy-done.1
  6.4 0.0 copy-done.4
  6.4 0.7 %project_out.1.out_part = f32[32,256]{1,0:T(8,128)S(1)} custom-call(f32[8,128]{1,0:T(8,128)S(1)} %stage.1.token, bf16[256,4096]{1,0:T(8,128)(2,1)S(1)} %bitcast.5, bf16[32,4096]{1,0:T(8,128)(2,1)S(1)} %copy-done.4), custom_call_target="tpu_custom_call" | custom-call | flops 67108864 | bytes 2359296 | tf_op jit(solution)/shard_map/project_out/pallas_call | solution.py:39
  7.1 0.0 copy-done
  7.2 0.0 copy-done.3
  7.2 0.0 copy-start.2
  7.2 1.4 %project_in.1 = (f32[64,256]{1,0:T(8,128)S(1)}, bf16[256,512]{1,0:T(8,128)(2,1)S(1)}) custom-call(f32[32,256]{1,0:T(8,128)S(1)} %project_out.1.out_part, bf16[14784,256]{1,0:T(8,128)(2,1)S(1)} %bitcast.4, bf16[32,14784]{1,0:T(8,128)(2,1)S(1)} %copy-done.3, bf16[256,512]{1,0:T(8,128)(2,1)} %queries), custom_call_target="tpu_custom_call" | custom-call | flops 242221056 | bytes 8515584 | tf_op jit(solution)/shard_map/project_in/pallas_call | solution.py:56
  8.6 0.4 %collective-permute-start.2 = (f32[64,256]{1,0:T(8,128)S(1)}, f32[64,256]{1,0:T(8,128)S(1)}, u32[]{:S(2)}, u32[]{:S(2)}) collective-permute-start(f32[64,256]{1,0:T(8,128)S(1)} %get-tuple-element.39.mine), channel_id=1, source_target_pairs={{0,1},{1,0},{2,3},{3,2},{4,5},{5,4},{6,7},{7,6},{8,9},{9,8},{10,11... | collective-permute-start | bytes 196616 | tf_op jit(solution)/shard_map/ppermute | solution.py:302
  9.1 0.0 copy-done.2
  9.1 0.3 %prepare.1 = (bf16[512,1024]{1,0:T(8,128)(2,1)S(1)}, bf16[512,1024]{1,0:T(8,128)(2,1)S(1)}) custom-call(f32[512,1024]{1,0:T(8,128)S(1)} %copy-done.2), custom_call_target="tpu_custom_call" | custom-call | flops 1 | bytes 1 | tf_op jit(solution)/shard_map/prepare/pallas_call | solution.py:129
  9.4 0.6 %collective-permute-done.2.other = f32[64,256]{1,0:T(8,128)S(1)} collective-permute-done((f32[64,256]{1,0:T(8,128)S(1)}, f32[64,256]{1,0:T(8,128)S(1)}, u32[]{:S(2)}, u32[]{:S(2)}) %collective-permute-start.2) | collective-permute-done | bytes 65568 | tf_op jit(solution)/shard_map/ppermute | solution.py:302
  10.0 0.2 %outer.1.grad = f32[8,128]{1,0:T(8,128)S(1)} custom-call(f32[64,256]{1,0:T(8,128)S(1)} %get-tuple-element.39.mine, f32[64,256]{1,0:T(8,128)S(1)} %collective-permute-done.2.other), custom_call_target="tpu_custom_call" | custom-call | tf_op jit(solution)/shard_map/outer/pallas_call | solution.py:108
  10.2 0.7 %precondition.1.mine = f32[1,512]{1,0:T(1,128)S(1)} custom-call(f32[8,128]{1,0:T(8,128)S(1)} %outer.1.grad, bf16[512,1024]{1,0:T(8,128)(2,1)S(1)} %get-tuple-element.40.high, bf16[512,1024]{1,0:T(8,128)(2,1)S(1)} %get-tuple-element.41.low), custom_call_target="tpu_custom_call" | custom-call | flops 1 | bytes 1 | tf_op jit(solution)/shard_map/precondition/pallas_call | solution.py:129
  10.8 0.4 %collective-permute-start.5 = (f32[1,512]{1,0:T(1,128)S(1)}, f32[1,512]{1,0:T(1,128)S(1)}, u32[]{:S(2)}, u32[]{:S(2)}) collective-permute-start(f32[1,512]{1,0:T(1,128)S(1)} %precondition.1.mine), channel_id=1, source_target_pairs={{0,1},{1,0},{2,3},{3,2},{4,5},{5,4},{6,7},{7,6},{8,9},{9,8},{10,11... | collective-permute-start | bytes 6152 | tf_op jit(solution)/shard_map/ppermute | solution.py:302
  11.2 0.8 %collective-permute-done.5.other = f32[1,512]{1,0:T(1,128)S(1)} collective-permute-done((f32[1,512]{1,0:T(1,128)S(1)}, f32[1,512]{1,0:T(1,128)S(1)}, u32[]{:S(2)}, u32[]{:S(2)}) %collective-permute-start.5) | collective-permute-done | bytes 2080 | tf_op jit(solution)/shard_map/ppermute | solution.py:302
  12.0 0.0 collective-permute-done.6
  12.0 0.0 collective-permute-done.7
  12.0 4.2 %conditional.2 = ((f32[1,1024]{1,0:T(1,128)S(1)}, f32[1,1024]{1,0:T(1,128)S(1)}, bf16[6,1024]{1,0:T(8,128)(2,1)S(1)})) conditional(s32[]{:T(128)} %convert_element_type.6, () %tuple.22, (f32[1,1024]{1,0:T(1,128)S(1)}, bf16[256,512]{1,0:T(8,128)(2,1)S(1)}, bf16[256,512]{1,0:T(8,128)(2,1)S(1)}, bf16[256,512]{1,0:T(8,128)(2,1)S(1)}) %tuple.23), branch_computations={%region_0.0_spmd, %region_1.0_spmd} | conditional | flops 8 | bytes 3162281 | solution.py:322
  12.0 1.7 %collective-permute-start.1 = (f32[1,1024]{1,0:T(1,128)S(1)}, f32[1,1024]{1,0:T(1,128)S(1)}, u32[]{:S(2)}, u32[]{:S(2)}) collective-permute-start(f32[1,1024]{1,0:T(1,128)S(1)} %get-tuple-element.20.refs_0_), channel_id=1, source_target_pairs={{0,1},{1,9},{2,3},{3,11},{4,5},{5,13},{6,7},{7,15},{8,0},{9,8},{10... | collective-permute-start | bytes 12296 | tf_op jit(solution)/shard_map/cond/branch_1_fun/ppermute | solution.py:299
  13.7 2.5 %conditional = (bf16[3,256,512]{2,1,0:T(8,128)(2,1)S(1)}) conditional(s32[]{:T(128)} %convert_element_type.4, () %tuple.15, (bf16[256,512]{1,0:T(8,128)(2,1)S(1)}, bf16[256,512]{1,0:T(8,128)(2,1)S(1)}, bf16[256,512]{1,0:T(8,128)(2,1)S(1)}) %tuple.16), branch_computations={%region_2.0_spmd, %region_3.0_spmd} | conditional | flops 2 | bytes 3145778 | solution.py:322
  13.7 0.1 stack.1
  13.8 0.1 collective-permute-start
  13.8 2.3 %collective-permute-done.values = bf16[3,256,512]{2,1,0:T(8,128)(2,1)S(1)} collective-permute-done((bf16[3,256,512]{2,1,0:T(8,128)(2,1)S(1)}, bf16[3,256,512]{2,1,0:T(8,128)(2,1)S(1)}, u32[]{:S(2)}, u32[]{:S(2)}) %collective-permute-start) | collective-permute-done | bytes 786464 | tf_op jit(solution)/shard_map/cond/branch_1_fun/cond/branch_1_fun/ppermute | solution.py:302
  16.1 0.1 keep.1
  16.2 0.0 collective-permute-done.1.refs_1_
  16.2 0.0 collective-permute-done.3.refs_0_
  16.2 0.0 collective-permute-done.4.refs_1_
  16.3 1.5 %collective-permute-start.8 = (f32[1,1024]{1,0:T(1,128)S(1)}, f32[1,1024]{1,0:T(1,128)S(1)}, u32[]{:S(2)}, u32[]{:S(2)}) collective-permute-start(f32[1,1024]{1,0:T(1,128)S(1)} %get-tuple-element.47), channel_id=1, source_target_pairs={{0,8},{1,0},{2,10},{3,2},{4,12},{5,4},{6,14},{7,6},{8,9},{9,1},{10... | collective-permute-start | bytes 12296 | tf_op jit(solution)/shard_map/ppermute | solution.py:299
  17.8 2.2 %collective-permute-done.8.returned = f32[1,1024]{1,0:T(1,128)S(1)} collective-permute-done((f32[1,1024]{1,0:T(1,128)S(1)}, f32[1,1024]{1,0:T(1,128)S(1)}, u32[]{:S(2)}, u32[]{:S(2)}) %collective-permute-start.8) | collective-permute-done | bytes 4128 | tf_op jit(solution)/shard_map/ppermute | solution.py:299
  19.9 0.6 %finish.1 = (f32[1,512]{1,0:T(1,128)}, f32[1,1024]{1,0:T(1,128)}) custom-call(f32[8,128]{1,0:T(8,128)S(1)} %outer.1.grad, f32[1,1024]{1,0:T(1,128)S(1)} %get-tuple-element.46.near, f32[1,1024]{1,0:T(1,128)S(1)} %collective-permute-done.8.returned), custom_call_target="tpu_custom_call" | custom-call | flops 1 | bytes 1 | tf_op jit(solution)/shard_map/finish/pallas_call | solution.py:129
  (4 shorter events, 0.1 us)
Async XLA Ops:
  0.6 5.8 %copy-start.1 = (bf16[1,256,4096]{2,1,0:T(8,128)(2,1)S(1)}, bf16[1,256,4096]{2,1,0:T(8,128)(2,1)}, u32[]{:S(2)}) copy-start(bf16[1,256,4096]{2,1,0:T(8,128)(2,1)} %param.11) | copy-start | bytes 6291460
  0.6 5.8 %copy-start.4 = (bf16[32,4096]{1,0:T(8,128)(2,1)S(1)}, bf16[32,4096]{1,0:T(8,128)(2,1)}, u32[]{:S(2)}) copy-start(bf16[32,4096]{1,0:T(8,128)(2,1)} %out_f.1) | copy-start | bytes 786436
  0.6 6.5 %copy-start = (bf16[1,256,14784]{1,2,0:T(8,128)(2,1)S(1)}, bf16[1,256,14784]{1,2,0:T(8,128)(2,1)}, u32[]{:S(2)}) copy-start(bf16[1,256,14784]{1,2,0:T(8,128)(2,1)} %param.10) | copy-start | bytes 22708228
  0.7 6.5 %copy-start.3 = (bf16[32,14784]{1,0:T(8,128)(2,1)S(1)}, bf16[32,14784]{1,0:T(8,128)(2,1)}, u32[]{:S(2)}) copy-start(bf16[32,14784]{1,0:T(8,128)(2,1)} %in_f.1) | copy-start | bytes 2838532
  0.7 11.3 %collective-permute-start.6 = (bf16[256,512]{1,0:T(8,128)(2,1)}, bf16[256,512]{1,0:T(8,128)(2,1)S(1)}, u32[]{:S(2)}, u32[]{:S(2)}) collective-permute-start(bf16[256,512]{1,0:T(8,128)(2,1)} %queries), channel_id=1, source_target_pairs={{0,2},{1,5},{2,6},{3,1},{4,0},{5,7},{6,4},{7,3},{8,10},{9,13},{10,... | collective-permute-start | bytes 786440 | tf_op jit(solution)/shard_map/ppermute | solution.py:299
  2.9 9.2 %collective-permute-start.7 = (bf16[256,512]{1,0:T(8,128)(2,1)}, bf16[256,512]{1,0:T(8,128)(2,1)S(1)}, u32[]{:S(2)}, u32[]{:S(2)}) collective-permute-start(bf16[256,512]{1,0:T(8,128)(2,1)} %queries), channel_id=1, source_target_pairs={{0,4},{1,3},{2,0},{3,7},{4,6},{5,1},{6,2},{7,5},{8,12},{9,11},{10,... | collective-permute-start | bytes 786440 | tf_op jit(solution)/shard_map/ppermute | solution.py:299
  2.9 13.3 %collective-permute-start.3 = (bf16[256,512]{1,0:T(8,128)(2,1)}, bf16[256,512]{1,0:T(8,128)(2,1)S(1)}, u32[]{:S(2)}, u32[]{:S(2)}) collective-permute-start(bf16[256,512]{1,0:T(8,128)(2,1)} %queries), channel_id=1, source_target_pairs={{0,6},{1,17},{2,4},{3,19},{4,2},{5,21},{6,0},{7,23},{8,24},{9,15},... | collective-permute-start | bytes 786440 | tf_op jit(solution)/shard_map/ppermute | solution.py:299
  4.2 12.0 %collective-permute-start.4 = (bf16[256,512]{1,0:T(8,128)(2,1)}, bf16[256,512]{1,0:T(8,128)(2,1)S(1)}, u32[]{:S(2)}, u32[]{:S(2)}) collective-permute-start(bf16[256,512]{1,0:T(8,128)(2,1)} %queries), channel_id=1, source_target_pairs={{0,1},{1,6},{2,3},{3,4},{4,5},{5,2},{6,7},{7,0},{8,15},{9,8},{10,1... | collective-permute-start | bytes 786440 | tf_op jit(solution)/shard_map/ppermute | solution.py:299
  7.2 1.9 %copy-start.2 = (f32[512,1024]{1,0:T(8,128)S(1)}, f32[512,1024]{1,0:T(8,128)}, u32[]{:S(2)}) copy-start(f32[512,1024]{1,0:T(8,128)} %values.3) | copy-start | bytes 6291460
  8.6 1.3 %collective-permute-start.2 = (f32[64,256]{1,0:T(8,128)S(1)}, f32[64,256]{1,0:T(8,128)S(1)}, u32[]{:S(2)}, u32[]{:S(2)}) collective-permute-start(f32[64,256]{1,0:T(8,128)S(1)} %get-tuple-element.39.mine), channel_id=1, source_target_pairs={{0,1},{1,0},{2,3},{3,2},{4,5},{5,4},{6,7},{7,6},{8,9},{9,8},{10,11... | collective-permute-start | bytes 196616 | tf_op jit(solution)/shard_map/ppermute | solution.py:302
  10.8 1.2 %collective-permute-start.5 = (f32[1,512]{1,0:T(1,128)S(1)}, f32[1,512]{1,0:T(1,128)S(1)}, u32[]{:S(2)}, u32[]{:S(2)}) collective-permute-start(f32[1,512]{1,0:T(1,128)S(1)} %precondition.1.mine), channel_id=1, source_target_pairs={{0,1},{1,0},{2,3},{3,2},{4,5},{5,4},{6,7},{7,6},{8,9},{9,8},{10,11... | collective-permute-start | bytes 6152 | tf_op jit(solution)/shard_map/ppermute | solution.py:302
  12.0 4.1 %collective-permute-start.1 = (f32[1,1024]{1,0:T(1,128)S(1)}, f32[1,1024]{1,0:T(1,128)S(1)}, u32[]{:S(2)}, u32[]{:S(2)}) collective-permute-start(f32[1,1024]{1,0:T(1,128)S(1)} %get-tuple-element.20.refs_0_), channel_id=1, source_target_pairs={{0,1},{1,9},{2,3},{3,11},{4,5},{5,13},{6,7},{7,15},{8,0},{9,8},{10... | collective-permute-start | bytes 12296 | tf_op jit(solution)/shard_map/cond/branch_1_fun/ppermute | solution.py:299
  13.8 2.4 %collective-permute-start = (bf16[3,256,512]{2,1,0:T(8,128)(2,1)S(1)}, bf16[3,256,512]{2,1,0:T(8,128)(2,1)S(1)}, u32[]{:S(2)}, u32[]{:S(2)}) collective-permute-start(bf16[3,256,512]{2,1,0:T(8,128)(2,1)S(1)} %stack.1), channel_id=1, source_target_pairs={{0,1},{1,0},{2,3},{3,2},{4,5},{5,4},{6,7},{7,6},{8,9},{9,8},{10,11... | collective-permute-start | bytes 2359304 | tf_op jit(solution)/shard_map/cond/branch_1_fun/cond/branch_1_fun/ppermute | solution.py:302
  16.3 3.7 %collective-permute-start.8 = (f32[1,1024]{1,0:T(1,128)S(1)}, f32[1,1024]{1,0:T(1,128)S(1)}, u32[]{:S(2)}, u32[]{:S(2)}) collective-permute-start(f32[1,1024]{1,0:T(1,128)S(1)} %get-tuple-element.47), channel_id=1, source_target_pairs={{0,8},{1,0},{2,10},{3,2},{4,12},{5,4},{6,14},{7,6},{8,9},{9,1},{10... | collective-permute-start | bytes 12296 | tf_op jit(solution)/shard_map/ppermute | solution.py:299

commit v6 on v5

--- a/solution.py
+++ b/solution.py
@@ -326,17 +326,14 @@
         half_precond = precondition(grad, high, low)
         return grad, both_halves(half_precond, swap(half_precond))
 
-    def exchange(precond, *blocks):
-        far = send(precond, lambda g, e, t, on: (g, e, 1 - t) if on else (g, e ^ half, t))
-        others = whole(lambda *values: keep(swap(stack(values))), *blocks)
-        return score(half, [(0, 0), *ways], (precond, far), blocks, others)
-
     out_part = project_out(token, out_grads[0], out_factor)
     part, own = project_in(out_part, activations[0].T, in_factor, queries)
     high, low = prepare(curvature_inv)
     grad, precond = gradient(part, high, low)
-    precond, *blocks = lax.optimization_barrier((precond, own, *early))
-    scores = whole(exchange, precond, *blocks)
+    blocks = [own, *early]
+    far_row = send(precond, lambda g, e, t, on: (g, e, 1 - t) if on else (g, e ^ half, t))
+    others = whole(lambda *values: keep(swap(stack(values))), *blocks)
+    scores = score(half, [(0, 0), *ways], (precond, far_row), blocks, others)
     if last:
         way = half - 1
         scores = score(half, [(way, way)], (), last[:1], last[1], scores)

time: 20.7 us -> 20.7 us (level)
  no operation moved by 1% of the time
where the time goes in v6:
time: 20.7 us; the launch traced here: 20.6 us
  starting transfers between devices  9.73 us (47%)
  waiting for transfers between devices  5.97 us (29%)
  Pallas kernels  4.04 us (20%)
  between operations  0.77 us (4%)
    ppermute x6, starting transfers between devices, send(): return lax.ppermute(values, axes, pairs)  8.85 us
    ppermute x3, waiting for transfers between devices, swap(): return lax.ppermute(values, 'tp', [(0, 1), (1, 0)])  3.7 us
    ppermute x6, waiting for transfers between devices, send(): return lax.ppermute(values, axes, pairs)  2.27 us
    pallas_call x8, Pallas kernels, small(): pl.pallas_call(kernel, out_shape=out_shape, in_specs=specs, out_specs=jax...  1.71 us
    pallas_call x1, Pallas kernels, project_in(): pl.pallas_call(in_kernel, out_shape=(jax.ShapeDtypeStruct((2 * rank, toke...  1.41 us
    ppermute x3, starting transfers between devices, swap(): return lax.ppermute(values, 'tp', [(0, 1), (1, 0)])  0.88 us
    pallas_call x1, Pallas kernels, project_out(): pl.pallas_call(out_kernel, out_shape=jax.ShapeDtypeStruct((out_factor.sha...  0.7 us
  transfers between devices with their start and end apart: 9, of which 4 were waited for; matrix products, arithmetic and copies ran while one was open for 0% of the time, Pallas kernels for 17%

profile of v6, /device:TPU:1, one launch (start us, length us, event | category | flops | bytes accessed | tf_op | source)
XLA Modules:
  0.0 20.6 jit_solution(3027895271104501520)
XLA Ops:
  0.6 0.0 copy-start.1
  0.6 0.0 copy-start.4
  0.6 0.0 copy-start
  0.7 0.0 copy-start.3
  0.7 2.2 %collective-permute-start.6 = (bf16[256,512]{1,0:T(8,128)(2,1)}, bf16[256,512]{1,0:T(8,128)(2,1)S(1)}, u32[]{:S(2)}, u32[]{:S(2)}) collective-permute-start(bf16[256,512]{1,0:T(8,128)(2,1)} %queries), channel_id=1, source_target_pairs={{0,2},{1,5},{2,6},{3,1},{4,0},{5,7},{6,4},{7,3},{8,10},{9,13},{10,... | collective-permute-start | bytes 786440 | tf_op jit(solution)/shard_map/ppermute | solution.py:299
  2.9 0.0 collective-permute-start.7
  2.9 1.4 %collective-permute-start.2 = (bf16[256,512]{1,0:T(8,128)(2,1)}, bf16[256,512]{1,0:T(8,128)(2,1)S(1)}, u32[]{:S(2)}, u32[]{:S(2)}) collective-permute-start(bf16[256,512]{1,0:T(8,128)(2,1)} %queries), channel_id=1, source_target_pairs={{0,6},{1,17},{2,4},{3,19},{4,2},{5,21},{6,0},{7,23},{8,24},{9,15},... | collective-permute-start | bytes 786440 | tf_op jit(solution)/shard_map/ppermute | solution.py:299
  4.2 2.2 %collective-permute-start.3 = (bf16[256,512]{1,0:T(8,128)(2,1)}, bf16[256,512]{1,0:T(8,128)(2,1)S(1)}, u32[]{:S(2)}, u32[]{:S(2)}) collective-permute-start(bf16[256,512]{1,0:T(8,128)(2,1)} %queries), channel_id=1, source_target_pairs={{0,1},{1,6},{2,3},{3,4},{4,5},{5,2},{6,7},{7,0},{8,15},{9,8},{10,1... | collective-permute-start | bytes 786440 | tf_op jit(solution)/shard_map/ppermute | solution.py:299
  6.4 0.0 copy-done.1
  6.4 0.0 copy-done.4
  6.4 0.7 %project_out.1.out_part = f32[32,256]{1,0:T(8,128)S(1)} custom-call(f32[8,128]{1,0:T(8,128)S(1)} %stage.1.token, bf16[256,4096]{1,0:T(8,128)(2,1)S(1)} %bitcast.5, bf16[32,4096]{1,0:T(8,128)(2,1)S(1)} %copy-done.4), custom_call_target="tpu_custom_call" | custom-call | flops 67108864 | bytes 2359296 | tf_op jit(solution)/shard_map/project_out/pallas_call | solution.py:39
  7.1 0.0 copy-done
  7.2 0.0 copy-done.3
  7.2 0.0 copy-start.2
  7.2 1.4 %project_in.1 = (f32[64,256]{1,0:T(8,128)S(1)}, bf16[256,512]{1,0:T(8,128)(2,1)S(1)}) custom-call(f32[32,256]{1,0:T(8,128)S(1)} %project_out.1.out_part, bf16[14784,256]{1,0:T(8,128)(2,1)S(1)} %bitcast.4, bf16[32,14784]{1,0:T(8,128)(2,1)S(1)} %copy-done.3, bf16[256,512]{1,0:T(8,128)(2,1)} %queries), custom_call_target="tpu_custom_call" | custom-call | flops 242221056 | bytes 8515584 | tf_op jit(solution)/shard_map/project_in/pallas_call | solution.py:56
  8.6 0.4 %collective-permute-start.1 = (f32[64,256]{1,0:T(8,128)S(1)}, f32[64,256]{1,0:T(8,128)S(1)}, u32[]{:S(2)}, u32[]{:S(2)}) collective-permute-start(f32[64,256]{1,0:T(8,128)S(1)} %get-tuple-element.27.mine), channel_id=1, source_target_pairs={{0,1},{1,0},{2,3},{3,2},{4,5},{5,4},{6,7},{7,6},{8,9},{9,8},{10,11... | collective-permute-start | bytes 196616 | tf_op jit(solution)/shard_map/ppermute | solution.py:302
  9.1 0.0 copy-done.2
  9.1 0.3 %prepare.1 = (bf16[512,1024]{1,0:T(8,128)(2,1)S(1)}, bf16[512,1024]{1,0:T(8,128)(2,1)S(1)}) custom-call(f32[512,1024]{1,0:T(8,128)S(1)} %copy-done.2), custom_call_target="tpu_custom_call" | custom-call | flops 1 | bytes 1 | tf_op jit(solution)/shard_map/prepare/pallas_call | solution.py:129
  9.4 0.6 %collective-permute-done.1.other = f32[64,256]{1,0:T(8,128)S(1)} collective-permute-done((f32[64,256]{1,0:T(8,128)S(1)}, f32[64,256]{1,0:T(8,128)S(1)}, u32[]{:S(2)}, u32[]{:S(2)}) %collective-permute-start.1) | collective-permute-done | bytes 65568 | tf_op jit(solution)/shard_map/ppermute | solution.py:302
  10.0 0.2 %outer.1.grad = f32[8,128]{1,0:T(8,128)S(1)} custom-call(f32[64,256]{1,0:T(8,128)S(1)} %get-tuple-element.27.mine, f32[64,256]{1,0:T(8,128)S(1)} %collective-permute-done.1.other), custom_call_target="tpu_custom_call" | custom-call | tf_op jit(solution)/shard_map/outer/pallas_call | solution.py:108
  10.2 0.7 %precondition.1.mine = f32[1,512]{1,0:T(1,128)S(1)} custom-call(f32[8,128]{1,0:T(8,128)S(1)} %outer.1.grad, bf16[512,1024]{1,0:T(8,128)(2,1)S(1)} %get-tuple-element.28.high, bf16[512,1024]{1,0:T(8,128)(2,1)S(1)} %get-tuple-element.29.low), custom_call_target="tpu_custom_call" | custom-call | flops 1 | bytes 1 | tf_op jit(solution)/shard_map/precondition/pallas_call | solution.py:129
  10.8 0.4 %collective-permute-start.4 = (f32[1,512]{1,0:T(1,128)S(1)}, f32[1,512]{1,0:T(1,128)S(1)}, u32[]{:S(2)}, u32[]{:S(2)}) collective-permute-start(f32[1,512]{1,0:T(1,128)S(1)} %precondition.1.mine), channel_id=1, source_target_pairs={{0,1},{1,0},{2,3},{3,2},{4,5},{5,4},{6,7},{7,6},{8,9},{9,8},{10,11... | collective-permute-start | bytes 6152 | tf_op jit(solution)/shard_map/ppermute | solution.py:302
  11.2 0.8 %collective-permute-done.4.other = f32[1,512]{1,0:T(1,128)S(1)} collective-permute-done((f32[1,512]{1,0:T(1,128)S(1)}, f32[1,512]{1,0:T(1,128)S(1)}, u32[]{:S(2)}, u32[]{:S(2)}) %collective-permute-start.4) | collective-permute-done | bytes 2080 | tf_op jit(solution)/shard_map/ppermute | solution.py:302
  12.0 1.6 %collective-permute-start.5 = (f32[1,1024]{1,0:T(1,128)S(1)}, f32[1,1024]{1,0:T(1,128)S(1)}, u32[]{:S(2)}, u32[]{:S(2)}) collective-permute-start(f32[1,1024]{1,0:T(1,128)S(1)} %both_halves.1.refs_0_), channel_id=1, source_target_pairs={{0,1},{1,9},{2,3},{3,11},{4,5},{5,13},{6,7},{7,15},{8,0},{9,8},{10... | collective-permute-start | bytes 12296 | tf_op jit(solution)/shard_map/ppermute | solution.py:299
  13.6 0.0 collective-permute-done.6.refs_3_
  13.6 0.0 collective-permute-done.7.refs_4_
  13.6 2.5 %conditional.1 = (bf16[3,256,512]{2,1,0:T(8,128)(2,1)S(1)}) conditional(s32[]{:T(128)} %convert_element_type.3, () %tuple.15, (bf16[256,512]{1,0:T(8,128)(2,1)S(1)}, bf16[256,512]{1,0:T(8,128)(2,1)S(1)}, bf16[256,512]{1,0:T(8,128)(2,1)S(1)}) %tuple.16), branch_computations={%region_0.0_spmd, %region_1.0_spmd} | conditional | flops 2 | bytes 3145778 | solution.py:322
  13.6 0.1 stack.1
  13.7 0.1 collective-permute-start
  13.8 2.3 %collective-permute-done.values = bf16[3,256,512]{2,1,0:T(8,128)(2,1)S(1)} collective-permute-done((bf16[3,256,512]{2,1,0:T(8,128)(2,1)S(1)}, bf16[3,256,512]{2,1,0:T(8,128)(2,1)S(1)}, u32[]{:S(2)}, u32[]{:S(2)}) %collective-permute-start) | collective-permute-done | bytes 786464 | tf_op jit(solution)/shard_map/cond/branch_1_fun/ppermute | solution.py:302
  16.0 0.1 keep.1
  16.1 0.0 collective-permute-done.5.refs_1_
  16.1 0.0 collective-permute-done.2.refs_0_
  16.1 0.0 collective-permute-done.3.refs_1_
  16.2 1.5 %collective-permute-start.8 = (f32[1,1024]{1,0:T(1,128)S(1)}, f32[1,1024]{1,0:T(1,128)S(1)}, u32[]{:S(2)}, u32[]{:S(2)}) collective-permute-start(f32[1,1024]{1,0:T(1,128)S(1)} %get-tuple-element.35), channel_id=1, source_target_pairs={{0,8},{1,0},{2,10},{3,2},{4,12},{5,4},{6,14},{7,6},{8,9},{9,1},{10... | collective-permute-start | bytes 12296 | tf_op jit(solution)/shard_map/ppermute | solution.py:299
  17.7 2.3 %collective-permute-done.8.returned = f32[1,1024]{1,0:T(1,128)S(1)} collective-permute-done((f32[1,1024]{1,0:T(1,128)S(1)}, f32[1,1024]{1,0:T(1,128)S(1)}, u32[]{:S(2)}, u32[]{:S(2)}) %collective-permute-start.8) | collective-permute-done | bytes 4128 | tf_op jit(solution)/shard_map/ppermute | solution.py:299
  19.9 0.6 %finish.1 = (f32[1,512]{1,0:T(1,128)}, f32[1,1024]{1,0:T(1,128)}) custom-call(f32[8,128]{1,0:T(8,128)S(1)} %outer.1.grad, f32[1,1024]{1,0:T(1,128)S(1)} %get-tuple-element.34.near, f32[1,1024]{1,0:T(1,128)S(1)} %collective-permute-done.8.returned), custom_call_target="tpu_custom_call" | custom-call | flops 1 | bytes 1 | tf_op jit(solution)/shard_map/finish/pallas_call | solution.py:129
  (4 shorter events, 0.1 us)
Async XLA Ops:
  0.6 5.8 %copy-start.1 = (bf16[1,256,4096]{2,1,0:T(8,128)(2,1)S(1)}, bf16[1,256,4096]{2,1,0:T(8,128)(2,1)}, u32[]{:S(2)}) copy-start(bf16[1,256,4096]{2,1,0:T(8,128)(2,1)} %param.9) | copy-start | bytes 6291460
  0.6 5.8 %copy-start.4 = (bf16[32,4096]{1,0:T(8,128)(2,1)S(1)}, bf16[32,4096]{1,0:T(8,128)(2,1)}, u32[]{:S(2)}) copy-start(bf16[32,4096]{1,0:T(8,128)(2,1)} %out_f.1) | copy-start | bytes 786436
  0.6 6.5 %copy-start = (bf16[1,256,14784]{1,2,0:T(8,128)(2,1)S(1)}, bf16[1,256,14784]{1,2,0:T(8,128)(2,1)}, u32[]{:S(2)}) copy-start(bf16[1,256,14784]{1,2,0:T(8,128)(2,1)} %param.8) | copy-start | bytes 22708228
  0.7 6.5 %copy-start.3 = (bf16[32,14784]{1,0:T(8,128)(2,1)S(1)}, bf16[32,14784]{1,0:T(8,128)(2,1)}, u32[]{:S(2)}) copy-start(bf16[32,14784]{1,0:T(8,128)(2,1)} %in_f.1) | copy-start | bytes 2838532
  0.7 12.9 %collective-permute-start.6 = (bf16[256,512]{1,0:T(8,128)(2,1)}, bf16[256,512]{1,0:T(8,128)(2,1)S(1)}, u32[]{:S(2)}, u32[]{:S(2)}) collective-permute-start(bf16[256,512]{1,0:T(8,128)(2,1)} %queries), channel_id=1, source_target_pairs={{0,2},{1,5},{2,6},{3,1},{4,0},{5,7},{6,4},{7,3},{8,10},{9,13},{10,... | collective-permute-start | bytes 786440 | tf_op jit(solution)/shard_map/ppermute | solution.py:299
  2.9 10.8 %collective-permute-start.7 = (bf16[256,512]{1,0:T(8,128)(2,1)}, bf16[256,512]{1,0:T(8,128)(2,1)S(1)}, u32[]{:S(2)}, u32[]{:S(2)}) collective-permute-start(bf16[256,512]{1,0:T(8,128)(2,1)} %queries), channel_id=1, source_target_pairs={{0,4},{1,3},{2,0},{3,7},{4,6},{5,1},{6,2},{7,5},{8,12},{9,11},{10,... | collective-permute-start | bytes 786440 | tf_op jit(solution)/shard_map/ppermute | solution.py:299
  2.9 13.3 %collective-permute-start.2 = (bf16[256,512]{1,0:T(8,128)(2,1)}, bf16[256,512]{1,0:T(8,128)(2,1)S(1)}, u32[]{:S(2)}, u32[]{:S(2)}) collective-permute-start(bf16[256,512]{1,0:T(8,128)(2,1)} %queries), channel_id=1, source_target_pairs={{0,6},{1,17},{2,4},{3,19},{4,2},{5,21},{6,0},{7,23},{8,24},{9,15},... | collective-permute-start | bytes 786440 | tf_op jit(solution)/shard_map/ppermute | solution.py:299
  4.2 11.9 %collective-permute-start.3 = (bf16[256,512]{1,0:T(8,128)(2,1)}, bf16[256,512]{1,0:T(8,128)(2,1)S(1)}, u32[]{:S(2)}, u32[]{:S(2)}) collective-permute-start(bf16[256,512]{1,0:T(8,128)(2,1)} %queries), channel_id=1, source_target_pairs={{0,1},{1,6},{2,3},{3,4},{4,5},{5,2},{6,7},{7,0},{8,15},{9,8},{10,1... | collective-permute-start | bytes 786440 | tf_op jit(solution)/shard_map/ppermute | solution.py:299
  7.2 1.9 %copy-start.2 = (f32[512,1024]{1,0:T(8,128)S(1)}, f32[512,1024]{1,0:T(8,128)}, u32[]{:S(2)}) copy-start(f32[512,1024]{1,0:T(8,128)} %values.3) | copy-start | bytes 6291460
  8.6 1.3 %collective-permute-start.1 = (f32[64,256]{1,0:T(8,128)S(1)}, f32[64,256]{1,0:T(8,128)S(1)}, u32[]{:S(2)}, u32[]{:S(2)}) collective-permute-start(f32[64,256]{1,0:T(8,128)S(1)} %get-tuple-element.27.mine), channel_id=1, source_target_pairs={{0,1},{1,0},{2,3},{3,2},{4,5},{5,4},{6,7},{7,6},{8,9},{9,8},{10,11... | collective-permute-start | bytes 196616 | tf_op jit(solution)/shard_map/ppermute | solution.py:302
  10.8 1.2 %collective-permute-start.4 = (f32[1,512]{1,0:T(1,128)S(1)}, f32[1,512]{1,0:T(1,128)S(1)}, u32[]{:S(2)}, u32[]{:S(2)}) collective-permute-start(f32[1,512]{1,0:T(1,128)S(1)} %precondition.1.mine), channel_id=1, source_target_pairs={{0,1},{1,0},{2,3},{3,2},{4,5},{5,4},{6,7},{7,6},{8,9},{9,8},{10,11... | collective-permute-start | bytes 6152 | tf_op jit(solution)/shard_map/ppermute | solution.py:302
  12.0 4.1 %collective-permute-start.5 = (f32[1,1024]{1,0:T(1,128)S(1)}, f32[1,1024]{1,0:T(1,128)S(1)}, u32[]{:S(2)}, u32[]{:S(2)}) collective-permute-start(f32[1,1024]{1,0:T(1,128)S(1)} %both_halves.1.refs_0_), channel_id=1, source_target_pairs={{0,1},{1,9},{2,3},{3,11},{4,5},{5,13},{6,7},{7,15},{8,0},{9,8},{10... | collective-permute-start | bytes 12296 | tf_op jit(solution)/shard_map/ppermute | solution.py:299
  13.7 2.4 %collective-permute-start = (bf16[3,256,512]{2,1,0:T(8,128)(2,1)S(1)}, bf16[3,256,512]{2,1,0:T(8,128)(2,1)S(1)}, u32[]{:S(2)}, u32[]{:S(2)}) collective-permute-start(bf16[3,256,512]{2,1,0:T(8,128)(2,1)S(1)} %stack.1), channel_id=1, source_target_pairs={{0,1},{1,0},{2,3},{3,2},{4,5},{5,4},{6,7},{7,6},{8,9},{9,8},{10,11... | collective-permute-start | bytes 2359304 | tf_op jit(solution)/shard_map/cond/branch_1_fun/ppermute | solution.py:302
  16.2 3.8 %collective-permute-start.8 = (f32[1,1024]{1,0:T(1,128)S(1)}, f32[1,1024]{1,0:T(1,128)S(1)}, u32[]{:S(2)}, u32[]{:S(2)}) collective-permute-start(f32[1,1024]{1,0:T(1,128)S(1)} %get-tuple-element.35), channel_id=1, source_target_pairs={{0,8},{1,0},{2,10},{3,2},{4,12},{5,4},{6,14},{7,6},{8,9},{9,1},{10... | collective-permute-start | bytes 12296 | tf_op jit(solution)/shard_map/ppermute | solution.py:299

commit v7 on v6

--- a/solution.py
+++ b/solution.py
@@ -76,7 +76,7 @@
     rank = mine.shape[0] // 2
     for i in range(lanes.shape[0]):
         cut = slice(i * LANES, (i + 1) * LANES)
-        lanes[i] = mine[:rank, cut] + other[:rank, cut]
+        lanes[i, :rank] = mine[:rank, cut] + other[:rank, cut]
     fold = LANES // rank
     rows = jnp.concatenate(
         [
@@ -110,7 +110,7 @@
         out_shape=jax.ShapeDtypeStruct((rank * rank // LANES, LANES), jnp.float32),
         in_specs=[VMEM, VMEM],
         out_specs=VMEM,
-        scratch_shapes=[pltpu.VMEM((tokens // LANES, rank, LANES), jnp.float32)],
+        scratch_shapes=[pltpu.VMEM((tokens // LANES, rank + LANES // rank, LANES), jnp.float32)],
         compiler_params=pltpu.CompilerParams(vmem_limit_bytes=16 << 20),
         name="outer",
     )(mine, other)

time: 20.7 us -> 20.7 us (level)
  no operation moved by 1% of the time
where the time goes in v7:
time: 20.7 us; the launch traced here: 20.6 us
  starting transfers between devices  9.73 us (47%)
  waiting for transfers between devices  5.97 us (29%)
  Pallas kernels  4.04 us (20%)
  between operations  0.77 us (4%)
    ppermute x6, starting transfers between devices, send(): return lax.ppermute(values, axes, pairs)  8.85 us
    ppermute x3, waiting for transfers between devices, swap(): return lax.ppermute(values, 'tp', [(0, 1), (1, 0)])  3.7 us
    ppermute x6, waiting for transfers between devices, send(): return lax.ppermute(values, axes, pairs)  2.27 us
    pallas_call x8, Pallas kernels, small(): pl.pallas_call(kernel, out_shape=out_shape, in_specs=specs, out_specs=jax...  1.71 us
    pallas_call x1, Pallas kernels, project_in(): pl.pallas_call(in_kernel, out_shape=(jax.ShapeDtypeStruct((2 * rank, toke...  1.41 us
    ppermute x3, starting transfers between devices, swap(): return lax.ppermute(values, 'tp', [(0, 1), (1, 0)])  0.88 us
    pallas_call x1, Pallas kernels, project_out(): pl.pallas_call(out_kernel, out_shape=jax.ShapeDtypeStruct((out_factor.sha...  0.7 us
  transfers between devices with their start and end apart: 9, of which 4 were waited for; matrix products, arithmetic and copies ran while one was open for 0% of the time, Pallas kernels for 17%

profile of v7, /device:TPU:1, one launch (start us, length us, event | category | flops | bytes accessed | tf_op | source)
XLA Modules:
  0.0 20.6 jit_solution(9304984429685500356)
XLA Ops:
  0.6 0.0 copy-start.1
  0.6 0.0 copy-start.4
  0.6 0.0 copy-start
  0.7 0.0 copy-start.3
  0.7 2.2 %collective-permute-start.6 = (bf16[256,512]{1,0:T(8,128)(2,1)}, bf16[256,512]{1,0:T(8,128)(2,1)S(1)}, u32[]{:S(2)}, u32[]{:S(2)}) collective-permute-start(bf16[256,512]{1,0:T(8,128)(2,1)} %queries), channel_id=1, source_target_pairs={{0,2},{1,5},{2,6},{3,1},{4,0},{5,7},{6,4},{7,3},{8,10},{9,13},{10,... | collective-permute-start | bytes 786440 | tf_op jit(solution)/shard_map/ppermute | solution.py:299
  2.9 0.0 collective-permute-start.7
  2.9 1.4 %collective-permute-start.2 = (bf16[256,512]{1,0:T(8,128)(2,1)}, bf16[256,512]{1,0:T(8,128)(2,1)S(1)}, u32[]{:S(2)}, u32[]{:S(2)}) collective-permute-start(bf16[256,512]{1,0:T(8,128)(2,1)} %queries), channel_id=1, source_target_pairs={{0,6},{1,17},{2,4},{3,19},{4,2},{5,21},{6,0},{7,23},{8,24},{9,15},... | collective-permute-start | bytes 786440 | tf_op jit(solution)/shard_map/ppermute | solution.py:299
  4.2 2.2 %collective-permute-start.3 = (bf16[256,512]{1,0:T(8,128)(2,1)}, bf16[256,512]{1,0:T(8,128)(2,1)S(1)}, u32[]{:S(2)}, u32[]{:S(2)}) collective-permute-start(bf16[256,512]{1,0:T(8,128)(2,1)} %queries), channel_id=1, source_target_pairs={{0,1},{1,6},{2,3},{3,4},{4,5},{5,2},{6,7},{7,0},{8,15},{9,8},{10,1... | collective-permute-start | bytes 786440 | tf_op jit(solution)/shard_map/ppermute | solution.py:299
  6.4 0.0 copy-done.1
  6.4 0.0 copy-done.4
  6.4 0.7 %project_out.1.out_part = f32[32,256]{1,0:T(8,128)S(1)} custom-call(f32[8,128]{1,0:T(8,128)S(1)} %stage.1.token, bf16[256,4096]{1,0:T(8,128)(2,1)S(1)} %bitcast.5, bf16[32,4096]{1,0:T(8,128)(2,1)S(1)} %copy-done.4), custom_call_target="tpu_custom_call" | custom-call | flops 67108864 | bytes 2359296 | tf_op jit(solution)/shard_map/project_out/pallas_call | solution.py:39
  7.1 0.0 copy-done
  7.2 0.0 copy-done.3
  7.2 0.0 copy-start.2
  7.2 1.4 %project_in.1 = (f32[64,256]{1,0:T(8,128)S(1)}, bf16[256,512]{1,0:T(8,128)(2,1)S(1)}) custom-call(f32[32,256]{1,0:T(8,128)S(1)} %project_out.1.out_part, bf16[14784,256]{1,0:T(8,128)(2,1)S(1)} %bitcast.4, bf16[32,14784]{1,0:T(8,128)(2,1)S(1)} %copy-done.3, bf16[256,512]{1,0:T(8,128)(2,1)} %queries), custom_call_target="tpu_custom_call" | custom-call | flops 242221056 | bytes 8515584 | tf_op jit(solution)/shard_map/project_in/pallas_call | solution.py:56
  8.6 0.4 %collective-permute-start.1 = (f32[64,256]{1,0:T(8,128)S(1)}, f32[64,256]{1,0:T(8,128)S(1)}, u32[]{:S(2)}, u32[]{:S(2)}) collective-permute-start(f32[64,256]{1,0:T(8,128)S(1)} %get-tuple-element.27.mine), channel_id=1, source_target_pairs={{0,1},{1,0},{2,3},{3,2},{4,5},{5,4},{6,7},{7,6},{8,9},{9,8},{10,11... | collective-permute-start | bytes 196616 | tf_op jit(solution)/shard_map/ppermute | solution.py:302
  9.1 0.0 copy-done.2
  9.1 0.3 %prepare.1 = (bf16[512,1024]{1,0:T(8,128)(2,1)S(1)}, bf16[512,1024]{1,0:T(8,128)(2,1)S(1)}) custom-call(f32[512,1024]{1,0:T(8,128)S(1)} %copy-done.2), custom_call_target="tpu_custom_call" | custom-call | flops 1 | bytes 1 | tf_op jit(solution)/shard_map/prepare/pallas_call | solution.py:129
  9.4 0.6 %collective-permute-done.1.other = f32[64,256]{1,0:T(8,128)S(1)} collective-permute-done((f32[64,256]{1,0:T(8,128)S(1)}, f32[64,256]{1,0:T(8,128)S(1)}, u32[]{:S(2)}, u32[]{:S(2)}) %collective-permute-start.1) | collective-permute-done | bytes 65568 | tf_op jit(solution)/shard_map/ppermute | solution.py:302
  10.0 0.2 %outer.1.grad = f32[8,128]{1,0:T(8,128)S(1)} custom-call(f32[64,256]{1,0:T(8,128)S(1)} %get-tuple-element.27.mine, f32[64,256]{1,0:T(8,128)S(1)} %collective-permute-done.1.other), custom_call_target="tpu_custom_call" | custom-call | tf_op jit(solution)/shard_map/outer/pallas_call | solution.py:108
  10.2 0.7 %precondition.1.mine = f32[1,512]{1,0:T(1,128)S(1)} custom-call(f32[8,128]{1,0:T(8,128)S(1)} %outer.1.grad, bf16[512,1024]{1,0:T(8,128)(2,1)S(1)} %get-tuple-element.28.high, bf16[512,1024]{1,0:T(8,128)(2,1)S(1)} %get-tuple-element.29.low), custom_call_target="tpu_custom_call" | custom-call | flops 1 | bytes 1 | tf_op jit(solution)/shard_map/precondition/pallas_call | solution.py:129
  10.8 0.4 %collective-permute-start.4 = (f32[1,512]{1,0:T(1,128)S(1)}, f32[1,512]{1,0:T(1,128)S(1)}, u32[]{:S(2)}, u32[]{:S(2)}) collective-permute-start(f32[1,512]{1,0:T(1,128)S(1)} %precondition.1.mine), channel_id=1, source_target_pairs={{0,1},{1,0},{2,3},{3,2},{4,5},{5,4},{6,7},{7,6},{8,9},{9,8},{10,11... | collective-permute-start | bytes 6152 | tf_op jit(solution)/shard_map/ppermute | solution.py:302
  11.2 0.8 %collective-permute-done.4.other = f32[1,512]{1,0:T(1,128)S(1)} collective-permute-done((f32[1,512]{1,0:T(1,128)S(1)}, f32[1,512]{1,0:T(1,128)S(1)}, u32[]{:S(2)}, u32[]{:S(2)}) %collective-permute-start.4) | collective-permute-done | bytes 2080 | tf_op jit(solution)/shard_map/ppermute | solution.py:302
  12.0 1.6 %collective-permute-start.5 = (f32[1,1024]{1,0:T(1,128)S(1)}, f32[1,1024]{1,0:T(1,128)S(1)}, u32[]{:S(2)}, u32[]{:S(2)}) collective-permute-start(f32[1,1024]{1,0:T(1,128)S(1)} %both_halves.1.refs_0_), channel_id=1, source_target_pairs={{0,1},{1,9},{2,3},{3,11},{4,5},{5,13},{6,7},{7,15},{8,0},{9,8},{10... | collective-permute-start | bytes 12296 | tf_op jit(solution)/shard_map/ppermute | solution.py:299
  13.6 0.0 collective-permute-done.6.refs_3_
  13.6 0.0 collective-permute-done.7.refs_4_
  13.6 2.5 %conditional.1 = (bf16[3,256,512]{2,1,0:T(8,128)(2,1)S(1)}) conditional(s32[]{:T(128)} %convert_element_type.3, () %tuple.15, (bf16[256,512]{1,0:T(8,128)(2,1)S(1)}, bf16[256,512]{1,0:T(8,128)(2,1)S(1)}, bf16[256,512]{1,0:T(8,128)(2,1)S(1)}) %tuple.16), branch_computations={%region_0.0_spmd, %region_1.0_spmd} | conditional | flops 2 | bytes 3145778 | solution.py:322
  13.6 0.1 stack.1
  13.7 0.1 collective-permute-start
  13.8 2.3 %collective-permute-done.values = bf16[3,256,512]{2,1,0:T(8,128)(2,1)S(1)} collective-permute-done((bf16[3,256,512]{2,1,0:T(8,128)(2,1)S(1)}, bf16[3,256,512]{2,1,0:T(8,128)(2,1)S(1)}, u32[]{:S(2)}, u32[]{:S(2)}) %collective-permute-start) | collective-permute-done | bytes 786464 | tf_op jit(solution)/shard_map/cond/branch_1_fun/ppermute | solution.py:302
  16.0 0.1 keep.1
  16.1 0.0 collective-permute-done.5.refs_1_
  16.1 0.0 collective-permute-done.2.refs_0_
  16.1 0.0 collective-permute-done.3.refs_1_
  16.2 1.5 %collective-permute-start.8 = (f32[1,1024]{1,0:T(1,128)S(1)}, f32[1,1024]{1,0:T(1,128)S(1)}, u32[]{:S(2)}, u32[]{:S(2)}) collective-permute-start(f32[1,1024]{1,0:T(1,128)S(1)} %get-tuple-element.35), channel_id=1, source_target_pairs={{0,8},{1,0},{2,10},{3,2},{4,12},{5,4},{6,14},{7,6},{8,9},{9,1},{10... | collective-permute-start | bytes 12296 | tf_op jit(solution)/shard_map/ppermute | solution.py:299
  17.7 2.3 %collective-permute-done.8.returned = f32[1,1024]{1,0:T(1,128)S(1)} collective-permute-done((f32[1,1024]{1,0:T(1,128)S(1)}, f32[1,1024]{1,0:T(1,128)S(1)}, u32[]{:S(2)}, u32[]{:S(2)}) %collective-permute-start.8) | collective-permute-done | bytes 4128 | tf_op jit(solution)/shard_map/ppermute | solution.py:299
  19.9 0.6 %finish.1 = (f32[1,512]{1,0:T(1,128)}, f32[1,1024]{1,0:T(1,128)}) custom-call(f32[8,128]{1,0:T(8,128)S(1)} %outer.1.grad, f32[1,1024]{1,0:T(1,128)S(1)} %get-tuple-element.34.near, f32[1,1024]{1,0:T(1,128)S(1)} %collective-permute-done.8.returned), custom_call_target="tpu_custom_call" | custom-call | flops 1 | bytes 1 | tf_op jit(solution)/shard_map/finish/pallas_call | solution.py:129
  (4 shorter events, 0.1 us)
Async XLA Ops:
  0.6 5.8 %copy-start.1 = (bf16[1,256,4096]{2,1,0:T(8,128)(2,1)S(1)}, bf16[1,256,4096]{2,1,0:T(8,128)(2,1)}, u32[]{:S(2)}) copy-start(bf16[1,256,4096]{2,1,0:T(8,128)(2,1)} %param.9) | copy-start | bytes 6291460
  0.6 5.8 %copy-start.4 = (bf16[32,4096]{1,0:T(8,128)(2,1)S(1)}, bf16[32,4096]{1,0:T(8,128)(2,1)}, u32[]{:S(2)}) copy-start(bf16[32,4096]{1,0:T(8,128)(2,1)} %out_f.1) | copy-start | bytes 786436
  0.6 6.5 %copy-start = (bf16[1,256,14784]{1,2,0:T(8,128)(2,1)S(1)}, bf16[1,256,14784]{1,2,0:T(8,128)(2,1)}, u32[]{:S(2)}) copy-start(bf16[1,256,14784]{1,2,0:T(8,128)(2,1)} %param.8) | copy-start | bytes 22708228
  0.7 6.5 %copy-start.3 = (bf16[32,14784]{1,0:T(8,128)(2,1)S(1)}, bf16[32,14784]{1,0:T(8,128)(2,1)}, u32[]{:S(2)}) copy-start(bf16[32,14784]{1,0:T(8,128)(2,1)} %in_f.1) | copy-start | bytes 2838532
  0.7 12.9 %collective-permute-start.6 = (bf16[256,512]{1,0:T(8,128)(2,1)}, bf16[256,512]{1,0:T(8,128)(2,1)S(1)}, u32[]{:S(2)}, u32[]{:S(2)}) collective-permute-start(bf16[256,512]{1,0:T(8,128)(2,1)} %queries), channel_id=1, source_target_pairs={{0,2},{1,5},{2,6},{3,1},{4,0},{5,7},{6,4},{7,3},{8,10},{9,13},{10,... | collective-permute-start | bytes 786440 | tf_op jit(solution)/shard_map/ppermute | solution.py:299
  2.9 10.8 %collective-permute-start.7 = (bf16[256,512]{1,0:T(8,128)(2,1)}, bf16[256,512]{1,0:T(8,128)(2,1)S(1)}, u32[]{:S(2)}, u32[]{:S(2)}) collective-permute-start(bf16[256,512]{1,0:T(8,128)(2,1)} %queries), channel_id=1, source_target_pairs={{0,4},{1,3},{2,0},{3,7},{4,6},{5,1},{6,2},{7,5},{8,12},{9,11},{10,... | collective-permute-start | bytes 786440 | tf_op jit(solution)/shard_map/ppermute | solution.py:299
  2.9 13.3 %collective-permute-start.2 = (bf16[256,512]{1,0:T(8,128)(2,1)}, bf16[256,512]{1,0:T(8,128)(2,1)S(1)}, u32[]{:S(2)}, u32[]{:S(2)}) collective-permute-start(bf16[256,512]{1,0:T(8,128)(2,1)} %queries), channel_id=1, source_target_pairs={{0,6},{1,17},{2,4},{3,19},{4,2},{5,21},{6,0},{7,23},{8,24},{9,15},... | collective-permute-start | bytes 786440 | tf_op jit(solution)/shard_map/ppermute | solution.py:299
  4.2 11.9 %collective-permute-start.3 = (bf16[256,512]{1,0:T(8,128)(2,1)}, bf16[256,512]{1,0:T(8,128)(2,1)S(1)}, u32[]{:S(2)}, u32[]{:S(2)}) collective-permute-start(bf16[256,512]{1,0:T(8,128)(2,1)} %queries), channel_id=1, source_target_pairs={{0,1},{1,6},{2,3},{3,4},{4,5},{5,2},{6,7},{7,0},{8,15},{9,8},{10,1... | collective-permute-start | bytes 786440 | tf_op jit(solution)/shard_map/ppermute | solution.py:299
  7.2 1.9 %copy-start.2 = (f32[512,1024]{1,0:T(8,128)S(1)}, f32[512,1024]{1,0:T(8,128)}, u32[]{:S(2)}) copy-start(f32[512,1024]{1,0:T(8,128)} %values.3) | copy-start | bytes 6291460
  8.6 1.3 %collective-permute-start.1 = (f32[64,256]{1,0:T(8,128)S(1)}, f32[64,256]{1,0:T(8,128)S(1)}, u32[]{:S(2)}, u32[]{:S(2)}) collective-permute-start(f32[64,256]{1,0:T(8,128)S(1)} %get-tuple-element.27.mine), channel_id=1, source_target_pairs={{0,1},{1,0},{2,3},{3,2},{4,5},{5,4},{6,7},{7,6},{8,9},{9,8},{10,11... | collective-permute-start | bytes 196616 | tf_op jit(solution)/shard_map/ppermute | solution.py:302
  10.8 1.2 %collective-permute-start.4 = (f32[1,512]{1,0:T(1,128)S(1)}, f32[1,512]{1,0:T(1,128)S(1)}, u32[]{:S(2)}, u32[]{:S(2)}) collective-permute-start(f32[1,512]{1,0:T(1,128)S(1)} %precondition.1.mine), channel_id=1, source_target_pairs={{0,1},{1,0},{2,3},{3,2},{4,5},{5,4},{6,7},{7,6},{8,9},{9,8},{10,11... | collective-permute-start | bytes 6152 | tf_op jit(solution)/shard_map/ppermute | solution.py:302
  12.0 4.1 %collective-permute-start.5 = (f32[1,1024]{1,0:T(1,128)S(1)}, f32[1,1024]{1,0:T(1,128)S(1)}, u32[]{:S(2)}, u32[]{:S(2)}) collective-permute-start(f32[1,1024]{1,0:T(1,128)S(1)} %both_halves.1.refs_0_), channel_id=1, source_target_pairs={{0,1},{1,9},{2,3},{3,11},{4,5},{5,13},{6,7},{7,15},{8,0},{9,8},{10... | collective-permute-start | bytes 12296 | tf_op jit(solution)/shard_map/ppermute | solution.py:299
  13.7 2.4 %collective-permute-start = (bf16[3,256,512]{2,1,0:T(8,128)(2,1)S(1)}, bf16[3,256,512]{2,1,0:T(8,128)(2,1)S(1)}, u32[]{:S(2)}, u32[]{:S(2)}) collective-permute-start(bf16[3,256,512]{2,1,0:T(8,128)(2,1)S(1)} %stack.1), channel_id=1, source_target_pairs={{0,1},{1,0},{2,3},{3,2},{4,5},{5,4},{6,7},{7,6},{8,9},{9,8},{10,11... | collective-permute-start | bytes 2359304 | tf_op jit(solution)/shard_map/cond/branch_1_fun/ppermute | solution.py:302
  16.2 3.8 %collective-permute-start.8 = (f32[1,1024]{1,0:T(1,128)S(1)}, f32[1,1024]{1,0:T(1,128)S(1)}, u32[]{:S(2)}, u32[]{:S(2)}) collective-permute-start(f32[1,1024]{1,0:T(1,128)S(1)} %get-tuple-element.35), channel_id=1, source_target_pairs={{0,8},{1,0},{2,10},{3,2},{4,12},{5,4},{6,14},{7,6},{8,9},{9,1},{10... | collective-permute-start | bytes 12296 | tf_op jit(solution)/shard_map/ppermute | solution.py:299

commit v8 on v7

--- a/solution.py
+++ b/solution.py
@@ -23,7 +23,11 @@
 
 
 def out_kernel(token, grads, out_f, result):
-    result[...] = lax.dot_general(out_f[...], grads[...], NT, preferred_element_type=jnp.float32)
+    for cut in range(0, grads.shape[0], LANES):
+        columns = slice(cut, cut + LANES)
+        result[:, columns] = lax.dot_general(
+            out_f[...], grads[columns], NT, preferred_element_type=jnp.float32
+        )
 
 
 def in_kernel(out_part, acts, in_f, queries, result, own, sem):
@@ -31,7 +35,11 @@
     copy.start()
     rank = in_f.shape[0]
     result[:rank] = out_part[...]
-    result[rank:] = jnp.dot(in_f[...], acts[...], preferred_element_type=jnp.float32)
+    for cut in range(0, acts.shape[1], LANES):
+        columns = slice(cut, cut + LANES)
+        result[rank:, columns] = jnp.dot(
+            in_f[...], acts[:, columns], preferred_element_type=jnp.float32
+        )
     copy.wait()
 
 

time: 20.7 us -> 20.7 us (level)
    pallas_call x1, Pallas kernels: 1.41 us -> 1.16 us  [project_in(): pl.pallas_call(in_kernel, out_shape=(jax.ShapeDtypeStruct((2 * rank, toke...]
  transfers between devices with their start and end apart: 9 -> 9, of which waited for: 4 -> 4; matrix products, arithmetic and copies ran while one was open for 0% -> 0% of each run, Pallas kernels for 17% -> 16%
where the time goes in v8:
time: 20.7 us; the launch traced here: 20.6 us
  starting transfers between devices  9.83 us (47%)
  waiting for transfers between devices  5.99 us (29%)
  Pallas kernels  3.86 us (19%)
  between operations  0.76 us (4%)
    ppermute x6, starting transfers between devices, send(): return lax.ppermute(values, axes, pairs)  8.96 us
    ppermute x3, waiting for transfers between devices, swap(): return lax.ppermute(values, 'tp', [(0, 1), (1, 0)])  3.64 us
    ppermute x6, waiting for transfers between devices, send(): return lax.ppermute(values, axes, pairs)  2.35 us
    pallas_call x8, Pallas kernels, small(): pl.pallas_call(kernel, out_shape=out_shape, in_specs=specs, out_specs=jax...  1.71 us
    pallas_call x1, Pallas kernels, project_in(): pl.pallas_call(in_kernel, out_shape=(jax.ShapeDtypeStruct((2 * rank, toke...  1.16 us
    ppermute x3, starting transfers between devices, swap(): return lax.ppermute(values, 'tp', [(0, 1), (1, 0)])  0.88 us
    pallas_call x1, Pallas kernels, project_out(): pl.pallas_call(out_kernel, out_shape=jax.ShapeDtypeStruct((out_factor.sha...  0.79 us
  transfers between devices with their start and end apart: 9, of which 4 were waited for; matrix products, arithmetic and copies ran while one was open for 0% of the time, Pallas kernels for 16%

profile of v8, /device:TPU:1, one launch (start us, length us, event | category | flops | bytes accessed | tf_op | source)
XLA Modules:
  0.0 20.6 jit_solution(3039805458689633564)
XLA Ops:
  0.6 0.0 copy-start.1
  0.6 0.0 copy-start.4
  0.6 0.0 copy-start
  0.7 0.0 copy-start.3
  0.7 2.2 %collective-permute-start.6 = (bf16[256,512]{1,0:T(8,128)(2,1)}, bf16[256,512]{1,0:T(8,128)(2,1)S(1)}, u32[]{:S(2)}, u32[]{:S(2)}) collective-permute-start(bf16[256,512]{1,0:T(8,128)(2,1)} %queries), channel_id=1, source_target_pairs={{0,2},{1,5},{2,6},{3,1},{4,0},{5,7},{6,4},{7,3},{8,10},{9,13},{10,... | collective-permute-start | bytes 786440 | tf_op jit(solution)/shard_map/ppermute | solution.py:307
  2.9 0.0 collective-permute-start.7
  2.9 1.4 %collective-permute-start.2 = (bf16[256,512]{1,0:T(8,128)(2,1)}, bf16[256,512]{1,0:T(8,128)(2,1)S(1)}, u32[]{:S(2)}, u32[]{:S(2)}) collective-permute-start(bf16[256,512]{1,0:T(8,128)(2,1)} %queries), channel_id=1, source_target_pairs={{0,6},{1,17},{2,4},{3,19},{4,2},{5,21},{6,0},{7,23},{8,24},{9,15},... | collective-permute-start | bytes 786440 | tf_op jit(solution)/shard_map/ppermute | solution.py:307
  4.2 2.2 %collective-permute-start.3 = (bf16[256,512]{1,0:T(8,128)(2,1)}, bf16[256,512]{1,0:T(8,128)(2,1)S(1)}, u32[]{:S(2)}, u32[]{:S(2)}) collective-permute-start(bf16[256,512]{1,0:T(8,128)(2,1)} %queries), channel_id=1, source_target_pairs={{0,1},{1,6},{2,3},{3,4},{4,5},{5,2},{6,7},{7,0},{8,15},{9,8},{10,1... | collective-permute-start | bytes 786440 | tf_op jit(solution)/shard_map/ppermute | solution.py:307
  6.4 0.0 copy-done.1
  6.4 0.0 copy-done.4
  6.4 0.8 %project_out.1.out_part = f32[32,256]{1,0:T(8,128)S(1)} custom-call(f32[8,128]{1,0:T(8,128)S(1)} %stage.1.token, bf16[256,4096]{1,0:T(8,128)(2,1)S(1)} %bitcast.5, bf16[32,4096]{1,0:T(8,128)(2,1)S(1)} %copy-done.4), custom_call_target="tpu_custom_call" | custom-call | flops 67108864 | bytes 2359296 | tf_op jit(solution)/shard_map/project_out/pallas_call | solution.py:47
  7.2 0.0 copy-done
  7.2 0.0 copy-done.3
  7.3 0.0 copy-start.2
  7.3 1.2 %project_in.1 = (f32[64,256]{1,0:T(8,128)S(1)}, bf16[256,512]{1,0:T(8,128)(2,1)S(1)}) custom-call(f32[32,256]{1,0:T(8,128)S(1)} %project_out.1.out_part, bf16[14784,256]{1,0:T(8,128)(2,1)S(1)} %bitcast.4, bf16[32,14784]{1,0:T(8,128)(2,1)S(1)} %copy-done.3, bf16[256,512]{1,0:T(8,128)(2,1)} %queries), custom_call_target="tpu_custom_call" | custom-call | flops 242221056 | bytes 8515584 | tf_op jit(solution)/shard_map/project_in/pallas_call | solution.py:64
  8.4 0.4 %collective-permute-start.1 = (f32[64,256]{1,0:T(8,128)S(1)}, f32[64,256]{1,0:T(8,128)S(1)}, u32[]{:S(2)}, u32[]{:S(2)}) collective-permute-start(f32[64,256]{1,0:T(8,128)S(1)} %get-tuple-element.27.mine), channel_id=1, source_target_pairs={{0,1},{1,0},{2,3},{3,2},{4,5},{5,4},{6,7},{7,6},{8,9},{9,8},{10,11... | collective-permute-start | bytes 196616 | tf_op jit(solution)/shard_map/ppermute | solution.py:310
  8.9 0.1 copy-done.2
  8.9 0.3 %prepare.1 = (bf16[512,1024]{1,0:T(8,128)(2,1)S(1)}, bf16[512,1024]{1,0:T(8,128)(2,1)S(1)}) custom-call(f32[512,1024]{1,0:T(8,128)S(1)} %copy-done.2), custom_call_target="tpu_custom_call" | custom-call | flops 1 | bytes 1 | tf_op jit(solution)/shard_map/prepare/pallas_call | solution.py:137
  9.2 0.5 %collective-permute-done.1.other = f32[64,256]{1,0:T(8,128)S(1)} collective-permute-done((f32[64,256]{1,0:T(8,128)S(1)}, f32[64,256]{1,0:T(8,128)S(1)}, u32[]{:S(2)}, u32[]{:S(2)}) %collective-permute-start.1) | collective-permute-done | bytes 65568 | tf_op jit(solution)/shard_map/ppermute | solution.py:310
  9.8 0.2 %outer.1.grad = f32[8,128]{1,0:T(8,128)S(1)} custom-call(f32[64,256]{1,0:T(8,128)S(1)} %get-tuple-element.27.mine, f32[64,256]{1,0:T(8,128)S(1)} %collective-permute-done.1.other), custom_call_target="tpu_custom_call" | custom-call | tf_op jit(solution)/shard_map/outer/pallas_call | solution.py:116
  10.0 0.7 %precondition.1.mine = f32[1,512]{1,0:T(1,128)S(1)} custom-call(f32[8,128]{1,0:T(8,128)S(1)} %outer.1.grad, bf16[512,1024]{1,0:T(8,128)(2,1)S(1)} %get-tuple-element.28.high, bf16[512,1024]{1,0:T(8,128)(2,1)S(1)} %get-tuple-element.29.low), custom_call_target="tpu_custom_call" | custom-call | flops 1 | bytes 1 | tf_op jit(solution)/shard_map/precondition/pallas_call | solution.py:137
  10.6 0.4 %collective-permute-start.4 = (f32[1,512]{1,0:T(1,128)S(1)}, f32[1,512]{1,0:T(1,128)S(1)}, u32[]{:S(2)}, u32[]{:S(2)}) collective-permute-start(f32[1,512]{1,0:T(1,128)S(1)} %precondition.1.mine), channel_id=1, source_target_pairs={{0,1},{1,0},{2,3},{3,2},{4,5},{5,4},{6,7},{7,6},{8,9},{9,8},{10,11... | collective-permute-start | bytes 6152 | tf_op jit(solution)/shard_map/ppermute | solution.py:310
  11.0 0.8 %collective-permute-done.4.other = f32[1,512]{1,0:T(1,128)S(1)} collective-permute-done((f32[1,512]{1,0:T(1,128)S(1)}, f32[1,512]{1,0:T(1,128)S(1)}, u32[]{:S(2)}, u32[]{:S(2)}) %collective-permute-start.4) | collective-permute-done | bytes 2080 | tf_op jit(solution)/shard_map/ppermute | solution.py:310
  11.8 1.6 %collective-permute-start.5 = (f32[1,1024]{1,0:T(1,128)S(1)}, f32[1,1024]{1,0:T(1,128)S(1)}, u32[]{:S(2)}, u32[]{:S(2)}) collective-permute-start(f32[1,1024]{1,0:T(1,128)S(1)} %both_halves.1.refs_0_), channel_id=1, source_target_pairs={{0,1},{1,9},{2,3},{3,11},{4,5},{5,13},{6,7},{7,15},{8,0},{9,8},{10... | collective-permute-start | bytes 12296 | tf_op jit(solution)/shard_map/ppermute | solution.py:307
  13.4 0.0 collective-permute-done.6.refs_3_
  13.4 0.0 collective-permute-done.7.refs_4_
  13.4 2.5 %conditional.1 = (bf16[3,256,512]{2,1,0:T(8,128)(2,1)S(1)}) conditional(s32[]{:T(128)} %convert_element_type.3, () %tuple.15, (bf16[256,512]{1,0:T(8,128)(2,1)S(1)}, bf16[256,512]{1,0:T(8,128)(2,1)S(1)}, bf16[256,512]{1,0:T(8,128)(2,1)S(1)}) %tuple.16), branch_computations={%region_0.0_spmd, %region_1.0_spmd} | conditional | flops 2 | bytes 3145778 | solution.py:330
  13.4 0.1 stack.1
  13.5 0.1 collective-permute-start
  13.6 2.3 %collective-permute-done.values = bf16[3,256,512]{2,1,0:T(8,128)(2,1)S(1)} collective-permute-done((bf16[3,256,512]{2,1,0:T(8,128)(2,1)S(1)}, bf16[3,256,512]{2,1,0:T(8,128)(2,1)S(1)}, u32[]{:S(2)}, u32[]{:S(2)}) %collective-permute-start) | collective-permute-done | bytes 786464 | tf_op jit(solution)/shard_map/cond/branch_1_fun/ppermute | solution.py:310
  15.8 0.1 keep.1
  15.9 0.0 collective-permute-done.5.refs_1_
  15.9 0.0 collective-permute-done.2.refs_0_
  16.0 0.0 collective-permute-done.3.refs_1_
  16.0 1.6 %collective-permute-start.8 = (f32[1,1024]{1,0:T(1,128)S(1)}, f32[1,1024]{1,0:T(1,128)S(1)}, u32[]{:S(2)}, u32[]{:S(2)}) collective-permute-start(f32[1,1024]{1,0:T(1,128)S(1)} %get-tuple-element.35), channel_id=1, source_target_pairs={{0,8},{1,0},{2,10},{3,2},{4,12},{5,4},{6,14},{7,6},{8,9},{9,1},{10... | collective-permute-start | bytes 12296 | tf_op jit(solution)/shard_map/ppermute | solution.py:307
  17.6 2.3 %collective-permute-done.8.returned = f32[1,1024]{1,0:T(1,128)S(1)} collective-permute-done((f32[1,1024]{1,0:T(1,128)S(1)}, f32[1,1024]{1,0:T(1,128)S(1)}, u32[]{:S(2)}, u32[]{:S(2)}) %collective-permute-start.8) | collective-permute-done | bytes 4128 | tf_op jit(solution)/shard_map/ppermute | solution.py:307
  19.9 0.6 %finish.1 = (f32[1,512]{1,0:T(1,128)}, f32[1,1024]{1,0:T(1,128)}) custom-call(f32[8,128]{1,0:T(8,128)S(1)} %outer.1.grad, f32[1,1024]{1,0:T(1,128)S(1)} %get-tuple-element.34.near, f32[1,1024]{1,0:T(1,128)S(1)} %collective-permute-done.8.returned), custom_call_target="tpu_custom_call" | custom-call | flops 1 | bytes 1 | tf_op jit(solution)/shard_map/finish/pallas_call | solution.py:137
  (4 shorter events, 0.1 us)
Async XLA Ops:
  0.6 5.8 %copy-start.1 = (bf16[1,256,4096]{2,1,0:T(8,128)(2,1)S(1)}, bf16[1,256,4096]{2,1,0:T(8,128)(2,1)}, u32[]{:S(2)}) copy-start(bf16[1,256,4096]{2,1,0:T(8,128)(2,1)} %param.9) | copy-start | bytes 6291460
  0.6 5.8 %copy-start.4 = (bf16[32,4096]{1,0:T(8,128)(2,1)S(1)}, bf16[32,4096]{1,0:T(8,128)(2,1)}, u32[]{:S(2)}) copy-start(bf16[32,4096]{1,0:T(8,128)(2,1)} %out_f.1) | copy-start | bytes 786436
  0.6 6.6 %copy-start = (bf16[1,256,14784]{1,2,0:T(8,128)(2,1)S(1)}, bf16[1,256,14784]{1,2,0:T(8,128)(2,1)}, u32[]{:S(2)}) copy-start(bf16[1,256,14784]{1,2,0:T(8,128)(2,1)} %param.8) | copy-start | bytes 22708228
  0.7 6.6 %copy-start.3 = (bf16[32,14784]{1,0:T(8,128)(2,1)S(1)}, bf16[32,14784]{1,0:T(8,128)(2,1)}, u32[]{:S(2)}) copy-start(bf16[32,14784]{1,0:T(8,128)(2,1)} %in_f.1) | copy-start | bytes 2838532
  0.7 12.8 %collective-permute-start.6 = (bf16[256,512]{1,0:T(8,128)(2,1)}, bf16[256,512]{1,0:T(8,128)(2,1)S(1)}, u32[]{:S(2)}, u32[]{:S(2)}) collective-permute-start(bf16[256,512]{1,0:T(8,128)(2,1)} %queries), channel_id=1, source_target_pairs={{0,2},{1,5},{2,6},{3,1},{4,0},{5,7},{6,4},{7,3},{8,10},{9,13},{10,... | collective-permute-start | bytes 786440 | tf_op jit(solution)/shard_map/ppermute | solution.py:307
  2.9 10.6 %collective-permute-start.7 = (bf16[256,512]{1,0:T(8,128)(2,1)}, bf16[256,512]{1,0:T(8,128)(2,1)S(1)}, u32[]{:S(2)}, u32[]{:S(2)}) collective-permute-start(bf16[256,512]{1,0:T(8,128)(2,1)} %queries), channel_id=1, source_target_pairs={{0,4},{1,3},{2,0},{3,7},{4,6},{5,1},{6,2},{7,5},{8,12},{9,11},{10,... | collective-permute-start | bytes 786440 | tf_op jit(solution)/shard_map/ppermute | solution.py:307
  2.9 13.1 %collective-permute-start.2 = (bf16[256,512]{1,0:T(8,128)(2,1)}, bf16[256,512]{1,0:T(8,128)(2,1)S(1)}, u32[]{:S(2)}, u32[]{:S(2)}) collective-permute-start(bf16[256,512]{1,0:T(8,128)(2,1)} %queries), channel_id=1, source_target_pairs={{0,6},{1,17},{2,4},{3,19},{4,2},{5,21},{6,0},{7,23},{8,24},{9,15},... | collective-permute-start | bytes 786440 | tf_op jit(solution)/shard_map/ppermute | solution.py:307
  4.2 11.7 %collective-permute-start.3 = (bf16[256,512]{1,0:T(8,128)(2,1)}, bf16[256,512]{1,0:T(8,128)(2,1)S(1)}, u32[]{:S(2)}, u32[]{:S(2)}) collective-permute-start(bf16[256,512]{1,0:T(8,128)(2,1)} %queries), channel_id=1, source_target_pairs={{0,1},{1,6},{2,3},{3,4},{4,5},{5,2},{6,7},{7,0},{8,15},{9,8},{10,1... | collective-permute-start | bytes 786440 | tf_op jit(solution)/shard_map/ppermute | solution.py:307
  7.3 1.7 %copy-start.2 = (f32[512,1024]{1,0:T(8,128)S(1)}, f32[512,1024]{1,0:T(8,128)}, u32[]{:S(2)}) copy-start(f32[512,1024]{1,0:T(8,128)} %values.3) | copy-start | bytes 6291460
  8.4 1.3 %collective-permute-start.1 = (f32[64,256]{1,0:T(8,128)S(1)}, f32[64,256]{1,0:T(8,128)S(1)}, u32[]{:S(2)}, u32[]{:S(2)}) collective-permute-start(f32[64,256]{1,0:T(8,128)S(1)} %get-tuple-element.27.mine), channel_id=1, source_target_pairs={{0,1},{1,0},{2,3},{3,2},{4,5},{5,4},{6,7},{7,6},{8,9},{9,8},{10,11... | collective-permute-start | bytes 196616 | tf_op jit(solution)/shard_map/ppermute | solution.py:310
  10.6 1.2 %collective-permute-start.4 = (f32[1,512]{1,0:T(1,128)S(1)}, f32[1,512]{1,0:T(1,128)S(1)}, u32[]{:S(2)}, u32[]{:S(2)}) collective-permute-start(f32[1,512]{1,0:T(1,128)S(1)} %precondition.1.mine), channel_id=1, source_target_pairs={{0,1},{1,0},{2,3},{3,2},{4,5},{5,4},{6,7},{7,6},{8,9},{9,8},{10,11... | collective-permute-start | bytes 6152 | tf_op jit(solution)/shard_map/ppermute | solution.py:310
  11.8 4.1 %collective-permute-start.5 = (f32[1,1024]{1,0:T(1,128)S(1)}, f32[1,1024]{1,0:T(1,128)S(1)}, u32[]{:S(2)}, u32[]{:S(2)}) collective-permute-start(f32[1,1024]{1,0:T(1,128)S(1)} %both_halves.1.refs_0_), channel_id=1, source_target_pairs={{0,1},{1,9},{2,3},{3,11},{4,5},{5,13},{6,7},{7,15},{8,0},{9,8},{10... | collective-permute-start | bytes 12296 | tf_op jit(solution)/shard_map/ppermute | solution.py:307
  13.5 2.4 %collective-permute-start = (bf16[3,256,512]{2,1,0:T(8,128)(2,1)S(1)}, bf16[3,256,512]{2,1,0:T(8,128)(2,1)S(1)}, u32[]{:S(2)}, u32[]{:S(2)}) collective-permute-start(bf16[3,256,512]{2,1,0:T(8,128)(2,1)S(1)} %stack.1), channel_id=1, source_target_pairs={{0,1},{1,0},{2,3},{3,2},{4,5},{5,4},{6,7},{7,6},{8,9},{9,8},{10,11... | collective-permute-start | bytes 2359304 | tf_op jit(solution)/shard_map/cond/branch_1_fun/ppermute | solution.py:310
  16.0 3.9 %collective-permute-start.8 = (f32[1,1024]{1,0:T(1,128)S(1)}, f32[1,1024]{1,0:T(1,128)S(1)}, u32[]{:S(2)}, u32[]{:S(2)}) collective-permute-start(f32[1,1024]{1,0:T(1,128)S(1)} %get-tuple-element.35), channel_id=1, source_target_pairs={{0,8},{1,0},{2,10},{3,2},{4,12},{5,4},{6,14},{7,6},{8,9},{9,1},{10... | collective-permute-start | bytes 12296 | tf_op jit(solution)/shard_map/ppermute | solution.py:307

commit v9 on v7

--- a/solution.py
+++ b/solution.py
@@ -195,28 +195,22 @@
     return small("both_halves", halves_kernel, shape, (mine, other))
 
 
-def score_kernel(half, ways, last, *refs):
-    rows, refs = ((), refs) if last else (refs[:2], refs[2:])
-    mine, others, refs = refs[: len(ways)], refs[len(ways)], refs[len(ways) + 1 :]
-    before, (near, far, *lefts) = (refs[:3], refs[3:]) if last else ((), refs)
+def score_kernel(half, ways, *refs):
+    rows, mine, others = refs[:2], refs[2 : 2 + len(ways)], refs[2 + len(ways)]
+    near, far, mine_left, other_left = refs[3 + len(ways) :]
 
     @pl.when(serves(half))
     def _():
-        if last:
-            near[...] = before[0][...]
-            far[...] = before[1][...]
-            left = before[2][...]
-        else:
-            values = jnp.concatenate([ref[...] for ref in rows], axis=0)
-            left = jnp.concatenate(split(values, 3), axis=0)
-            lefts[0][...] = left
+        values = jnp.concatenate([ref[...] for ref in rows], axis=0)
+        left = jnp.concatenate(split(values, 3), axis=0)
         place = lax.axis_index("ex") % half
         second = lax.axis_index("tp") == 1
         feats = left.shape[1] // 2
         halves = [left[:, :feats], left[:, feats:]]
         halves = [jnp.where(second, halves[1 - i], halves[i]) for i in range(2)]
+        mine_left[...], other_left[...] = halves
         for i, (first_way, second_way) in enumerate(ways):
-            other = others[ways.index((second_way, first_way))] if len(others.shape) > 2 else others[...]
+            other = others[ways.index((second_way, first_way))]
             sums = lax.dot_general(
                 halves[0], mine[i][...], NT, preferred_element_type=jnp.float32
             ) + lax.dot_general(halves[1], other, NT, preferred_element_type=jnp.float32)
@@ -229,20 +223,46 @@
             far[:, at] = total[1:2]
 
 
-def score(half, ways, rows, mine, others, before=()):
+def score(half, ways, rows, mine, others):
     row = jax.ShapeDtypeStruct((1, half * mine[0].shape[0]), jnp.float32)
-    shapes = (row, row)
-    if not before:
-        shapes += (jax.ShapeDtypeStruct((3 * len(rows), rows[0].shape[1]), jnp.bfloat16),)
+    left = jax.ShapeDtypeStruct((3 * len(rows), rows[0].shape[1] // 2), jnp.bfloat16)
     return small(
         "score",
-        functools.partial(score_kernel, half, tuple(ways), bool(before)),
-        shapes,
-        (*rows, *mine, others, *before),
-    )
-
-
-def finish_kernel(half, grad, near, returned, share, result):
+        functools.partial(score_kernel, half, tuple(ways)),
+        (row, row, left, left),
+        (*rows, *mine, others),
+    )
+
+
+def last_kernel(half, mine, other, block, other_block, far_before, far, near_end):
+    @pl.when(serves(half))
+    def _():
+        far[...] = far_before[...]
+        sums = lax.dot_general(
+            mine[...], block[...], NT, preferred_element_type=jnp.float32
+        ) + lax.dot_general(other[...], other_block[...], NT, preferred_element_type=jnp.float32)
+        total = sums[0:2] + sums[2:4] + sums[4:6]
+        far[:, last_block(half, total.shape[1])] = total[1:2]
+        near_end[...] = total[0:1]
+
+
+def last_block(half, width):
+    place = (lax.axis_index("ex") % half) ^ (half - 1)
+    return pl.ds(pl.multiple_of(place * width, width), width)
+
+
+def score_last(half, far, lefts, blocks):
+    end = jax.ShapeDtypeStruct((1, blocks[0].shape[0]), jnp.float32)
+    return small(
+        "score_last",
+        functools.partial(last_kernel, half),
+        (jax.ShapeDtypeStruct(far.shape, jnp.float32), end),
+        (*lefts, *blocks, far),
+    )
+
+
+def finish_kernel(half, grad, near, returned, *refs):
+    near_end, (share, result) = refs[:-2], refs[-2:]
     rows = grad.shape[0] // 2
     half_grad = jnp.where(lax.axis_index("tp") == 0, grad[:rows], grad[rows:])
     for k in range(rows):
@@ -251,19 +271,21 @@
     @pl.when(serves(half))
     def _():
         result[...] = near[...]
+        if near_end:
+            result[:, last_block(half, near_end[0].shape[1])] = near_end[0][...]
 
     @pl.when(jnp.logical_not(serves(half)))
     def _():
         result[...] = returned[...]
 
 
-def finish(half, grad, near, returned):
+def finish(half, grad, near, returned, near_end):
     shapes = (
         jax.ShapeDtypeStruct((1, grad.size // 2), jnp.float32),
         jax.ShapeDtypeStruct(near.shape, near.dtype),
     )
     return small(
-        "finish", functools.partial(finish_kernel, half), shapes, (grad, near, returned)
+        "finish", functools.partial(finish_kernel, half), shapes, (grad, near, returned, *near_end)
     )
 
 
@@ -333,13 +355,12 @@
     blocks = [own, *early]
     far_row = send(precond, lambda g, e, t, on: (g, e, 1 - t) if on else (g, e ^ half, t))
     others = whole(lambda *values: keep(swap(stack(values))), *blocks)
-    scores = score(half, [(0, 0), *ways], (precond, far_row), blocks, others)
+    near, far_scores, *lefts = score(half, [(0, 0), *ways], (precond, far_row), blocks, others)
+    near_end = []
     if last:
-        way = half - 1
-        scores = score(half, [(way, way)], (), last[:1], last[1], scores)
-    near, far = scores[:2]
-    returned = send(far, lambda g, e, t, on: (g, e ^ half, t) if on else (g, e, 1 - t))
-    return finish(half, grad, near, returned)
+        far_scores, *near_end = score_last(half, far_scores, lefts, last)
+    returned = send(far_scores, lambda g, e, t, on: (g, e ^ half, t) if on else (g, e, 1 - t))
+    return finish(half, grad, near, returned, near_end)
 
 
 def solution(mesh):

time: 20.7 us -> 20.7 us (level)
  no operation moved by 1% of the time
where the time goes in v9:
time: 20.7 us; the launch traced here: 20.6 us
  starting transfers between devices  9.73 us (47%)
  waiting for transfers between devices  5.97 us (29%)
  Pallas kernels  4.04 us (20%)
  between operations  0.77 us (4%)
    ppermute x6, starting transfers between devices, send(): return lax.ppermute(values, axes, pairs)  8.85 us
    ppermute x3, waiting for transfers between devices, swap(): return lax.ppermute(values, 'tp', [(0, 1), (1, 0)])  3.7 us
    ppermute x6, waiting for transfers between devices, send(): return lax.ppermute(values, axes, pairs)  2.27 us
    pallas_call x8, Pallas kernels, small(): pl.pallas_call(kernel, out_shape=out_shape, in_specs=specs, out_specs=jax...  1.71 us
    pallas_call x1, Pallas kernels, project_in(): pl.pallas_call(in_kernel, out_shape=(jax.ShapeDtypeStruct((2 * rank, toke...  1.41 us
    ppermute x3, starting transfers between devices, swap(): return lax.ppermute(values, 'tp', [(0, 1), (1, 0)])  0.88 us
    pallas_call x1, Pallas kernels, project_out(): pl.pallas_call(out_kernel, out_shape=jax.ShapeDtypeStruct((out_factor.sha...  0.7 us
  transfers between devices with their start and end apart: 9, of which 4 were waited for; matrix products, arithmetic and copies ran while one was open for 0% of the time, Pallas kernels for 17%

profile of v9, /device:TPU:1, one launch (start us, length us, event | category | flops | bytes accessed | tf_op | source)
XLA Modules:
  0.0 20.6 jit_solution(4287482222062919299)
XLA Ops:
  0.6 0.0 copy-start.1
  0.6 0.0 copy-start.4
  0.6 0.0 copy-start
  0.7 0.0 copy-start.3
  0.7 2.2 %collective-permute-start.4 = (bf16[256,512]{1,0:T(8,128)(2,1)}, bf16[256,512]{1,0:T(8,128)(2,1)S(1)}, u32[]{:S(2)}, u32[]{:S(2)}) collective-permute-start(bf16[256,512]{1,0:T(8,128)(2,1)} %queries), channel_id=1, source_target_pairs={{0,2},{1,5},{2,6},{3,1},{4,0},{5,7},{6,4},{7,3},{8,10},{9,13},{10,... | collective-permute-start | bytes 786440 | tf_op jit(solution)/shard_map/ppermute | solution.py:321
  2.9 0.0 collective-permute-start.5
  2.9 1.4 %collective-permute-start.6 = (bf16[256,512]{1,0:T(8,128)(2,1)}, bf16[256,512]{1,0:T(8,128)(2,1)S(1)}, u32[]{:S(2)}, u32[]{:S(2)}) collective-permute-start(bf16[256,512]{1,0:T(8,128)(2,1)} %queries), channel_id=1, source_target_pairs={{0,6},{1,17},{2,4},{3,19},{4,2},{5,21},{6,0},{7,23},{8,24},{9,15},... | collective-permute-start | bytes 786440 | tf_op jit(solution)/shard_map/ppermute | solution.py:321
  4.2 2.2 %collective-permute-start.7 = (bf16[256,512]{1,0:T(8,128)(2,1)}, bf16[256,512]{1,0:T(8,128)(2,1)S(1)}, u32[]{:S(2)}, u32[]{:S(2)}) collective-permute-start(bf16[256,512]{1,0:T(8,128)(2,1)} %queries), channel_id=1, source_target_pairs={{0,1},{1,6},{2,3},{3,4},{4,5},{5,2},{6,7},{7,0},{8,15},{9,8},{10,1... | collective-permute-start | bytes 786440 | tf_op jit(solution)/shard_map/ppermute | solution.py:321
  6.4 0.0 copy-done.1
  6.4 0.0 copy-done.4
  6.4 0.7 %project_out.1.out_part = f32[32,256]{1,0:T(8,128)S(1)} custom-call(f32[8,128]{1,0:T(8,128)S(1)} %stage.1.token, bf16[256,4096]{1,0:T(8,128)(2,1)S(1)} %bitcast.5, bf16[32,4096]{1,0:T(8,128)(2,1)S(1)} %copy-done.4), custom_call_target="tpu_custom_call" | custom-call | flops 67108864 | bytes 2359296 | tf_op jit(solution)/shard_map/project_out/pallas_call | solution.py:39
  7.1 0.0 copy-done
  7.2 0.0 copy-done.3
  7.2 0.0 copy-start.2
  7.2 1.4 %project_in.1 = (f32[64,256]{1,0:T(8,128)S(1)}, bf16[256,512]{1,0:T(8,128)(2,1)S(1)}) custom-call(f32[32,256]{1,0:T(8,128)S(1)} %project_out.1.out_part, bf16[14784,256]{1,0:T(8,128)(2,1)S(1)} %bitcast.4, bf16[32,14784]{1,0:T(8,128)(2,1)S(1)} %copy-done.3, bf16[256,512]{1,0:T(8,128)(2,1)} %queries), custom_call_target="tpu_custom_call" | custom-call | flops 242221056 | bytes 8515584 | tf_op jit(solution)/shard_map/project_in/pallas_call | solution.py:56
  8.6 0.4 %collective-permute-start.1 = (f32[64,256]{1,0:T(8,128)S(1)}, f32[64,256]{1,0:T(8,128)S(1)}, u32[]{:S(2)}, u32[]{:S(2)}) collective-permute-start(f32[64,256]{1,0:T(8,128)S(1)} %get-tuple-element.28.mine), channel_id=1, source_target_pairs={{0,1},{1,0},{2,3},{3,2},{4,5},{5,4},{6,7},{7,6},{8,9},{9,8},{10,11... | collective-permute-start | bytes 196616 | tf_op jit(solution)/shard_map/ppermute | solution.py:324
  9.1 0.0 copy-done.2
  9.1 0.3 %prepare.1 = (bf16[512,1024]{1,0:T(8,128)(2,1)S(1)}, bf16[512,1024]{1,0:T(8,128)(2,1)S(1)}) custom-call(f32[512,1024]{1,0:T(8,128)S(1)} %copy-done.2), custom_call_target="tpu_custom_call" | custom-call | flops 1 | bytes 1 | tf_op jit(solution)/shard_map/prepare/pallas_call | solution.py:129
  9.4 0.6 %collective-permute-done.1.other = f32[64,256]{1,0:T(8,128)S(1)} collective-permute-done((f32[64,256]{1,0:T(8,128)S(1)}, f32[64,256]{1,0:T(8,128)S(1)}, u32[]{:S(2)}, u32[]{:S(2)}) %collective-permute-start.1) | collective-permute-done | bytes 65568 | tf_op jit(solution)/shard_map/ppermute | solution.py:324
  10.0 0.2 %outer.1.grad = f32[8,128]{1,0:T(8,128)S(1)} custom-call(f32[64,256]{1,0:T(8,128)S(1)} %get-tuple-element.28.mine, f32[64,256]{1,0:T(8,128)S(1)} %collective-permute-done.1.other), custom_call_target="tpu_custom_call" | custom-call | tf_op jit(solution)/shard_map/outer/pallas_call | solution.py:108
  10.2 0.7 %precondition.1.mine = f32[1,512]{1,0:T(1,128)S(1)} custom-call(f32[8,128]{1,0:T(8,128)S(1)} %outer.1.grad, bf16[512,1024]{1,0:T(8,128)(2,1)S(1)} %get-tuple-element.29.high, bf16[512,1024]{1,0:T(8,128)(2,1)S(1)} %get-tuple-element.30.low), custom_call_target="tpu_custom_call" | custom-call | flops 1 | bytes 1 | tf_op jit(solution)/shard_map/precondition/pallas_call | solution.py:129
  10.8 0.4 %collective-permute-start.2 = (f32[1,512]{1,0:T(1,128)S(1)}, f32[1,512]{1,0:T(1,128)S(1)}, u32[]{:S(2)}, u32[]{:S(2)}) collective-permute-start(f32[1,512]{1,0:T(1,128)S(1)} %precondition.1.mine), channel_id=1, source_target_pairs={{0,1},{1,0},{2,3},{3,2},{4,5},{5,4},{6,7},{7,6},{8,9},{9,8},{10,11... | collective-permute-start | bytes 6152 | tf_op jit(solution)/shard_map/ppermute | solution.py:324
  11.2 0.8 %collective-permute-done.2.other = f32[1,512]{1,0:T(1,128)S(1)} collective-permute-done((f32[1,512]{1,0:T(1,128)S(1)}, f32[1,512]{1,0:T(1,128)S(1)}, u32[]{:S(2)}, u32[]{:S(2)}) %collective-permute-start.2) | collective-permute-done | bytes 2080 | tf_op jit(solution)/shard_map/ppermute | solution.py:324
  12.0 1.6 %collective-permute-start.3 = (f32[1,1024]{1,0:T(1,128)S(1)}, f32[1,1024]{1,0:T(1,128)S(1)}, u32[]{:S(2)}, u32[]{:S(2)}) collective-permute-start(f32[1,1024]{1,0:T(1,128)S(1)} %both_halves.1.refs_0_), channel_id=1, source_target_pairs={{0,1},{1,9},{2,3},{3,11},{4,5},{5,13},{6,7},{7,15},{8,0},{9,8},{10... | collective-permute-start | bytes 12296 | tf_op jit(solution)/shard_map/ppermute | solution.py:321
  13.6 0.0 collective-permute-done.4.refs_3_
  13.6 0.0 collective-permute-done.5.refs_4_
  13.6 2.5 %conditional.1 = (bf16[3,256,512]{2,1,0:T(8,128)(2,1)S(1)}) conditional(s32[]{:T(128)} %convert_element_type.3, () %tuple.15, (bf16[256,512]{1,0:T(8,128)(2,1)S(1)}, bf16[256,512]{1,0:T(8,128)(2,1)S(1)}, bf16[256,512]{1,0:T(8,128)(2,1)S(1)}) %tuple.16), branch_computations={%region_0.0_spmd, %region_1.0_spmd} | conditional | flops 2 | bytes 3145778 | solution.py:344
  13.6 0.1 stack.1
  13.7 0.1 collective-permute-start
  13.8 2.3 %collective-permute-done.values = bf16[3,256,512]{2,1,0:T(8,128)(2,1)S(1)} collective-permute-done((bf16[3,256,512]{2,1,0:T(8,128)(2,1)S(1)}, bf16[3,256,512]{2,1,0:T(8,128)(2,1)S(1)}, u32[]{:S(2)}, u32[]{:S(2)}) %collective-permute-start) | collective-permute-done | bytes 786464 | tf_op jit(solution)/shard_map/cond/branch_1_fun/ppermute | solution.py:324
  16.0 0.1 keep.1
  16.1 0.0 collective-permute-done.3.refs_1_
  16.1 0.0 collective-permute-done.6.block
  16.1 0.0 collective-permute-done.7.other_block
  16.2 1.5 %collective-permute-start.8 = (f32[1,1024]{1,0:T(1,128)S(1)}, f32[1,1024]{1,0:T(1,128)S(1)}, u32[]{:S(2)}, u32[]{:S(2)}) collective-permute-start(f32[1,1024]{1,0:T(1,128)S(1)} %get-tuple-element.36), channel_id=1, source_target_pairs={{0,8},{1,0},{2,10},{3,2},{4,12},{5,4},{6,14},{7,6},{8,9},{9,1},{10... | collective-permute-start | bytes 12296 | tf_op jit(solution)/shard_map/ppermute | solution.py:321
  17.7 2.3 %collective-permute-done.8.returned = f32[1,1024]{1,0:T(1,128)S(1)} collective-permute-done((f32[1,1024]{1,0:T(1,128)S(1)}, f32[1,1024]{1,0:T(1,128)S(1)}, u32[]{:S(2)}, u32[]{:S(2)}) %collective-permute-start.8) | collective-permute-done | bytes 4128 | tf_op jit(solution)/shard_map/ppermute | solution.py:321
  19.9 0.6 %finish.1 = (f32[1,512]{1,0:T(1,128)}, f32[1,1024]{1,0:T(1,128)}) custom-call(f32[8,128]{1,0:T(8,128)S(1)} %outer.1.grad, f32[1,1024]{1,0:T(1,128)S(1)} %get-tuple-element.32.near, f32[1,1024]{1,0:T(1,128)S(1)} %collective-permute-done.8.returned, f32[1,256]{1,0:T(1,128)S(1)} %get-tuple-element.37.refs_0_), custom_call_target="tpu_custom_call" | custom-call | flops 1 | bytes 1 | tf_op jit(solution)/shard_map/finish/pallas_call | solution.py:129
  (4 shorter events, 0.1 us)
Async XLA Ops:
  0.6 5.8 %copy-start.1 = (bf16[1,256,4096]{2,1,0:T(8,128)(2,1)S(1)}, bf16[1,256,4096]{2,1,0:T(8,128)(2,1)}, u32[]{:S(2)}) copy-start(bf16[1,256,4096]{2,1,0:T(8,128)(2,1)} %param.9) | copy-start | bytes 6291460
  0.6 5.8 %copy-start.4 = (bf16[32,4096]{1,0:T(8,128)(2,1)S(1)}, bf16[32,4096]{1,0:T(8,128)(2,1)}, u32[]{:S(2)}) copy-start(bf16[32,4096]{1,0:T(8,128)(2,1)} %out_f.1) | copy-start | bytes 786436
  0.6 6.5 %copy-start = (bf16[1,256,14784]{1,2,0:T(8,128)(2,1)S(1)}, bf16[1,256,14784]{1,2,0:T(8,128)(2,1)}, u32[]{:S(2)}) copy-start(bf16[1,256,14784]{1,2,0:T(8,128)(2,1)} %param.8) | copy-start | bytes 22708228
  0.7 6.5 %copy-start.3 = (bf16[32,14784]{1,0:T(8,128)(2,1)S(1)}, bf16[32,14784]{1,0:T(8,128)(2,1)}, u32[]{:S(2)}) copy-start(bf16[32,14784]{1,0:T(8,128)(2,1)} %in_f.1) | copy-start | bytes 2838532
  0.7 12.9 %collective-permute-start.4 = (bf16[256,512]{1,0:T(8,128)(2,1)}, bf16[256,512]{1,0:T(8,128)(2,1)S(1)}, u32[]{:S(2)}, u32[]{:S(2)}) collective-permute-start(bf16[256,512]{1,0:T(8,128)(2,1)} %queries), channel_id=1, source_target_pairs={{0,2},{1,5},{2,6},{3,1},{4,0},{5,7},{6,4},{7,3},{8,10},{9,13},{10,... | collective-permute-start | bytes 786440 | tf_op jit(solution)/shard_map/ppermute | solution.py:321
  2.9 10.8 %collective-permute-start.5 = (bf16[256,512]{1,0:T(8,128)(2,1)}, bf16[256,512]{1,0:T(8,128)(2,1)S(1)}, u32[]{:S(2)}, u32[]{:S(2)}) collective-permute-start(bf16[256,512]{1,0:T(8,128)(2,1)} %queries), channel_id=1, source_target_pairs={{0,4},{1,3},{2,0},{3,7},{4,6},{5,1},{6,2},{7,5},{8,12},{9,11},{10,... | collective-permute-start | bytes 786440 | tf_op jit(solution)/shard_map/ppermute | solution.py:321
  2.9 13.3 %collective-permute-start.6 = (bf16[256,512]{1,0:T(8,128)(2,1)}, bf16[256,512]{1,0:T(8,128)(2,1)S(1)}, u32[]{:S(2)}, u32[]{:S(2)}) collective-permute-start(bf16[256,512]{1,0:T(8,128)(2,1)} %queries), channel_id=1, source_target_pairs={{0,6},{1,17},{2,4},{3,19},{4,2},{5,21},{6,0},{7,23},{8,24},{9,15},... | collective-permute-start | bytes 786440 | tf_op jit(solution)/shard_map/ppermute | solution.py:321
  4.2 11.9 %collective-permute-start.7 = (bf16[256,512]{1,0:T(8,128)(2,1)}, bf16[256,512]{1,0:T(8,128)(2,1)S(1)}, u32[]{:S(2)}, u32[]{:S(2)}) collective-permute-start(bf16[256,512]{1,0:T(8,128)(2,1)} %queries), channel_id=1, source_target_pairs={{0,1},{1,6},{2,3},{3,4},{4,5},{5,2},{6,7},{7,0},{8,15},{9,8},{10,1... | collective-permute-start | bytes 786440 | tf_op jit(solution)/shard_map/ppermute | solution.py:321
  7.2 1.9 %copy-start.2 = (f32[512,1024]{1,0:T(8,128)S(1)}, f32[512,1024]{1,0:T(8,128)}, u32[]{:S(2)}) copy-start(f32[512,1024]{1,0:T(8,128)} %values.3) | copy-start | bytes 6291460
  8.6 1.3 %collective-permute-start.1 = (f32[64,256]{1,0:T(8,128)S(1)}, f32[64,256]{1,0:T(8,128)S(1)}, u32[]{:S(2)}, u32[]{:S(2)}) collective-permute-start(f32[64,256]{1,0:T(8,128)S(1)} %get-tuple-element.28.mine), channel_id=1, source_target_pairs={{0,1},{1,0},{2,3},{3,2},{4,5},{5,4},{6,7},{7,6},{8,9},{9,8},{10,11... | collective-permute-start | bytes 196616 | tf_op jit(solution)/shard_map/ppermute | solution.py:324
  10.8 1.2 %collective-permute-start.2 = (f32[1,512]{1,0:T(1,128)S(1)}, f32[1,512]{1,0:T(1,128)S(1)}, u32[]{:S(2)}, u32[]{:S(2)}) collective-permute-start(f32[1,512]{1,0:T(1,128)S(1)} %precondition.1.mine), channel_id=1, source_target_pairs={{0,1},{1,0},{2,3},{3,2},{4,5},{5,4},{6,7},{7,6},{8,9},{9,8},{10,11... | collective-permute-start | bytes 6152 | tf_op jit(solution)/shard_map/ppermute | solution.py:324
  12.0 4.1 %collective-permute-start.3 = (f32[1,1024]{1,0:T(1,128)S(1)}, f32[1,1024]{1,0:T(1,128)S(1)}, u32[]{:S(2)}, u32[]{:S(2)}) collective-permute-start(f32[1,1024]{1,0:T(1,128)S(1)} %both_halves.1.refs_0_), channel_id=1, source_target_pairs={{0,1},{1,9},{2,3},{3,11},{4,5},{5,13},{6,7},{7,15},{8,0},{9,8},{10... | collective-permute-start | bytes 12296 | tf_op jit(solution)/shard_map/ppermute | solution.py:321
  13.7 2.4 %collective-permute-start = (bf16[3,256,512]{2,1,0:T(8,128)(2,1)S(1)}, bf16[3,256,512]{2,1,0:T(8,128)(2,1)S(1)}, u32[]{:S(2)}, u32[]{:S(2)}) collective-permute-start(bf16[3,256,512]{2,1,0:T(8,128)(2,1)S(1)} %stack.1), channel_id=1, source_target_pairs={{0,1},{1,0},{2,3},{3,2},{4,5},{5,4},{6,7},{7,6},{8,9},{9,8},{10,11... | collective-permute-start | bytes 2359304 | tf_op jit(solution)/shard_map/cond/branch_1_fun/ppermute | solution.py:324
  16.2 3.8 %collective-permute-start.8 = (f32[1,1024]{1,0:T(1,128)S(1)}, f32[1,1024]{1,0:T(1,128)S(1)}, u32[]{:S(2)}, u32[]{:S(2)}) collective-permute-start(f32[1,1024]{1,0:T(1,128)S(1)} %get-tuple-element.36), channel_id=1, source_target_pairs={{0,8},{1,0},{2,10},{3,2},{4,12},{5,4},{6,14},{7,6},{8,9},{9,1},{10... | collective-permute-start | bytes 12296 | tf_op jit(solution)/shard_map/ppermute | solution.py:321

commit v10 on v7

--- a/solution.py
+++ b/solution.py
@@ -242,29 +242,35 @@
     )
 
 
-def finish_kernel(half, grad, near, returned, share, result):
+def finish_kernel(half, grad, near, returned, share, result, row, sems):
+    on = serves(half)
+    kept = pltpu.make_async_copy(near, result, sems.at[0])
+    got = pltpu.make_async_copy(returned, result, sems.at[0])
+    pl.when(on)(kept.start)
+    pl.when(jnp.logical_not(on))(got.start)
     rows = grad.shape[0] // 2
     half_grad = jnp.where(lax.axis_index("tp") == 0, grad[:rows], grad[rows:])
     for k in range(rows):
-        share[:, k * LANES : (k + 1) * LANES] = half_grad[k : k + 1]
-
-    @pl.when(serves(half))
-    def _():
-        result[...] = near[...]
-
-    @pl.when(jnp.logical_not(serves(half)))
-    def _():
-        result[...] = returned[...]
+        row[:, k * LANES : (k + 1) * LANES] = half_grad[k : k + 1]
+    written = pltpu.make_async_copy(row, share, sems.at[1])
+    written.start()
+    written.wait()
+    pl.when(on)(kept.wait)
+    pl.when(jnp.logical_not(on))(got.wait)
 
 
 def finish(half, grad, near, returned):
-    shapes = (
-        jax.ShapeDtypeStruct((1, grad.size // 2), jnp.float32),
-        jax.ShapeDtypeStruct(near.shape, near.dtype),
-    )
-    return small(
-        "finish", functools.partial(finish_kernel, half), shapes, (grad, near, returned)
-    )
+    share = jax.ShapeDtypeStruct((1, grad.size // 2), jnp.float32)
+    return pl.pallas_call(
+        functools.partial(finish_kernel, half),
+        out_shape=(share, jax.ShapeDtypeStruct(near.shape, near.dtype)),
+        in_specs=[VMEM] * 3,
+        out_specs=(ANY, ANY),
+        scratch_shapes=[pltpu.VMEM(share.shape, share.dtype), pltpu.SemaphoreType.DMA((2,))],
+        compiler_params=pltpu.CompilerParams(vmem_limit_bytes=16 << 20),
+        cost_estimate=pl.CostEstimate(flops=1, bytes_accessed=1, transcendentals=0),
+        name="finish",
+    )(grad, near, returned)
 
 
 def stage_kernel(values, result):

time: 20.7 us -> 20.7 us (level)
    pallas_call x0 -> x1, Pallas kernels: none -> 0.62 us  [finish(): pl.pallas_call(functools.partial(finish_kernel, half), out_shape=(share,...]
    pallas_call x8 -> x7, Pallas kernels: 1.71 us -> 1.1 us  [small(): pl.pallas_call(kernel, out_shape=out_shape, in_specs=specs, out_specs=jax...]
where the time goes in v10:
time: 20.7 us; the launch traced here: 20.6 us
  starting transfers between devices  9.73 us (47%)
  waiting for transfers between devices  5.97 us (29%)
  Pallas kernels  4.05 us (20%)
  between operations  0.77 us (4%)
    ppermute x6, starting transfers between devices, send(): return lax.ppermute(values, axes, pairs)  8.85 us
    ppermute x3, waiting for transfers between devices, swap(): return lax.ppermute(values, 'tp', [(0, 1), (1, 0)])  3.7 us
    ppermute x6, waiting for transfers between devices, send(): return lax.ppermute(values, axes, pairs)  2.27 us
    pallas_call x1, Pallas kernels, project_in(): pl.pallas_call(in_kernel, out_shape=(jax.ShapeDtypeStruct((2 * rank, toke...  1.41 us
    pallas_call x7, Pallas kernels, small(): pl.pallas_call(kernel, out_shape=out_shape, in_specs=specs, out_specs=jax...  1.1 us
    ppermute x3, starting transfers between devices, swap(): return lax.ppermute(values, 'tp', [(0, 1), (1, 0)])  0.88 us
    pallas_call x1, Pallas kernels, project_out(): pl.pallas_call(out_kernel, out_shape=jax.ShapeDtypeStruct((out_factor.sha...  0.7 us
    pallas_call x1, Pallas kernels, finish(): pl.pallas_call(functools.partial(finish_kernel, half), out_shape=(share,...  0.62 us
  transfers between devices with their start and end apart: 9, of which 4 were waited for; matrix products, arithmetic and copies ran while one was open for 0% of the time, Pallas kernels for 17%

profile of v10, /device:TPU:1, one launch (start us, length us, event | category | flops | bytes accessed | tf_op | source)
XLA Modules:
  0.0 20.6 jit_solution(11113281777281065597)
XLA Ops:
  0.6 0.0 copy-start.1
  0.6 0.0 copy-start.4
  0.6 0.0 copy-start
  0.7 0.0 copy-start.3
  0.7 2.2 %collective-permute-start.6 = (bf16[256,512]{1,0:T(8,128)(2,1)}, bf16[256,512]{1,0:T(8,128)(2,1)S(1)}, u32[]{:S(2)}, u32[]{:S(2)}) collective-permute-start(bf16[256,512]{1,0:T(8,128)(2,1)} %queries), channel_id=1, source_target_pairs={{0,2},{1,5},{2,6},{3,1},{4,0},{5,7},{6,4},{7,3},{8,10},{9,13},{10,... | collective-permute-start | bytes 786440 | tf_op jit(solution)/shard_map/ppermute | solution.py:305
  2.9 0.0 collective-permute-start.7
  2.9 1.4 %collective-permute-start.2 = (bf16[256,512]{1,0:T(8,128)(2,1)}, bf16[256,512]{1,0:T(8,128)(2,1)S(1)}, u32[]{:S(2)}, u32[]{:S(2)}) collective-permute-start(bf16[256,512]{1,0:T(8,128)(2,1)} %queries), channel_id=1, source_target_pairs={{0,6},{1,17},{2,4},{3,19},{4,2},{5,21},{6,0},{7,23},{8,24},{9,15},... | collective-permute-start | bytes 786440 | tf_op jit(solution)/shard_map/ppermute | solution.py:305
  4.2 2.2 %collective-permute-start.3 = (bf16[256,512]{1,0:T(8,128)(2,1)}, bf16[256,512]{1,0:T(8,128)(2,1)S(1)}, u32[]{:S(2)}, u32[]{:S(2)}) collective-permute-start(bf16[256,512]{1,0:T(8,128)(2,1)} %queries), channel_id=1, source_target_pairs={{0,1},{1,6},{2,3},{3,4},{4,5},{5,2},{6,7},{7,0},{8,15},{9,8},{10,1... | collective-permute-start | bytes 786440 | tf_op jit(solution)/shard_map/ppermute | solution.py:305
  6.4 0.0 copy-done.1
  6.4 0.0 copy-done.4
  6.4 0.7 %project_out.1.out_part = f32[32,256]{1,0:T(8,128)S(1)} custom-call(f32[8,128]{1,0:T(8,128)S(1)} %stage.1.token, bf16[256,4096]{1,0:T(8,128)(2,1)S(1)} %bitcast.5, bf16[32,4096]{1,0:T(8,128)(2,1)S(1)} %copy-done.4), custom_call_target="tpu_custom_call" | custom-call | flops 67108864 | bytes 2359296 | tf_op jit(solution)/shard_map/project_out/pallas_call | solution.py:39
  7.1 0.0 copy-done
  7.2 0.0 copy-done.3
  7.2 0.0 copy-start.2
  7.2 1.4 %project_in.1 = (f32[64,256]{1,0:T(8,128)S(1)}, bf16[256,512]{1,0:T(8,128)(2,1)S(1)}) custom-call(f32[32,256]{1,0:T(8,128)S(1)} %project_out.1.out_part, bf16[14784,256]{1,0:T(8,128)(2,1)S(1)} %bitcast.4, bf16[32,14784]{1,0:T(8,128)(2,1)S(1)} %copy-done.3, bf16[256,512]{1,0:T(8,128)(2,1)} %queries), custom_call_target="tpu_custom_call" | custom-call | flops 242221056 | bytes 8515584 | tf_op jit(solution)/shard_map/project_in/pallas_call | solution.py:56
  8.6 0.4 %collective-permute-start.1 = (f32[64,256]{1,0:T(8,128)S(1)}, f32[64,256]{1,0:T(8,128)S(1)}, u32[]{:S(2)}, u32[]{:S(2)}) collective-permute-start(f32[64,256]{1,0:T(8,128)S(1)} %get-tuple-element.27.mine), channel_id=1, source_target_pairs={{0,1},{1,0},{2,3},{3,2},{4,5},{5,4},{6,7},{7,6},{8,9},{9,8},{10,11... | collective-permute-start | bytes 196616 | tf_op jit(solution)/shard_map/ppermute | solution.py:308
  9.1 0.0 copy-done.2
  9.1 0.3 %prepare.1 = (bf16[512,1024]{1,0:T(8,128)(2,1)S(1)}, bf16[512,1024]{1,0:T(8,128)(2,1)S(1)}) custom-call(f32[512,1024]{1,0:T(8,128)S(1)} %copy-done.2), custom_call_target="tpu_custom_call" | custom-call | flops 1 | bytes 1 | tf_op jit(solution)/shard_map/prepare/pallas_call | solution.py:129
  9.4 0.6 %collective-permute-done.1.other = f32[64,256]{1,0:T(8,128)S(1)} collective-permute-done((f32[64,256]{1,0:T(8,128)S(1)}, f32[64,256]{1,0:T(8,128)S(1)}, u32[]{:S(2)}, u32[]{:S(2)}) %collective-permute-start.1) | collective-permute-done | bytes 65568 | tf_op jit(solution)/shard_map/ppermute | solution.py:308
  10.0 0.2 %outer.1.grad = f32[8,128]{1,0:T(8,128)S(1)} custom-call(f32[64,256]{1,0:T(8,128)S(1)} %get-tuple-element.27.mine, f32[64,256]{1,0:T(8,128)S(1)} %collective-permute-done.1.other), custom_call_target="tpu_custom_call" | custom-call | tf_op jit(solution)/shard_map/outer/pallas_call | solution.py:108
  10.2 0.7 %precondition.1.mine = f32[1,512]{1,0:T(1,128)S(1)} custom-call(f32[8,128]{1,0:T(8,128)S(1)} %outer.1.grad, bf16[512,1024]{1,0:T(8,128)(2,1)S(1)} %get-tuple-element.28.high, bf16[512,1024]{1,0:T(8,128)(2,1)S(1)} %get-tuple-element.29.low), custom_call_target="tpu_custom_call" | custom-call | flops 1 | bytes 1 | tf_op jit(solution)/shard_map/precondition/pallas_call | solution.py:129
  10.8 0.4 %collective-permute-start.4 = (f32[1,512]{1,0:T(1,128)S(1)}, f32[1,512]{1,0:T(1,128)S(1)}, u32[]{:S(2)}, u32[]{:S(2)}) collective-permute-start(f32[1,512]{1,0:T(1,128)S(1)} %precondition.1.mine), channel_id=1, source_target_pairs={{0,1},{1,0},{2,3},{3,2},{4,5},{5,4},{6,7},{7,6},{8,9},{9,8},{10,11... | collective-permute-start | bytes 6152 | tf_op jit(solution)/shard_map/ppermute | solution.py:308
  11.2 0.8 %collective-permute-done.4.other = f32[1,512]{1,0:T(1,128)S(1)} collective-permute-done((f32[1,512]{1,0:T(1,128)S(1)}, f32[1,512]{1,0:T(1,128)S(1)}, u32[]{:S(2)}, u32[]{:S(2)}) %collective-permute-start.4) | collective-permute-done | bytes 2080 | tf_op jit(solution)/shard_map/ppermute | solution.py:308
  12.0 1.6 %collective-permute-start.5 = (f32[1,1024]{1,0:T(1,128)S(1)}, f32[1,1024]{1,0:T(1,128)S(1)}, u32[]{:S(2)}, u32[]{:S(2)}) collective-permute-start(f32[1,1024]{1,0:T(1,128)S(1)} %both_halves.1.refs_0_), channel_id=1, source_target_pairs={{0,1},{1,9},{2,3},{3,11},{4,5},{5,13},{6,7},{7,15},{8,0},{9,8},{10... | collective-permute-start | bytes 12296 | tf_op jit(solution)/shard_map/ppermute | solution.py:305
  13.6 0.0 collective-permute-done.6.refs_3_
  13.6 0.0 collective-permute-done.7.refs_4_
  13.6 2.5 %conditional.1 = (bf16[3,256,512]{2,1,0:T(8,128)(2,1)S(1)}) conditional(s32[]{:T(128)} %convert_element_type.3, () %tuple.15, (bf16[256,512]{1,0:T(8,128)(2,1)S(1)}, bf16[256,512]{1,0:T(8,128)(2,1)S(1)}, bf16[256,512]{1,0:T(8,128)(2,1)S(1)}) %tuple.16), branch_computations={%region_0.0_spmd, %region_1.0_spmd} | conditional | flops 2 | bytes 3145778 | solution.py:328
  13.6 0.1 stack.1
  13.7 0.1 collective-permute-start
  13.8 2.3 %collective-permute-done.values = bf16[3,256,512]{2,1,0:T(8,128)(2,1)S(1)} collective-permute-done((bf16[3,256,512]{2,1,0:T(8,128)(2,1)S(1)}, bf16[3,256,512]{2,1,0:T(8,128)(2,1)S(1)}, u32[]{:S(2)}, u32[]{:S(2)}) %collective-permute-start) | collective-permute-done | bytes 786464 | tf_op jit(solution)/shard_map/cond/branch_1_fun/ppermute | solution.py:308
  16.0 0.1 keep.1
  16.1 0.0 collective-permute-done.5.refs_1_
  16.1 0.0 collective-permute-done.2.refs_0_
  16.1 0.0 collective-permute-done.3.refs_1_
  16.2 1.5 %collective-permute-start.8 = (f32[1,1024]{1,0:T(1,128)S(1)}, f32[1,1024]{1,0:T(1,128)S(1)}, u32[]{:S(2)}, u32[]{:S(2)}) collective-permute-start(f32[1,1024]{1,0:T(1,128)S(1)} %get-tuple-element.35), channel_id=1, source_target_pairs={{0,8},{1,0},{2,10},{3,2},{4,12},{5,4},{6,14},{7,6},{8,9},{9,1},{10... | collective-permute-start | bytes 12296 | tf_op jit(solution)/shard_map/ppermute | solution.py:305
  17.7 2.3 %collective-permute-done.8.returned = f32[1,1024]{1,0:T(1,128)S(1)} collective-permute-done((f32[1,1024]{1,0:T(1,128)S(1)}, f32[1,1024]{1,0:T(1,128)S(1)}, u32[]{:S(2)}, u32[]{:S(2)}) %collective-permute-start.8) | collective-permute-done | bytes 4128 | tf_op jit(solution)/shard_map/ppermute | solution.py:305
  19.9 0.6 %finish.1 = (f32[1,512]{1,0:T(1,128)}, f32[1,1024]{1,0:T(1,128)}) custom-call(f32[8,128]{1,0:T(8,128)S(1)} %outer.1.grad, f32[1,1024]{1,0:T(1,128)S(1)} %get-tuple-element.34.near, f32[1,1024]{1,0:T(1,128)S(1)} %collective-permute-done.8.returned), custom_call_target="tpu_custom_call" | custom-call | flops 1 | bytes 1 | tf_op jit(solution)/shard_map/finish/pallas_call | solution.py:264
  (4 shorter events, 0.1 us)
Async XLA Ops:
  0.6 5.8 %copy-start.1 = (bf16[1,256,4096]{2,1,0:T(8,128)(2,1)S(1)}, bf16[1,256,4096]{2,1,0:T(8,128)(2,1)}, u32[]{:S(2)}) copy-start(bf16[1,256,4096]{2,1,0:T(8,128)(2,1)} %param.9) | copy-start | bytes 6291460
  0.6 5.8 %copy-start.4 = (bf16[32,4096]{1,0:T(8,128)(2,1)S(1)}, bf16[32,4096]{1,0:T(8,128)(2,1)}, u32[]{:S(2)}) copy-start(bf16[32,4096]{1,0:T(8,128)(2,1)} %out_f.1) | copy-start | bytes 786436
  0.6 6.5 %copy-start = (bf16[1,256,14784]{1,2,0:T(8,128)(2,1)S(1)}, bf16[1,256,14784]{1,2,0:T(8,128)(2,1)}, u32[]{:S(2)}) copy-start(bf16[1,256,14784]{1,2,0:T(8,128)(2,1)} %param.8) | copy-start | bytes 22708228
  0.7 6.5 %copy-start.3 = (bf16[32,14784]{1,0:T(8,128)(2,1)S(1)}, bf16[32,14784]{1,0:T(8,128)(2,1)}, u32[]{:S(2)}) copy-start(bf16[32,14784]{1,0:T(8,128)(2,1)} %in_f.1) | copy-start | bytes 2838532
  0.7 12.9 %collective-permute-start.6 = (bf16[256,512]{1,0:T(8,128)(2,1)}, bf16[256,512]{1,0:T(8,128)(2,1)S(1)}, u32[]{:S(2)}, u32[]{:S(2)}) collective-permute-start(bf16[256,512]{1,0:T(8,128)(2,1)} %queries), channel_id=1, source_target_pairs={{0,2},{1,5},{2,6},{3,1},{4,0},{5,7},{6,4},{7,3},{8,10},{9,13},{10,... | collective-permute-start | bytes 786440 | tf_op jit(solution)/shard_map/ppermute | solution.py:305
  2.9 10.8 %collective-permute-start.7 = (bf16[256,512]{1,0:T(8,128)(2,1)}, bf16[256,512]{1,0:T(8,128)(2,1)S(1)}, u32[]{:S(2)}, u32[]{:S(2)}) collective-permute-start(bf16[256,512]{1,0:T(8,128)(2,1)} %queries), channel_id=1, source_target_pairs={{0,4},{1,3},{2,0},{3,7},{4,6},{5,1},{6,2},{7,5},{8,12},{9,11},{10,... | collective-permute-start | bytes 786440 | tf_op jit(solution)/shard_map/ppermute | solution.py:305
  2.9 13.3 %collective-permute-start.2 = (bf16[256,512]{1,0:T(8,128)(2,1)}, bf16[256,512]{1,0:T(8,128)(2,1)S(1)}, u32[]{:S(2)}, u32[]{:S(2)}) collective-permute-start(bf16[256,512]{1,0:T(8,128)(2,1)} %queries), channel_id=1, source_target_pairs={{0,6},{1,17},{2,4},{3,19},{4,2},{5,21},{6,0},{7,23},{8,24},{9,15},... | collective-permute-start | bytes 786440 | tf_op jit(solution)/shard_map/ppermute | solution.py:305
  4.2 11.9 %collective-permute-start.3 = (bf16[256,512]{1,0:T(8,128)(2,1)}, bf16[256,512]{1,0:T(8,128)(2,1)S(1)}, u32[]{:S(2)}, u32[]{:S(2)}) collective-permute-start(bf16[256,512]{1,0:T(8,128)(2,1)} %queries), channel_id=1, source_target_pairs={{0,1},{1,6},{2,3},{3,4},{4,5},{5,2},{6,7},{7,0},{8,15},{9,8},{10,1... | collective-permute-start | bytes 786440 | tf_op jit(solution)/shard_map/ppermute | solution.py:305
  7.2 1.9 %copy-start.2 = (f32[512,1024]{1,0:T(8,128)S(1)}, f32[512,1024]{1,0:T(8,128)}, u32[]{:S(2)}) copy-start(f32[512,1024]{1,0:T(8,128)} %values.3) | copy-start | bytes 6291460
  8.6 1.3 %collective-permute-start.1 = (f32[64,256]{1,0:T(8,128)S(1)}, f32[64,256]{1,0:T(8,128)S(1)}, u32[]{:S(2)}, u32[]{:S(2)}) collective-permute-start(f32[64,256]{1,0:T(8,128)S(1)} %get-tuple-element.27.mine), channel_id=1, source_target_pairs={{0,1},{1,0},{2,3},{3,2},{4,5},{5,4},{6,7},{7,6},{8,9},{9,8},{10,11... | collective-permute-start | bytes 196616 | tf_op jit(solution)/shard_map/ppermute | solution.py:308
  10.8 1.2 %collective-permute-start.4 = (f32[1,512]{1,0:T(1,128)S(1)}, f32[1,512]{1,0:T(1,128)S(1)}, u32[]{:S(2)}, u32[]{:S(2)}) collective-permute-start(f32[1,512]{1,0:T(1,128)S(1)} %precondition.1.mine), channel_id=1, source_target_pairs={{0,1},{1,0},{2,3},{3,2},{4,5},{5,4},{6,7},{7,6},{8,9},{9,8},{10,11... | collective-permute-start | bytes 6152 | tf_op jit(solution)/shard_map/ppermute | solution.py:308
  12.0 4.1 %collective-permute-start.5 = (f32[1,1024]{1,0:T(1,128)S(1)}, f32[1,1024]{1,0:T(1,128)S(1)}, u32[]{:S(2)}, u32[]{:S(2)}) collective-permute-start(f32[1,1024]{1,0:T(1,128)S(1)} %both_halves.1.refs_0_), channel_id=1, source_target_pairs={{0,1},{1,9},{2,3},{3,11},{4,5},{5,13},{6,7},{7,15},{8,0},{9,8},{10... | collective-permute-start | bytes 12296 | tf_op jit(solution)/shard_map/ppermute | solution.py:305
  13.7 2.4 %collective-permute-start = (bf16[3,256,512]{2,1,0:T(8,128)(2,1)S(1)}, bf16[3,256,512]{2,1,0:T(8,128)(2,1)S(1)}, u32[]{:S(2)}, u32[]{:S(2)}) collective-permute-start(bf16[3,256,512]{2,1,0:T(8,128)(2,1)S(1)} %stack.1), channel_id=1, source_target_pairs={{0,1},{1,0},{2,3},{3,2},{4,5},{5,4},{6,7},{7,6},{8,9},{9,8},{10,11... | collective-permute-start | bytes 2359304 | tf_op jit(solution)/shard_map/cond/branch_1_fun/ppermute | solution.py:308
  16.2 3.8 %collective-permute-start.8 = (f32[1,1024]{1,0:T(1,128)S(1)}, f32[1,1024]{1,0:T(1,128)S(1)}, u32[]{:S(2)}, u32[]{:S(2)}) collective-permute-start(f32[1,1024]{1,0:T(1,128)S(1)} %get-tuple-element.35), channel_id=1, source_target_pairs={{0,8},{1,0},{2,10},{3,2},{4,12},{5,4},{6,14},{7,6},{8,9},{9,1},{10... | collective-permute-start | bytes 12296 | tf_op jit(solution)/shard_map/ppermute | solution.py:305
